TPU v7x, 32 devices: a whole 2x2x4 slice. The times are simulated.
32 devices in a mesh: wide: 8 (over z, x), narrow: 4 (over y, core).
Axes of the slice: x: 2, y: 2, z: 4, core: 2. Of those that a mesh axis runs over, the one named last changes fastest.
Arguments:
- tokens: bfloat16 [16384, 512], P(('wide', 'narrow')), may hold values from -6 to 6
- cotangent: bfloat16 [16384, 512], P(('wide', 'narrow')), may hold values from -6 to 6
- segments: int32 [16384], P(('wide', 'narrow')), may hold values from 0 to 23, as said below
- padding: int32 [16384], P(('wide', 'narrow')), may hold values 0 or 1
- generative: int32 [16384], P(('wide', 'narrow')), may hold values 0 or 1
- in_weights: float32 [4, 512, 512], P(None, None, 'narrow'), may hold values from -0.25 to 0.25
- out_weights: float32 [2, 512, 512], P(None, 'narrow'), may hold values from -1.41421356 to 1.41421356
- in_momenta: float32 [4, 512, 512], P(None, None, 'narrow'), may hold values from -768 to 768
- out_momenta: float32 [2, 512, 512], P(None, 'narrow'), may hold values from -921.6 to 921.6
- in_average: float32 [4, 512, 512], P(None, None, 'narrow'), may hold values from -0.25 to 0.25
- out_average: float32 [2, 512, 512], P(None, 'narrow'), may hold values from -0.25 to 0.25
- shared_values: float32 [6, 512], replicated, may hold values from -1.2 to 1.4
- shared_moment1: float32 [6, 512], replicated, may hold values from -80 to 80
- shared_moment2: float32 [6, 512], replicated, may hold values from 16.384 to 65.536
- shared_average: float32 [6, 512], replicated, may hold values from -1.2 to 1.4
- split_values: float32 [3, 512], P(None, 'narrow'), may hold values from -1.75 to 1.75
- split_moment1: float32 [3, 512], P(None, 'narrow'), may hold values from -24 to 24
- split_moment2: float32 [3, 512], P(None, 'narrow'), may hold values from 1.6384 to 6.5536
- split_average: float32 [3, 512], P(None, 'narrow'), may hold values from -1.75 to 1.75
Outputs:
- out_tokens: bfloat16 [16384, 512], P(('wide', 'narrow'))
- grad_tokens: float32 [16384, 512], P(('wide', 'narrow'))
- in_momenta_new: float32 [4, 512, 512], P(None, None, 'narrow')
- out_momenta_new: float32 [2, 512, 512], P(None, 'narrow')
- in_weights_new: float32 [4, 512, 512], P(None, None, 'narrow')
- out_weights_new: float32 [2, 512, 512], P(None, 'narrow')
- in_weights_low: bfloat16 [4, 512, 512], P(None, None, 'narrow')
- out_weights_low: bfloat16 [2, 512, 512], P(None, 'narrow')
- in_average_new: float32 [4, 512, 512], P(None, None, 'narrow')
- out_average_new: float32 [2, 512, 512], P(None, 'narrow')
- shared_moment1_new: float32 [6, 512], replicated
- shared_moment2_new: float32 [6, 512], replicated
- shared_values_new: float32 [6, 512], replicated
- shared_average_new: float32 [6, 512], replicated
- split_moment1_new: float32 [3, 512], P(None, 'narrow')
- split_moment2_new: float32 [3, 512], P(None, 'narrow')
- split_values_new: float32 [3, 512], P(None, 'narrow')
- split_average_new: float32 [3, 512], P(None, 'narrow')
Inputs may be any that keep to these rules, and one draw needn't show every extreme that they name: `segments`: never falls along the tokens; tokens of different rows have different numbers.
All inputs are finite; a program needn't handle non-finite values. No bound on the sum of `padding` or of `generative` on one device may be relied on, other than what follows from the above.
Results may differ from a plain program's by a relative error of at most 0.018.
Values may be sent and summed in bfloat16 or wider, within the bound.
A program may use at most 128 MiB of HBM per device.

v0:
```python
import math

import jax
import jax.numpy as jnp
from jax import lax
from jax.sharding import PartitionSpec as P

D = 512
HD = 64
LEN = 2048
NS_ITERS = 3
STEP = 10


coef_a = 3.4445
coef_b = -4.775
coef_c = 2.0315


def layer_norm(values, gain_vec, shift_vec):
    center = values - jnp.mean(values, axis=-1, keepdims=True)
    spread = jnp.mean(center * center, axis=-1, keepdims=True)
    return center * lax.rsqrt(spread + 1e-05) * gain_vec + shift_vec


def gelu_exact(values):
    return jax.nn.gelu(values, approximate=False)


def muon_step(weights, orthogonal):
    return weights - 0.2 * (0.2 * math.sqrt(D) * orthogonal + 0.01 * weights)


def adam_step(values, moment_one, moment_two, gradient):
    moment_one = 0.9 * moment_one + 0.1 * gradient
    moment_two = 0.999 * moment_two + 0.001 * gradient * gradient
    step_ratio = (
        moment_one / (1.0 - 0.9**STEP) / (jnp.sqrt(moment_two / (1.0 - 0.999**STEP)) + 1e-08)
    )
    return (moment_one, moment_two, values - 0.3 * (step_ratio + 0.01 * values))


def blend(average, weights):
    return 0.6 * average + 0.4 * weights


def masked_scores(q_block, k_row, seg_block, pos_block, seg_row, open_row):
    places = jnp.arange(LEN, dtype=jnp.int32)
    raw_scores = jnp.einsum(
        "qhe,khe->hqk", q_block, k_row, preferred_element_type=jnp.float32
    ) * HD ** (-0.5)
    allowed = (seg_block[:, None] == seg_row[None, :]) & (
        open_row[None, :] | (pos_block[:, None] == places[None, :])
    )
    return jnp.where(allowed[None], raw_scores, -1e30)


def attention_forward(q_all, k_all, v_all, seg_rows, open_rows):
    block_len = min(512, LEN)
    block_num = LEN // block_len
    head_count = q_all.shape[2]
    places = jnp.arange(LEN, dtype=jnp.int32)

    def per_row(pieces):
        q_row, k_row, v_row, seg_row, open_row = pieces

        def per_block(inner_parts):
            q_block, seg_block, pos_block = inner_parts
            scores = masked_scores(q_block, k_row, seg_block, pos_block, seg_row, open_row)
            row_max = jnp.max(scores, axis=-1, keepdims=True)
            exp_terms = jnp.exp(scores - row_max)
            row_total = jnp.sum(exp_terms, axis=-1, keepdims=True)
            prob_rows = exp_terms / row_total
            context = jnp.einsum(
                "hqk,khe->qhe",
                prob_rows.astype(jnp.bfloat16),
                v_row,
                preferred_element_type=jnp.float32,
            )
            return (context, (row_max + jnp.log(row_total))[:, :, 0])

        return lax.map(
            per_block,
            (
                q_row.reshape(block_num, block_len, head_count, HD),
                seg_row.reshape(block_num, block_len),
                places.reshape(block_num, block_len),
            ),
        )

    return lax.map(per_row, (q_all, k_all, v_all, seg_rows, open_rows))


def attention_backward(q_all, k_all, v_all, seg_rows, open_rows, log_sums, grad_context):
    block_len = min(512, LEN)
    block_num = LEN // block_len
    head_count = q_all.shape[2]
    places = jnp.arange(LEN, dtype=jnp.int32)
    score_scale = HD ** (-0.5)

    def per_row(pieces):
        q_row, k_row, v_row, seg_row, open_row, lse_row, dc_row = pieces

        def per_block(carried, inner_parts):
            key_grad, value_grad = carried
            q_block, seg_block, pos_block, lse_block, dc_block = inner_parts
            scores = masked_scores(q_block, k_row, seg_block, pos_block, seg_row, open_row)
            prob_rows = jnp.exp(scores - lse_block[:, :, None])
            prob_grad = jnp.einsum(
                "qhe,khe->hqk", dc_block, v_row, preferred_element_type=jnp.float32
            )
            row_delta = jnp.sum(prob_grad * prob_rows, axis=-1, keepdims=True)
            score_grad = (prob_rows * (prob_grad - row_delta)).astype(jnp.bfloat16)
            query_grad = (
                jnp.einsum("hqk,khe->qhe", score_grad, k_row, preferred_element_type=jnp.float32)
                * score_scale
            )
            key_grad = (
                key_grad
                + jnp.einsum(
                    "hqk,qhe->khe", score_grad, q_block, preferred_element_type=jnp.float32
                )
                * score_scale
            )
            value_grad = value_grad + jnp.einsum(
                "hqk,qhe->khe",
                prob_rows.astype(jnp.bfloat16),
                dc_block,
                preferred_element_type=jnp.float32,
            )
            return ((key_grad, value_grad), query_grad)

        zero_keys = jnp.zeros(k_row.shape, jnp.float32)
        block_shape = (block_num, block_len, head_count, HD)
        inner_parts = (
            q_row.reshape(block_shape),
            seg_row.reshape(block_num, block_len),
            places.reshape(block_num, block_len),
            lse_row,
            dc_row.reshape(block_shape),
        )
        (key_grad, value_grad), query_grad = lax.scan(
            per_block, (zero_keys, zero_keys), inner_parts
        )
        return (query_grad.reshape(LEN, head_count, HD), key_grad, value_grad)

    return lax.map(per_row, (q_all, k_all, v_all, seg_rows, open_rows, log_sums, grad_context))


def single_newton(matrix):
    current = matrix / (jnp.sqrt(jnp.sum(matrix * matrix)) + 1e-07)
    for iteration in range(NS_ITERS):
        gram = jnp.dot(
            current, current.T, precision=lax.Precision.HIGHEST, preferred_element_type=jnp.float32
        )
        poly = coef_b * gram + coef_c * jnp.dot(
            gram, gram, precision=lax.Precision.HIGHEST, preferred_element_type=jnp.float32
        )
        current = coef_a * current + jnp.dot(
            poly, current, precision=lax.Precision.HIGHEST, preferred_element_type=jnp.float32
        )
    return current


def body(
    tokens,
    cotangent,
    segments,
    padding,
    generative,
    in_weights,
    out_weights,
    in_momenta,
    out_momenta,
    in_average,
    out_average,
    shared_values,
    shared_moment1,
    shared_moment2,
    shared_average,
    split_values,
    split_moment1,
    split_moment2,
    split_average,
):
    gathered, seg_all, pad_all, gen_all = (
        lax.all_gather(tokens, "narrow", axis=0, tiled=True),
        lax.all_gather(segments, "narrow", axis=0, tiled=True),
        lax.all_gather(padding, "narrow", axis=0, tiled=True),
        lax.all_gather(generative, "narrow", axis=0, tiled=True),
    )
    group_rows = gathered.shape[0]
    seq_count = group_rows // LEN
    low_in = in_weights.astype(jnp.bfloat16)
    low_out = out_weights.astype(jnp.bfloat16)
    columns = low_in.shape[2]
    head_count = columns // HD
    row_shape = (seq_count, LEN, head_count, HD)
    projected = jnp.einsum("td,kdc->ktc", gathered, low_in[:3], preferred_element_type=jnp.float32)
    q_all = (projected[0] + split_values[0]).astype(jnp.bfloat16).reshape(row_shape)
    k_all = projected[1].astype(jnp.bfloat16).reshape(row_shape)
    v_all = (projected[2] + split_values[1]).astype(jnp.bfloat16).reshape(row_shape)
    seg_rows = seg_all.reshape(seq_count, LEN)
    open_rows = ((pad_all == 0) & (gen_all == 0)).reshape(seq_count, LEN)
    context, log_sums = attention_forward(q_all, k_all, v_all, seg_rows, open_rows)
    context_low = context.reshape(group_rows, columns).astype(jnp.bfloat16)
    attention = lax.psum_scatter(
        jnp.dot(context_low, low_out[0], preferred_element_type=jnp.float32),
        "narrow",
        scatter_dimension=0,
        tiled=True,
    )
    first_in = tokens.astype(jnp.float32) + attention + shared_values[4]
    hidden, first_back = jax.vjp(layer_norm, first_in, shared_values[0], shared_values[1])
    hidden_all = lax.all_gather(hidden.astype(jnp.bfloat16), "narrow", axis=0, tiled=True)
    upper_in = jnp.dot(hidden_all, low_in[3], preferred_element_type=jnp.float32) + split_values[2]
    active_full, gelu_back = jax.vjp(gelu_exact, upper_in)
    active = active_full.astype(jnp.bfloat16)
    ff_out = lax.psum_scatter(
        jnp.dot(active, low_out[1], preferred_element_type=jnp.float32).astype(jnp.bfloat16),
        "narrow",
        scatter_dimension=0,
        tiled=True,
    ).astype(jnp.float32)
    second_in = hidden + ff_out + shared_values[5]
    result, second_back = jax.vjp(layer_norm, second_in, shared_values[2], shared_values[3])
    grad_second, gain_two, shift_two = second_back(cotangent.astype(jnp.float32))
    second_all = lax.all_gather(grad_second.astype(jnp.bfloat16), "narrow", axis=0, tiled=True)
    grad_active = jnp.einsum(
        "td,cd->tc", second_all, low_out[1], preferred_element_type=jnp.float32
    )
    grad_down = jnp.einsum("tc,td->cd", active, second_all, preferred_element_type=jnp.float32)
    grad_upper = gelu_back(grad_active)[0].astype(jnp.bfloat16)
    grad_up = jnp.einsum("td,tc->dc", hidden_all, grad_upper, preferred_element_type=jnp.float32)
    grad_hidden = grad_second + lax.psum_scatter(
        jnp.einsum("tc,dc->td", grad_upper, low_in[3], preferred_element_type=jnp.float32).astype(
            jnp.bfloat16
        ),
        "narrow",
        scatter_dimension=0,
        tiled=True,
    ).astype(jnp.float32)
    grad_first, gain_one, shift_one = first_back(grad_hidden)
    first_all = lax.all_gather(grad_first.astype(jnp.bfloat16), "narrow", axis=0, tiled=True)
    grad_context = jnp.einsum(
        "td,cd->tc", first_all, low_out[0], preferred_element_type=jnp.float32
    ).astype(jnp.bfloat16)
    grad_att = jnp.einsum("tc,td->cd", context_low, first_all, preferred_element_type=jnp.float32)
    query_grad, key_grad, value_grad = attention_backward(
        q_all, k_all, v_all, seg_rows, open_rows, log_sums, grad_context.reshape(row_shape)
    )
    grad_qkv = jnp.stack(
        [
            query_grad.reshape(group_rows, columns),
            key_grad.reshape(group_rows, columns),
            value_grad.reshape(group_rows, columns),
        ]
    ).astype(jnp.bfloat16)
    grad_proj = jnp.einsum("td,ktc->kdc", gathered, grad_qkv, preferred_element_type=jnp.float32)
    grad_tokens = (
        lax.psum_scatter(
            jnp.einsum(
                "ktc,kdc->td", grad_qkv, low_in[:3], preferred_element_type=jnp.float32
            ).astype(jnp.bfloat16),
            "narrow",
            scatter_dimension=0,
            tiled=True,
        ).astype(jnp.float32)
        + grad_first
    )
    grad_in = jnp.concatenate([grad_proj, grad_up[None]], axis=0)
    grad_out = jnp.stack([grad_att, grad_down])
    grad_split = jnp.stack(
        [
            jnp.sum(grad_qkv[0].astype(jnp.float32), axis=0),
            jnp.sum(grad_qkv[2].astype(jnp.float32), axis=0),
            jnp.sum(grad_upper.astype(jnp.float32), axis=0),
        ]
    )
    grad_shared = jnp.stack(
        [
            gain_one,
            shift_one,
            gain_two,
            shift_two,
            jnp.sum(grad_first, axis=0),
            jnp.sum(grad_second, axis=0),
        ]
    )
    sum_in, sum_out, sum_split = lax.psum((grad_in, grad_out, grad_split), "wide")
    sum_shared = lax.psum(grad_shared, ("wide", "narrow"))
    moment_in = 0.5 * in_momenta + sum_in
    moment_out = 0.5 * out_momenta + sum_out
    owner_slot = lax.axis_index("wide")
    stacked = jnp.concatenate([moment_in, jnp.transpose(moment_out, (0, 2, 1))], axis=0)
    chosen = lax.dynamic_index_in_dim(stacked, jnp.minimum(owner_slot, 5), 0, keepdims=False)
    full_matrix = lax.all_gather(chosen.astype(jnp.bfloat16), "narrow", axis=1, tiled=True).astype(
        chosen.dtype
    )
    finished = single_newton(full_matrix)
    place = lax.axis_index("narrow") * columns
    own_share = lax.dynamic_slice_in_dim(finished, place, columns, 1)
    selector = (jnp.arange(6, dtype=jnp.int32) == owner_slot).astype(jnp.float32)
    spread_back = lax.psum(selector[:, None, None] * own_share[None], "wide")
    ortho_in = spread_back[:4]
    ortho_out = jnp.transpose(spread_back[4:], (0, 2, 1))
    new_in = muon_step(in_weights, ortho_in)
    new_out = muon_step(out_weights, ortho_out)
    shared_one, shared_two, shared_new = adam_step(
        shared_values, shared_moment1, shared_moment2, sum_shared
    )
    split_one, split_two, split_new = adam_step(
        split_values, split_moment1, split_moment2, sum_split
    )
    return (
        result.astype(jnp.bfloat16),
        grad_tokens,
        moment_in,
        moment_out,
        new_in,
        new_out,
        new_in.astype(jnp.bfloat16),
        new_out.astype(jnp.bfloat16),
        blend(in_average, new_in),
        blend(out_average, new_out),
        shared_one,
        shared_two,
        shared_new,
        blend(shared_average, shared_new),
        split_one,
        split_two,
        split_new,
        blend(split_average, split_new),
    )


def solution(mesh):
    placed = (
        P(("wide", "narrow"), None),
        P(("wide", "narrow"), None),
        P(("wide", "narrow")),
        P(("wide", "narrow")),
        P(("wide", "narrow")),
        P(None, None, "narrow"),
        P(None, "narrow", None),
        P(None, None, "narrow"),
        P(None, "narrow", None),
        P(None, None, "narrow"),
        P(None, "narrow", None),
        P(),
        P(),
        P(),
        P(),
        P(None, "narrow"),
        P(None, "narrow"),
        P(None, "narrow"),
        P(None, "narrow"),
    )
    return jax.shard_map(
        body,
        mesh=mesh,
        in_specs=placed,
        out_specs=(
            P(("wide", "narrow"), None),
            P(("wide", "narrow"), None),
            P(None, None, "narrow"),
            P(None, "narrow", None),
            P(None, None, "narrow"),
            P(None, "narrow", None),
            P(None, None, "narrow"),
            P(None, "narrow", None),
            P(None, None, "narrow"),
            P(None, "narrow", None),
            P(),
            P(),
            P(),
            P(),
            P(None, "narrow"),
            P(None, "narrow"),
            P(None, "narrow"),
            P(None, "narrow"),
        ),
        check_vma=False,
    )
```

profile of v0, /device:TPU:0, one launch (start us, length us, event | category | flops | bytes accessed | tf_op | source)
XLA Modules:
  0.0 610.9 jit_solution(6306134578729636736)
XLA Ops:
  9.0 6.3 %all-gather.1 = s32[4,1,512]{2,1,0:T(1,128)S(1)} all-gather(s32[1,1,512]{2,1,0:T(1,128)} %bitcast.253), channel_id=1, replica_groups=mesh['wide'=8,'narrow'=4] {'narrow'}, dimensions={0}, use_global_device_ids=true | all-gather | bytes 10240 | tf_op jit(solution)/shard_map/all_gather | solution.py:188
  15.2 5.5 all-gather.2
  20.7 5.3 all-gather.3
  28.9 6.1 all-gather.9.cloned.1.call-done
  42.8 34.8 %while.47 = (s32[]{:T(128)}, bf16[4,512,2,64]{1,3,2,0:T(8,128)(2,1)S(1)}, f32[4,2,512]{2,1,0:T(2,128)S(1)}, s32[4,512]{1,0:T(4,128)S(1)}, s32[2048]{0:T(1024)S(1...) while((s32[]{:T(128)}, ...), condition=%wide.region_3.4_spmd, body=%wide.region_0.3_spmd.sunk | while | flops 566230016 | bytes 30857348 | solution.py:82
  48.8 2.7 fusion.165
  57.5 2.7 fusion.165
  66.2 2.7 fusion.165
  81.7 44.6 %reduce-scatter.5.cloned.1.call-done = f32[512,512]{1,0:T(8,128)} async-done(((f32[2048,512]{1,0:T(8,128)}), f32[512,512]{1,0:T(8,128)}) %reduce-scatter.5.cloned.1.call-update) | async-done | bytes 1048592 | tf_op jit(solution)/shard_map/reduce_scatter | solution.py:207
  129.6 22.2 %all-gather.11.cloned.1.call-done = bf16[2048,512]{1,0:T(8,128)(2,1)} async-done(((bf16[512,512]{1,0:T(8,128)(2,1)}), bf16[2048,512]{1,0:T(8,128)(2,1)}) %all-gather.11.cloned.1.call-update) | async-done | bytes 2097168 | tf_op jit(solution)/shard_map/all_gather | solution.py:215
  151.8 5.3 multiply_convert_fusion.1
  160.0 31.5 %reduce-scatter.7.cloned.1.call-done = bf16[512,512]{1,0:T(8,128)(2,1)} async-done(((bf16[2048,512]{1,0:T(8,128)(2,1)}), bf16[512,512]{1,0:T(8,128)(2,1)}) %reduce-scatter.7.cloned.1.call-update) | async-done | bytes 524304 | tf_op jit(solution)/shard_map/reduce_scatter | solution.py:219
  197.2 22.7 %all-gather.13.cloned.1.call-done = bf16[2048,512]{1,0:T(8,128)(2,1)} async-done(((bf16[512,512]{1,0:T(8,128)(2,1)}), bf16[2048,512]{1,0:T(8,128)(2,1)}) %all-gather.13.cloned.1.call-update) | async-done | bytes 2097168 | tf_op jit(solution)/shard_map/all_gather | solution.py:228
  219.9 2.9 convert_reduce_fusion.1
  223.6 2.9 convolution_convert_fusion
  226.6 31.5 %reduce-scatter.9.cloned.1.call-done = bf16[512,512]{1,0:T(8,128)(2,1)} async-done(((bf16[2048,512]{1,0:T(8,128)(2,1)}), bf16[512,512]{1,0:T(8,128)(2,1)}) %reduce-scatter.9.cloned.1.call-update) | async-done | bytes 524304 | tf_op jit(solution)/shard_map/reduce_scatter | solution.py:235
  263.4 3.0 convolution_bitcast_fusion.1
  266.4 2.9 convolution_bitcast_fusion.3
  269.3 16.9 %all-gather.15.cloned.1.call-done = bf16[2048,512]{1,0:T(8,128)(2,1)} async-done(((bf16[512,512]{1,0:T(8,128)(2,1)}), bf16[2048,512]{1,0:T(8,128)(2,1)}) %all-gather.15.cloned.1.call-update) | async-done | bytes 2097168 | tf_op jit(solution)/shard_map/all_gather | solution.py:244
  293.2 53.9 %while.48 = (s32[]{:T(128)}, f32[2048,2,64]{0,2,1:T(8,128)S(1)}, f32[2048,2,64]{0,2,1:T(8,128)}, bf16[4,512,2,64]{1,3,2,0:T(8,128)(2,1)}, bf16[4,512,2,64]{1,3,2...) while((s32[]{:T(128)}, f32[2048,2,64]{0,2,1:T(8,128)S(1)}, ...), condition=%wide.region_17.18_spmd.clone, body=%wide.region_15.17_spmd.clone.sunk | while | flops 1379204096 | bytes 86296872 | solution.py:142
  298.6 3.1 multiply_reduce_fusion.6
  312.1 3.1 multiply_reduce_fusion.6
  325.6 3.1 multiply_reduce_fusion.6
  339.1 3.1 multiply_reduce_fusion.6
  359.2 88.7 %all-reduce.6.cloned.1.call-done = (f32[4,512,128]{1,2,0:T(8,128)}, f32[2,128,512]{2,1,0:T(8,128)}) async-done(((f32[4,512,128]{1,2,0:T(8,128)}, f32[2,128,512]{2,1,0:T(8,128)}), (f32[4,512,128]{1,2,0:T(8,128)}, f32[2,128,512]{2,1,0:T(8,128)})) %all-reduce.6.cloned.1.call-update) | async-done | bytes 1572880 | tf_op jit(solution)/shard_map/psum | solution.py:290
  451.4 7.4 %all-gather = bf16[1,512,512]{1,2,0:T(8,128)(2,1)S(1)} all-gather(bf16[1,512,128]{1,2,0:T(8,128)(2,1)S(1)} %fusion.82), channel_id=2, replica_groups=mesh['wide'=8,'narrow'=4] {'narrow'}, dimensions={2}, use_global_device_ids=true | all-gather | bytes 655360 | tf_op jit(solution)/shard_map/all_gather | solution.py:297
  479.3 3.8 bitcast_convert_fusion
  483.2 40.2 %psum.38 = f32[6,512]{1,0:T(8,128)S(1)} all-reduce(f32[6,512]{1,0:T(8,128)S(1)} %stack.44), channel_id=1, replica_groups=mesh['wide'=8,'narrow'=4] {'wide','narrow'}, use_global_device_ids=true, to_apply=%region_29.30 | all-reduce | flops 3072 | bytes 24576 | tf_op jit(solution)/shard_map/psum | solution.py:291
  524.2 21.0 %psum.39 = f32[3,128]{1,0:T(4,128)S(1)} all-reduce(f32[3,128]{1,0:T(4,128)S(1)} %pad_maximum_fusion.5), channel_id=1, replica_groups=mesh['wide'=8,'narrow'=4] {'wide'}, use_global_device_ids=true, to_apply=%region_33.34 | all-reduce | flops 384 | bytes 3072 | tf_op jit(solution)/shard_map/psum | solution.py:290
  547.1 20.9 %all-reduce.4.cloned.1.call-done = f32[6,512,128]{1,2,0:T(8,128)} async-done(((f32[6,512,128]{1,2,0:T(8,128)}), f32[6,512,128]{1,2,0:T(8,128)}) %all-reduce.4.cloned.1.call-update) | async-done | bytes 1572880 | tf_op jit(solution)/shard_map/psum | solution.py:304
  569.9 2.7 multiply_add_fusion.3
  576.0 25.4 %reduce-scatter.11.cloned.1.call-done = bf16[512,512]{1,0:T(8,128)(2,1)} async-done(((bf16[2048,512]{1,0:T(8,128)(2,1)}), bf16[512,512]{1,0:T(8,128)(2,1)}) %reduce-scatter.11.cloned.1.call-update) | async-done | bytes 524304 | tf_op jit(solution)/shard_map/reduce_scatter | solution.py:261
  (262 shorter events, 154.2 us)
Async XLA Ops:
  7.2 27.8 %all-gather.9.cloned.1.call-start = ((), (), s32[]{:S(2)}) async-start(), calls=%async_computation.4 | async-start | bytes 2621440 | tf_op jit(solution)/shard_map/all_gather | solution.py:187
  7.9 118.4 %reduce-scatter.5.cloned.1.call-start = ((), (), s32[]{:S(2)}) async-start(), calls=%async_computation.5 | async-start | bytes 5242880 | tf_op jit(solution)/shard_map/reduce_scatter | solution.py:207
  28.7 10.3 %copy-start = (f32[4,512,128]{1,2,0:T(8,128)}, f32[4,512,128]{1,2,0:T(8,128)S(1)}, u32[]{:S(2)}) copy-start(f32[4,512,128]{1,2,0:T(8,128)S(1)} %copy.78) | copy-start | bytes 3145732
  28.8 123.0 %copy-start.16 = (bf16[4,512,128]{1,2,0:T(8,128)(2,1)}, bf16[4,512,128]{1,2,0:T(8,128)(2,1)S(1)}, u32[]{:S(2)}) copy-start(bf16[4,512,128]{1,2,0:T(8,128)(2,1)S(1)} %convert_element_type.115) | copy-start | bytes 1572868
  79.0 47.3 %copy-start.9 = (bf16[512,512]{1,0:T(8,128)(2,1)S(1)}, bf16[512,512]{1,0:T(8,128)(2,1)}, u32[]{:S(2)}) copy-start(bf16[512,512]{1,0:T(8,128)(2,1)} %param.23) | copy-start | bytes 1572868
  81.7 70.2 %all-gather.11.cloned.1.call-start = ((), (), s32[]{:S(2)}) async-start(), calls=%async_computation.6 | async-start | bytes 2621440 | tf_op jit(solution)/shard_map/all_gather | solution.py:215
  129.1 62.5 %reduce-scatter.7.cloned.1.call-start = ((), (), s32[]{:S(2)}) async-start(), calls=%async_computation.7 | async-start | bytes 2621440 | tf_op jit(solution)/shard_map/reduce_scatter | solution.py:219
  158.0 35.4 %copy-start.12 = (bf16[512,512]{1,0:T(8,128)(2,1)S(1)}, bf16[512,512]{1,0:T(8,128)(2,1)}, u32[]{:S(2)}) copy-start(bf16[512,512]{1,0:T(8,128)(2,1)} %param.24) | copy-start | bytes 1572868
  160.0 59.9 %all-gather.13.cloned.1.call-start = ((), (), s32[]{:S(2)}) async-start(), calls=%async_computation.8 | async-start | bytes 2621440 | tf_op jit(solution)/shard_map/all_gather | solution.py:228
  197.1 61.0 %reduce-scatter.9.cloned.1.call-start = ((), (), s32[]{:S(2)}) async-start(), calls=%async_computation.9 | async-start | bytes 2621440 | tf_op jit(solution)/shard_map/reduce_scatter | solution.py:235
  226.5 59.6 %all-gather.15.cloned.1.call-start = ((), (), s32[]{:S(2)}) async-start(), calls=%async_computation.10 | async-start | bytes 2621440 | tf_op jit(solution)/shard_map/all_gather | solution.py:244
  261.4 5.0 copy-start.28
  263.4 184.6 %all-reduce.6.cloned.1.call-start = ((), (), s32[]{:S(2)}) async-start(), calls=%async_computation.13 | async-start | bytes 3145728 | tf_op jit(solution)/shard_map/psum | solution.py:290
  266.4 26.8 %copy-start.5 = (bf16[4,512,2,64]{1,3,2,0:T(8,128)(2,1)S(1)}, bf16[4,512,2,64]{1,3,2,0:T(8,128)(2,1)}, u32[]{:S(2)}) copy-start(bf16[4,512,2,64]{1,3,2,0:T(8,128)(2,1)} %copy-done.4) | copy-start | bytes 1572868
  349.3 5.3 copy-start.23
  349.7 7.6 %copy-start.25 = (bf16[1,2048,128]{2,1,0:T(8,128)(2,1)}, bf16[1,2048,128]{2,1,0:T(8,128)(2,1)S(1)}, u32[]{:S(2)}) copy-start(bf16[1,2048,128]{2,1,0:T(8,128)(2,1)S(1)} %copy.85) | copy-start | bytes 1572868
  351.5 5.7 copy-start.26
  357.3 92.1 %copy-start.22 = (f32[2,128,512]{2,1,0:T(8,128)S(1)}, f32[2,128,512]{2,1,0:T(8,128)}, u32[]{:S(2)}) copy-start(f32[2,128,512]{2,1,0:T(8,128)} %param.31) | copy-start | bytes 1572868
  358.4 209.6 %all-reduce.4.cloned.1.call-start = ((), (), s32[]{:S(2)}) async-start(), calls=%async_computation.12 | async-start | bytes 3145728 | tf_op jit(solution)/shard_map/psum | solution.py:304
  479.2 44.2 %copy-start.31 = (f32[6,512]{1,0:T(8,128)S(1)}, f32[6,512]{1,0:T(8,128)}, u32[]{:S(2)}) copy-start(f32[6,512]{1,0:T(8,128)} %param.34) | copy-start | bytes 36868
  479.2 44.2 %copy-start.32 = (f32[6,512]{1,0:T(8,128)S(1)}, f32[6,512]{1,0:T(8,128)}, u32[]{:S(2)}) copy-start(f32[6,512]{1,0:T(8,128)} %param.37) | copy-start | bytes 36868
  479.2 44.2 %copy-start.33 = (f32[6,512]{1,0:T(8,128)S(1)}, f32[6,512]{1,0:T(8,128)}, u32[]{:S(2)}) copy-start(f32[6,512]{1,0:T(8,128)} %param.36) | copy-start | bytes 36868
  479.2 44.2 %copy-start.34 = (f32[6,512]{1,0:T(8,128)S(1)}, f32[6,512]{1,0:T(8,128)}, u32[]{:S(2)}) copy-start(f32[6,512]{1,0:T(8,128)} %param.35) | copy-start | bytes 36868
  479.2 66.0 %copy-start.35 = (f32[3,128]{1,0:T(4,128)S(1)}, f32[3,128]{1,0:T(4,128)}, u32[]{:S(2)}) copy-start(f32[3,128]{1,0:T(4,128)} %param.38) | copy-start | bytes 4612
  479.2 66.0 %copy-start.36 = (f32[3,128]{1,0:T(4,128)S(1)}, f32[3,128]{1,0:T(4,128)}, u32[]{:S(2)}) copy-start(f32[3,128]{1,0:T(4,128)} %param.41) | copy-start | bytes 4612
  479.2 66.0 %copy-start.37 = (f32[3,128]{1,0:T(4,128)S(1)}, f32[3,128]{1,0:T(4,128)}, u32[]{:S(2)}) copy-start(f32[3,128]{1,0:T(4,128)} %param.40) | copy-start | bytes 4612
  479.2 65.9 %copy-start.38 = (f32[3,128]{1,0:T(4,128)S(1)}, f32[3,128]{1,0:T(4,128)}, u32[]{:S(2)}) copy-start(f32[3,128]{1,0:T(4,128)} %param.39) | copy-start | bytes 4612
  479.3 122.1 %reduce-scatter.11.cloned.1.call-start = ((), (), s32[]{:S(2)}) async-start(), calls=%async_computation.11 | async-start | bytes 2621440 | tf_op jit(solution)/shard_map/reduce_scatter | solution.py:261
  483.1 84.9 %copy-start.1 = (f32[4,512,128]{1,2,0:T(8,128)S(1)}, f32[4,512,128]{1,2,0:T(8,128)}, u32[]{:S(2)}) copy-start(f32[4,512,128]{1,2,0:T(8,128)} %copy-done) | copy-start | bytes 3145732
  569.5 31.9 %copy-start.3 = (f32[512,512]{1,0:T(8,128)S(1)}, f32[512,512]{1,0:T(8,128)}, u32[]{:S(2)}) copy-start(f32[512,512]{1,0:T(8,128)} %copy-done.2) | copy-start | bytes 3145732
  569.9 33.7 %copy-start.8 = (f32[4,512,128]{2,1,0:T(8,128)}, f32[4,512,128]{2,1,0:T(8,128)S(1)}, u32[]{:S(2)}) copy-start(f32[4,512,128]{2,1,0:T(8,128)S(1)} %copy.99) | copy-start | bytes 3145732
  572.6 31.0 %copy-start.11 = (f32[2,128,512]{2,1,0:T(8,128)}, f32[2,128,512]{2,1,0:T(8,128)S(1)}, u32[]{:S(2)}) copy-start(f32[2,128,512]{2,1,0:T(8,128)S(1)} %get-tuple-element.411) | copy-start | bytes 1572868
  (29 other events, 62.9 us)
Sparse Core Ops, SparseCore 0:
  9.6 25.3 all-gather.8
  81.8 44.4 reduce-scatter.4
  129.2 22.5 all-gather.10
  160.1 31.4 reduce-scatter.6
  197.3 22.5 all-gather.12
  226.7 31.4 reduce-scatter.8
  263.5 22.5 all-gather.14
  358.5 89.4 all-reduce.5
  479.3 88.6 all-reduce.3
  570.5 30.8 reduce-scatter.10
where the time goes:
time: 620 us; the launch traced here: 611 us
  waiting for transfers between devices  311 us (50%)
  matrix products  108 us (17%)
  blocking collectives  85.6 us (14%)
  other arithmetic  67.3 us (11%)
  local copies, waits for them, and re-layouts  20.9 us (3%)
  between operations  16 us (3%)
    psum x1, waiting for transfers between devices, body(): lax.psum((grad_in, grad_out, grad_split), 'wide')  88.7 us
    reduce_scatter x1, waiting for transfers between devices, body(): lax.psum_scatter(jnp.dot(context_low, low_out[0], preferred_element_type=...  44.6 us
    psum x1, blocking collectives, body(): sum_shared = lax.psum(grad_shared, ('wide', 'narrow'))  40.2 us
    reduce_scatter x1, waiting for transfers between devices, body(): lax.psum_scatter(jnp.dot(active, low_out[1], preferred_element_type=jnp.f...  31.5 us
    reduce_scatter x1, waiting for transfers between devices, body(): lax.psum_scatter(jnp.einsum('tc,dc->td', grad_upper, low_in[3], preferred...  31.5 us
    reduce_scatter x1, waiting for transfers between devices, body(): lax.psum_scatter(jnp.einsum('ktc,kdc->td', grad_qkv, low_in[:3], preferre...  25.4 us
    all_gather x1, waiting for transfers between devices, body(): lax.all_gather(grad_second.astype(jnp.bfloat16), 'narrow', axis=0, tiled=...  22.7 us
    all_gather x1, waiting for transfers between devices, body(): lax.all_gather(hidden.astype(jnp.bfloat16), 'narrow', axis=0, tiled=True)  22.2 us
  transfers between devices with their start and end apart: 10, of which 10 were waited for; matrix products, arithmetic and copies ran while one was open for 4% of the time, Pallas kernels for 0%

commit v1 on v0

v1 whole, which is shorter than its diff:
```python
import functools
import math

import jax
import jax.numpy as jnp
from jax import lax
from jax.experimental import pallas as pl
from jax.experimental.pallas import tpu as pltpu
from jax.sharding import PartitionSpec as P

D = 512
HD = 64
LEN = 2048
NS_ITERS = 3
STEP = 10
NAR = 4
TB = LEN // NAR
CW = D // NAR
OWN = 8
PR = CW // OWN
MID = 256

F32 = jnp.float32
BF16 = jnp.bfloat16
MESH = pl.DeviceIdType.MESH

COEF_A = 3.4445
COEF_B = -4.775
COEF_C = 2.0315
NEG = -1e30
MB = 2**20


def mm(a, b):
    return jnp.dot(a, b, preferred_element_type=F32)


def mm_nt(a, b):
    return lax.dot_general(a, b, (((1,), (1,)), ((), ())), preferred_element_type=F32)


def mm_tn(a, b):
    return lax.dot_general(a, b, (((0,), (0,)), ((), ())), preferred_element_type=F32)


def layer_kernel(wide, *refs):
    (
        tok_h, cot_h, pay_i, win_h, wout_h, min_h, mout_h, shared, split,
        otok_h, ograd_h, omom_h, oorth_h, ovec, ovec2,
        tok, cot, pay, win_f, wout_f, mT, wqkvT, wqkv, wup, wod, bcol,
        qp, kTp, vTp, qT, rdn, s_ref, e_ref, ctxn, ctx_s, ctxf,
        hr, act, du, dr2r, dr1r, dr1, dcst, dcr, vecs, vecw, dkT, dvT, gT,
        gst, gr1, gs2, gr2, est, erx, lst, lrx, lv, mom, grp,
        dxs, dxr1, dxs2, dxr2,
        loc_sem, ag_s, ag_r, rly_s, rly_r, pay_s, pay_r, wg_s, wg_r, wr_s, wr_r,
        ctx_sem, ctx_rem, dc_sem, dc_rem, vn_s, vn_r, vw_s, vw_r,
        g1_s, g1_r, g2_s, g2_r, es_s, es_r, ls_s, ls_r, lv_s, lv_r, gp_s, gp_r,
        aw_s, aw_r, an_s, an_r, ar_s, ar_r, dx1_s, dx1_r, dx2_s, dx2_r,
    ) = refs
    n = lax.axis_index("narrow")
    w = lax.axis_index("wide")
    groups = wide // OWN
    g = w // OWN if groups > 1 else 0
    o = lax.rem(w, OWN) if groups > 1 else w
    b0 = lax.rem(n, 2)
    b1 = n // 2

    def rel(x):
        return lax.rem(b0 + x % 2, 2) + 2 * lax.rem(b1 + x // 2, 2)

    n1, n2, n3 = rel(1), rel(2), rel(3)

    def rows(t, size):
        return pl.ds(pl.multiple_of(t * size, size), size)

    def ncopy(src, dst, ssem, rsem, t):
        return pltpu.make_async_remote_copy(
            src_ref=src, dst_ref=dst, send_sem=ssem, recv_sem=rsem,
            device_id={"narrow": t}, device_id_type=MESH,
        )

    def wcopy(src, dst, ssem, rsem, u):
        return pltpu.make_async_remote_copy(
            src_ref=src, dst_ref=dst, send_sem=ssem, recv_sem=rsem,
            device_id={"wide": u}, device_id_type=MESH,
        )

    pending = []

    def start(copy):
        copy.start()
        pending.append(copy)
        return copy

    own = rows(n, TB)
    xbuf = s_ref.at[:, 0:D]
    ograd = s_ref.at[:, D:2 * D]
    orth = mT
    rln = rdn
    otok = cot

    l_tok = pltpu.make_async_copy(tok_h, tok.at[own], loc_sem.at[0])
    l_win = pltpu.make_async_copy(win_h, win_f, loc_sem.at[1])
    l_wout = pltpu.make_async_copy(wout_h, wout_f, loc_sem.at[2])
    l_cot = pltpu.make_async_copy(cot_h, cot, loc_sem.at[3])
    l_min = pltpu.make_async_copy(min_h, win_f, loc_sem.at[4])
    l_mout = pltpu.make_async_copy(mout_h, mT.at[pl.ds(4, 2)], loc_sem.at[5])
    for c in (l_tok, l_win, l_wout, l_cot, l_mout):
        c.start()

    barrier = pltpu.get_barrier_semaphore()
    for x in (1, 2, 3):
        pl.semaphore_signal(barrier, inc=1, device_id={"narrow": rel(x)}, device_id_type=MESH)

    def greet(i, c):
        pl.semaphore_signal(
            barrier, inc=1, device_id={"wide": g * OWN + lax.rem(o + i, OWN)}, device_id_type=MESH
        )
        return c

    lax.fori_loop(1, OWN, greet, 0)

    def greet_group(i, c):
        pl.semaphore_signal(
            barrier, inc=1, device_id={"wide": lax.rem(g + i, groups) * OWN + o}, device_id_type=MESH
        )
        return c

    if groups > 1:
        lax.fori_loop(1, groups, greet_group, 0)
    pay[n] = pay_i[...]
    l_tok.wait()
    pl.semaphore_wait(barrier, 3 + (OWN - 1) + (groups - 1))

    half = TB // 2

    def ag_rows(t, c):
        return tok.at[pl.ds(pl.multiple_of(t * TB + c * half, half), half)]

    for x in (1, 2, 3):
        start(ncopy(pay.at[n], pay.at[n], pay_s.at[x], pay_r.at[x], rel(x)))
    for c in (0, 1):
        start(ncopy(ag_rows(n, c), ag_rows(n, c), ag_s.at[2 + c], ag_r.at[2 + c], n2))
    for c in (0, 1):
        start(ncopy(ag_rows(n, c), ag_rows(n, c), ag_s.at[c], ag_r.at[c], n1))

    def arrived(slot, sem_s, sem_r, t):
        ncopy(slot, slot, sem_s, sem_r, t).wait_recv()

    l_win.wait()
    for k in range(3):
        piece = win_f[k]
        wqkvT[k * CW:(k + 1) * CW, :] = piece.T.astype(BF16)
        wqkv[:, k * CW:(k + 1) * CW] = piece.astype(BF16)
    mycols = pl.ds(pl.multiple_of(n * CW, CW), CW)
    wup[:, mycols] = win_f[3].astype(BF16)
    l_min.start()
    l_wout.wait()
    for k in range(2):
        wod[k, mycols, :] = wout_f[k].astype(BF16)

    def wg_list(sems, semr, x, t, target):
        cols = pl.ds(pl.multiple_of(t * CW, CW), CW)
        return [
            ncopy(wod.at[:, cols, :], wod.at[:, cols, :], sems.at[x, 0], semr.at[x, 0], target),
            ncopy(wup.at[:, cols], wup.at[:, cols], sems.at[x, 1], semr.at[x, 1], target),
        ]

    for x in (2, 1):
        for c in wg_list(wg_s, wg_r, x, n, rel(x)):
            start(c)

    bcol[0] = jnp.broadcast_to(split[0:1, :], (CW, CW)).T
    bcol[1] = jnp.broadcast_to(split[1:2, :], (CW, CW)).T

    def project(t):
        tb = tok[rows(t, TB), :]
        qk = mm(tb, wqkv[:, 0:2 * CW])
        q = (qk[:, :CW] + split[0:1, :]).astype(BF16)
        k = qk[:, CW:].astype(BF16)
        q8 = q.astype(F32) * 0.125
        prod = q8 * k.astype(F32)
        lane = lax.broadcasted_iota(jnp.int32, (TB, CW), 1)
        low = lane < HD
        d0 = jnp.sum(jnp.where(low, prod, 0.0), axis=1, keepdims=True)
        d1 = jnp.sum(jnp.where(low, 0.0, prod), axis=1, keepdims=True)
        rdn[rows(t, TB), :] = jnp.where(low, d0, d1)
        lane1 = lax.broadcasted_iota(jnp.int32, (CW, CW), 1).astype(F32)
        for j in range(TB // CW):
            seg = jnp.broadcast_to(pay[t, j:j + 1, :], (CW, CW)).T
            part = q8[j * CW:(j + 1) * CW, :]
            lowj = lane1 < HD
            hot = lambda base: jnp.where(seg == lane1 + base, 1.0, 0.0)
            rr = pl.ds(pl.multiple_of(t * TB + j * CW, CW), CW)
            qp[0, rr, 0:CW] = jnp.where(lowj, part, hot(-float(HD))).astype(BF16)
            qp[1, rr, 0:CW] = jnp.where(lowj, hot(0.0), part).astype(BF16)
            rest = hot(float(HD)).astype(BF16)
            qp[0, rr, CW:] = rest
            qp[1, rr, CW:] = rest
        tT = mm_nt(wqkvT[...], tb)
        bq = jnp.concatenate([bcol[0]] * (TB // CW), axis=1)
        bv = jnp.concatenate([bcol[1]] * (TB // CW), axis=1)
        cols = rows(t, TB)
        qT[:, cols] = ((tT[0:CW] + bq).astype(BF16).astype(F32) * 0.125).astype(BF16)
        kT = tT[CW:2 * CW].astype(BF16)
        vT = (tT[2 * CW:] + bv).astype(BF16)
        code = jnp.concatenate([pay[t, 4 + j:5 + j, :] for j in range(TB // CW)], axis=1)
        rowi = lax.broadcasted_iota(jnp.int32, (HD, TB), 0).astype(F32)
        keep = lambda base: jnp.where(code == rowi + base, 0.0, NEG).astype(BF16)
        first, second, third = keep(0.0), keep(float(HD)), keep(float(2 * HD))
        ones = jnp.ones((HD, TB), BF16)
        kTp[0, 0:HD, cols] = kT[0:HD]
        kTp[0, HD:CW, cols] = first
        kTp[1, 0:HD, cols] = first
        kTp[1, HD:CW, cols] = kT[HD:]
        vTp[0, 0:HD, cols] = vT[0:HD]
        vTp[0, HD:, cols] = ones
        vTp[1, 0:HD, cols] = ones
        vTp[1, HD:, cols] = vT[HD:]
        for h in range(2):
            kTp[h, CW:CW + HD, cols] = second
            kTp[h, CW + HD:, cols] = third

    def project_step(i, _):
        @pl.when(i == 1)
        def _():
            arrived(pay.at[n1], pay_s.at[1], pay_r.at[1], n1)
            for c in (0, 1):
                arrived(ag_rows(n1, c), ag_s.at[c], ag_r.at[c], n1)
            l_min.wait()
            for k in range(4):
                mT[k] = win_f[k].T

        @pl.when(i == 2)
        def _():
            arrived(pay.at[n2], pay_s.at[2], pay_r.at[2], n2)
            arrived(pay.at[n3], pay_s.at[3], pay_r.at[3], n3)
            for c in (0, 1):
                arrived(ag_rows(n2, c), ag_s.at[2 + c], ag_r.at[2 + c], n2)
                ncopy(ag_rows(n2, c), ag_rows(n2, c), rly_s.at[c], rly_r.at[c], n1).start()

        @pl.when(i == 3)
        def _():
            for c in (0, 1):
                arrived(ag_rows(n3, c), rly_s.at[c], rly_r.at[c], n1)

        project(rel(i))
        return 0

    lax.fori_loop(0, NAR, project_step, 0)
    for c in (0, 1):
        pending.append(ncopy(ag_rows(n2, c), ag_rows(n2, c), rly_s.at[c], rly_r.at[c], n1))

    eye = lax.broadcasted_iota(jnp.int32, (CW, CW), 0) == lax.broadcasted_iota(jnp.int32, (CW, CW), 1)

    def ctx_copy(x, t):
        return ncopy(
            ctx_s.at[rows(t, TB)], ctxf.at[:, mycols], ctx_sem.at[x], ctx_rem.at[x], t
        )

    def attend(i, _):
        hi = 1 - i // 2
        lo = lax.rem((i + 1) // 2, 2)
        t = lax.rem(b0 + lo, 2) + 2 * lax.rem(b1 + hi, 2)
        rr = rows(t, TB)
        parts = []
        for h in range(2):
            s_ref[...] = mm(qp[h, rr, :], kTp[h])
            for j in range(TB // CW):
                cc = pl.ds(pl.multiple_of(t * TB + j * CW, CW), CW)
                diag = rdn[cc, h * HD:h * HD + 1]
                sub = pl.ds(j * CW, CW)
                s_ref[sub, cc] = jnp.where(eye, diag, s_ref[sub, cc])
            s = s_ref[...]
            top = jnp.max(s, axis=1, keepdims=True)
            e = jnp.exp(s - top).astype(BF16)
            e_ref[h, rr, :] = e
            parts.append(mm_nt(vTp[h], e))
        num = jnp.concatenate([parts[0][:HD], parts[1][HD:]], axis=0)
        den = 1.0 / jnp.concatenate([parts[0][HD:], parts[1][:HD]], axis=0)
        cn = (num * den).T
        ctxn[rr, :] = cn
        rln[rr, :] = den.T
        ctx_s[rr, :] = cn.astype(BF16)

        @pl.when(i < 3)
        def _():
            x = lo + 2 * hi
            ctx_copy(x, t).start()

        @pl.when(i == 0)
        def _():
            for c in wg_list(wg_s, wg_r, 2, n2, n2):
                c.wait_recv()
            for c in wg_list(wr_s, wr_r, 0, n2, n1):
                c.start()

        return 0

    lax.fori_loop(0, NAR, attend, 0)
    pending.extend(wg_list(wr_s, wr_r, 0, n2, n1))
    for x in (1, 2, 3):
        pending.append(ctx_copy(x, rel(x)))
    ctxf[:, mycols] = ctx_s[own, :]
    for c in wg_list(wg_s, wg_r, 1, n1, n1):
        c.wait_recv()
    for c in wg_list(wr_s, wr_r, 0, n3, n1):
        c.wait_recv()
    l_cot.wait()
    l_mout.wait()
    for x in (2, 3, 1):
        cols = pl.ds(pl.multiple_of(rel(x) * CW, CW), CW)
        ncopy(ctx_s.at[own], ctxf.at[:, cols], ctx_sem.at[x], ctx_rem.at[x], rel(x)).wait_recv()

    up_bias = jnp.concatenate([pay[t, 8:9, :] for t in range(NAR)], axis=1)
    vecs[n] = jnp.zeros((8, D), F32)

    def dc_copy(x, c, t, me):
        rr = pl.ds(c * MID, MID)
        cols = pl.ds(pl.multiple_of(t * CW, CW), CW)
        dst = dcr.at[pl.ds(pl.multiple_of(me * TB + c * MID, MID), MID)]
        return ncopy(dcst.at[rr, cols], dst, dc_sem.at[x, c], dc_rem.at[x, c], t)

    def middle(c, _):
        rr = pl.ds(pl.multiple_of(c * MID, MID), MID)
        ga1, be1, ga2, be2, ba, bd = (shared[k:k + 1, :] for k in range(6))
        x0 = tok[pl.ds(pl.multiple_of(n * TB + c * MID, MID), MID), :].astype(F32)
        r1 = x0 + (mm(ctxf[rr, :], wod[0]) + ba)
        c1 = r1 - jnp.mean(r1, axis=1, keepdims=True)
        s1 = lax.rsqrt(jnp.mean(c1 * c1, axis=1, keepdims=True) + 1e-05)
        x1 = c1 * s1
        hidden = x1 * ga1 + be1
        low = hidden.astype(BF16)
        hr[rr, :] = low
        upper = mm(low, wup[...]) + up_bias
        cdf = 0.5 * (1.0 + lax.erf(upper * (1.0 / math.sqrt(2.0))))
        pdf = jnp.exp(-0.5 * upper * upper) * (1.0 / math.sqrt(2.0 * math.pi))
        slope = cdf + upper * pdf
        a = (upper * cdf).astype(BF16)
        act[rr, :] = a
        r2 = hidden + (mm(a, wod[1]) + bd)
        c2 = r2 - jnp.mean(r2, axis=1, keepdims=True)
        s2 = lax.rsqrt(jnp.mean(c2 * c2, axis=1, keepdims=True) + 1e-05)
        x2 = c2 * s2
        dy = cot[rr, :].astype(F32)
        otok[rr, :] = (x2 * ga2 + be2).astype(BF16)
        dn = dy * ga2
        dr2 = s2 * (
            dn - jnp.mean(dn, axis=1, keepdims=True) - x2 * jnp.mean(dn * x2, axis=1, keepdims=True)
        )
        d2 = dr2.astype(BF16)
        dr2r[rr, :] = d2
        dup = (mm_nt(d2, wod[1]) * slope).astype(BF16)
        du[rr, :] = dup
        dh = dr2 + mm_nt(dup, wup[...])
        en = dh * ga1
        d1f = s1 * (
            en - jnp.mean(en, axis=1, keepdims=True) - x1 * jnp.mean(en * x1, axis=1, keepdims=True)
        )
        dr1[rr, :] = d1f
        d1 = d1f.astype(BF16)
        dr1r[rr, :] = d1
        dcst[rr, :] = mm_nt(d1, wod[0]).astype(BF16)
        add = lambda v: jnp.sum(v, axis=0, keepdims=True)
        vecs[n] += jnp.concatenate(
            [
                add(dh * x1), add(dh), add(dy * x2), add(dy), add(d1f), add(dr2),
                add(dup.astype(F32)), jnp.zeros((1, D), F32),
            ],
            axis=0,
        )
        for k in range(TB // MID):
            @pl.when(c == k)
            def _():
                for x in (2, 3, 1):
                    dc_copy(x, k, rel(x), n).start()

        dcr[pl.ds(pl.multiple_of(n * TB + c * MID, MID), MID), :] = dcst[rr, mycols]
        return 0

    lax.fori_loop(0, TB // MID, middle, 0)
    for x in (1, 2, 3):
        for c in range(TB // MID):
            pending.append(dc_copy(x, c, rel(x), n))
    l_otok = pltpu.make_async_copy(otok, otok_h, loc_sem.at[6])
    l_otok.start()
    for x in (1, 2, 3):
        start(ncopy(vecs.at[n], vecs.at[n], vn_s.at[x], vn_r.at[x], rel(x)))

    for k, (left, right) in enumerate(((du, hr), (ctxf, dr1r), (act, dr2r))):
        grad = mm_tn(left[...], right[...]).astype(BF16)
        for t in range(NAR):
            gst[t, k] = grad[t * CW:(t + 1) * CW]
    start(ncopy(gst.at[n3], gr1.at[1], g1_s.at[1], g1_r.at[1], n1))
    start(ncopy(gst.at[n1], gr1.at[0], g1_s.at[0], g1_r.at[0], n1))

    def group_loop(fn, first=1, count=OWN):
        def go(i, c):
            fn(i)
            return c

        lax.fori_loop(first, count, go, 0)

    def member(i):
        return lax.rem(o + i, OWN)

    def scatter(i, src, dst, ssem, rsem):
        u = member(i)
        piece = pl.ds(pl.multiple_of(u * PR, PR), PR)
        return wcopy(src.at[:, piece, :], dst.at[o], ssem.at[i], rsem.at[o], g * OWN + u)

    def scatter_all(*where):
        group_loop(lambda i: scatter(i, *where).start())

    def scatter_done(*where):
        group_loop(lambda i: scatter(i, *where).wait_send())

    mine = pl.ds(pl.multiple_of(o * PR, PR), PR)
    place = pl.ds(pl.multiple_of(n * CW + o * PR, PR), PR)

    def across(k, i):
        return wcopy(
            grp.at[k, g], grp.at[k, g], gp_s.at[k, i], gp_r.at[k, g], lax.rem(g + i, groups) * OWN + o
        )

    def collect(base, src, dst, ssem, rsem):
        k = 0 if base == 3 else 1
        dst[o] = src[:, mine, :]

        def take(i):
            v = member(i)
            wcopy(src.at[:, mine, :], dst.at[v], ssem.at[0], rsem.at[v], g * OWN + v).wait_recv()

        group_loop(take)
        total = lax.fori_loop(
            0, OWN, lambda v, t: t + dst[v].astype(F32), jnp.zeros((3, PR, D), F32)
        )
        if groups > 1:
            grp[k, g] = total.astype(BF16)
            group_loop(lambda i: across(k, i).start(), 1, groups)

            def meet(i):
                v = lax.rem(g + i, groups)
                wcopy(grp.at[k, v], grp.at[k, v], gp_s.at[k, i], gp_r.at[k, v], v * OWN + o).wait_recv()

            group_loop(meet, 1, groups)
            total = lax.fori_loop(
                0, groups, lambda v, t: t + grp[k, v].astype(F32), jnp.zeros((3, PR, D), F32)
            )
        total = total + 0.5 * mT[pl.ds(base, 3), mine, :]
        mom[pl.ds(base, 3), place, :] = total.astype(BF16)
        group_loop(lambda i: share(base, o, i).start())

    def share(base, u, i):
        ref = mom.at[pl.ds(base, 3), pl.ds(pl.multiple_of(n * CW + u * PR, PR), PR), :]
        k = 0 if base == 3 else 1
        return wcopy(ref, ref, aw_s.at[k, i], aw_r.at[k, u], g * OWN + member(i))

    def share_wait(base):
        group_loop(lambda i: share(base, member(i), i).wait_recv())

    def share_done(base):
        group_loop(lambda i: share(base, o, i).wait_send())

    def vec_copy(buf, ss, rs, i, v):
        return wcopy(buf.at[v], buf.at[v], ss.at[i], rs.at[v], g * OWN + member(i))

    def vec_across(buf, ss, rs, i, v):
        ref = buf.at[OWN + v]
        return wcopy(ref, ref, ss.at[OWN + i], rs.at[OWN + v], lax.rem(g + i, groups) * OWN + o)

    def vec_send(*where):
        group_loop(lambda i: vec_copy(*where, i, o).start())

    def vec_sum(buf, ss, rs):
        group_loop(lambda i: vec_copy(buf, ss, rs, i, member(i)).wait_recv())
        zero = jnp.zeros(buf.shape[1:], F32)
        total = lax.fori_loop(0, OWN, lambda v, t: t + buf[v], zero)
        if groups > 1:
            buf[OWN + g] = total
            group_loop(lambda i: vec_across(buf, ss, rs, i, g).start(), 1, groups)
            group_loop(
                lambda i: vec_across(buf, ss, rs, i, lax.rem(g + i, groups)).wait_recv(), 1, groups
            )
            total = lax.fori_loop(0, groups, lambda v, t: t + buf[OWN + v], zero)
        return total

    def vec_done(buf, ss, rs):
        group_loop(lambda i: vec_copy(buf, ss, rs, i, o).wait_send())
        if groups > 1:
            group_loop(lambda i: vec_across(buf, ss, rs, i, g).wait_send(), 1, groups)

    def spread(m, x, t, target, sems, semr):
        ref = mom.at[m, pl.ds(pl.multiple_of(t * CW, CW), CW), :]
        return ncopy(ref, ref, sems.at[m, x], semr.at[m, x], target)

    dkT[...] = jnp.zeros_like(dkT)
    dvT[...] = jnp.zeros_like(dvT)
    lane = lax.broadcasted_iota(jnp.int32, (TB, CW), 1)
    low_lane = lane < HD

    def backward(i, _):
        t = rel(i)
        rr = rows(t, TB)

        @pl.when(i > 0)
        def _():
            for c in range(TB // MID):
                dst = dcr.at[pl.ds(pl.multiple_of(t * TB + c * MID, MID), MID)]
                ncopy(
                    dcst.at[pl.ds(c * MID, MID), mycols], dst, dc_sem.at[i, c], dc_rem.at[i, c], t
                ).wait_recv()

        dcs = (dcr[rr, :].astype(F32) * rln[rr, :]).astype(BF16)
        full = dcs.astype(F32)
        prod = full * ctxn[rr, :]
        delta = (
            jnp.sum(jnp.where(low_lane, prod, 0.0), axis=1, keepdims=True),
            jnp.sum(jnp.where(low_lane, 0.0, prod), axis=1, keepdims=True),
        )
        dcT = full.T.astype(BF16)
        for h in range(2):
            hs = slice(h * HD, (h + 1) * HD)
            top = delta[h].astype(BF16).astype(F32)
            tail = delta[h] - top
            base = (1 - h) * HD
            extra = jnp.where(lane == base, -top, jnp.where(lane == base + 1, -tail, 0.0))
            left = jnp.where(low_lane == (h == 0), full, extra).astype(BF16)
            s_ref[...] = mm(left, vTp[h])
            e = e_ref[h, rr, :]
            ds = e * s_ref[...].astype(BF16)
            gT[hs, rr] = (mm_nt(kTp[h, hs, :], ds) * 0.125).astype(BF16)
            dkT[hs, :] += mm(qT[hs, rr], ds)
            dvT[hs, :] += mm(dcT[hs, :], e)

        @pl.when(i == 0)
        def _():
            for k in (1, 0):
                ncopy(gst.at[n1], gr1.at[k], g1_s.at[k], g1_r.at[k], n1).wait_recv()
            gs2[...] = (gst[n2].astype(F32) + gr1[1].astype(F32)).astype(BF16)
            ncopy(gs2, gr2, g2_s, g2_r, n2).start()
            for x in (1, 2, 3):
                arrived(vecs.at[rel(x)], vn_s.at[x], vn_r.at[x], rel(x))
            vecw[o] = ((vecs[0] + vecs[1]) + vecs[2]) + vecs[3]
            vec_send(vecw, vw_s, vw_r)

        @pl.when(i == 2)
        def _():
            ncopy(gs2, gr2, g2_s, g2_r, n2).wait_recv()
            est[...] = (gst[n].astype(F32) + gr1[0].astype(F32) + gr2[...].astype(F32)).astype(BF16)
            scatter_all(est, erx, es_s, es_r)

        return 0

    lax.fori_loop(0, NAR, backward, 0)
    pending.append(ncopy(gs2, gr2, g2_s, g2_r, n2))
    gT[CW:2 * CW, :] = dkT[...].astype(BF16)
    gT[2 * CW:, :] = dvT[...].astype(BF16)

    gin = mm(gT[...], tok[...]).astype(BF16)
    for k in range(3):
        lst[k] = gin[k * CW:(k + 1) * CW]
    scatter_all(lst, lrx, ls_s, ls_r)
    one = jnp.ones((8, LEN), BF16)
    lv[o, 0:8, :] = mm_nt(one, gT[0:CW, :])
    lv[o, 8:16, :] = mm_nt(one, gT[2 * CW:, :])
    vec_send(lv, lv_s, lv_r)
    collect(3, est, erx, es_s, es_r)

    def dx(t):
        return mm(wqkv[...], gT[:, rows(t, TB)])

    dxs[1] = dx(n3).astype(BF16)
    start(ncopy(dxs.at[1], dxr1.at[1], dx1_s.at[1], dx1_r.at[1], n1))
    dxs[0] = dx(n1).astype(BF16)
    start(ncopy(dxs.at[0], dxr1.at[0], dx1_s.at[0], dx1_r.at[0], n1))
    over = dx(n2)
    ncopy(dxs.at[1], dxr1.at[1], dx1_s.at[1], dx1_r.at[1], n1).wait_recv()
    dxs2[...] = (over + dxr1[1].astype(F32)).astype(BF16)
    start(ncopy(dxs2, dxr2, dx2_s, dx2_r, n2))
    ograd[...] = dx(n).T + dr1[...]

    share_wait(3)

    def fan(base):
        for m in range(base, base + 3):
            start(spread(m, 1, n, n2, an_s, an_r))
            start(spread(m, 0, n, n1, an_s, an_r))

    def newton(m):
        xin = mom[m].astype(F32)
        norm = jnp.sqrt(jnp.sum(xin * xin)) + 1e-07
        xbuf[...] = xin / norm

        def step(_, c):
            x = xbuf[...]
            xl = x.astype(BF16)
            a = mm_nt(xl, xl)
            al = a.astype(BF16)
            p = (COEF_B * a + COEF_C * mm(al, al)).astype(BF16)
            xbuf[...] = COEF_A * x + mm(p, xl)
            return c

        lax.fori_loop(0, NS_ITERS, step, 0)
        orth[m] = xbuf[mycols, :]

    fan(3)
    collect(0, lst, lrx, ls_s, ls_r)
    for m in range(3, 6):
        spread(m, 1, n2, n2, an_s, an_r).wait_recv()
        start(spread(m, 0, n2, n1, ar_s, ar_r))
    share_wait(0)
    fan(0)
    for m in range(3, 6):
        spread(m, 0, n1, n1, an_s, an_r).wait_recv()
        spread(m, 0, n3, n1, ar_s, ar_r).wait_recv()

    def newton_late(m, c):
        newton(m)
        return c

    lax.fori_loop(3, 6, newton_late, 0)
    for m in range(0, 3):
        spread(m, 1, n2, n2, an_s, an_r).wait_recv()
        start(spread(m, 0, n2, n1, ar_s, ar_r))

    ncopy(dxs.at[0], dxr1.at[0], dx1_s.at[0], dx1_r.at[0], n1).wait_recv()
    ncopy(dxs2, dxr2, dx2_s, dx2_r, n2).wait_recv()
    ograd[...] = ograd[...] + (dxr1[0].astype(F32) + dxr2[...].astype(F32)).T
    l_ograd = pltpu.make_async_copy(ograd, ograd_h, loc_sem.at[7])
    l_ograd.start()

    for m in range(0, 3):
        spread(m, 0, n1, n1, an_s, an_r).wait_recv()
        spread(m, 0, n3, n1, ar_s, ar_r).wait_recv()
    l_mom = pltpu.make_async_copy(mom.at[:, mycols, :], omom_h, loc_sem.at[8])
    l_mom.start()
    lax.fori_loop(0, 3, newton_late, 0)
    l_orth = pltpu.make_async_copy(orth, oorth_h, loc_sem.at[9])
    l_orth.start()

    ovec[...] = vec_sum(vecw, vw_s, vw_r)
    ovec2[...] = vec_sum(lv, lv_s, lv_r)

    for c in pending:
        c.wait_send()
    vec_done(vecw, vw_s, vw_r)
    vec_done(lv, lv_s, lv_r)
    if groups > 1:
        for k in (0, 1):
            group_loop(lambda i: across(k, i).wait_send(), 1, groups)
    scatter_done(est, erx, es_s, es_r)
    scatter_done(lst, lrx, ls_s, ls_r)
    share_done(3)
    share_done(0)
    l_otok.wait()
    l_ograd.wait()
    l_mom.wait()
    l_orth.wait()


def run_layer(wide, tokens, cotangent, pay, in_w, out_w, in_m, out_m, shared, split):
    any_ = pl.BlockSpec(memory_space=pl.ANY)
    vm = pl.BlockSpec(memory_space=pltpu.VMEM)
    V = pltpu.VMEM
    dma = lambda *s: pltpu.SemaphoreType.DMA(s)
    one = pltpu.SemaphoreType.DMA
    groups = wide // OWN
    vslots = OWN + (groups if groups > 1 else 0)
    scratch = [
        V((LEN, D), BF16), V((TB, D), BF16), V((NAR, 16, CW), F32),
        V((4, D, CW), F32), V((2, CW, D), F32), V((6, CW, D), F32),
        V((3 * CW, D), BF16), V((D, 3 * CW), BF16),
        V((D, D), BF16), V((2, D, D), BF16), V((2, CW, CW), F32),
        V((2, LEN, 2 * CW), BF16), V((2, 2 * CW, LEN), BF16), V((2, CW, LEN), BF16), V((CW, LEN), BF16),
        V((LEN, CW), F32), V((TB, LEN), F32), V((2, LEN, LEN), BF16),
        V((LEN, CW), F32), V((LEN, CW), BF16), V((TB, D), BF16),
        V((TB, D), BF16), V((TB, D), BF16), V((TB, D), BF16), V((TB, D), BF16), V((TB, D), BF16),
        V((TB, D), F32), V((TB, D), BF16), V((LEN, CW), BF16),
        V((NAR, 8, D), F32), V((vslots, 8, D), F32), V((CW, LEN), F32), V((CW, LEN), F32), V((3 * CW, LEN), BF16),
        V((NAR, 3, CW, D), BF16), V((2, 3, CW, D), BF16), V((3, CW, D), BF16), V((3, CW, D), BF16),
        V((3, CW, D), BF16), V((OWN, 3, PR, D), BF16), V((3, CW, D), BF16), V((OWN, 3, PR, D), BF16),
        V((vslots, 16, CW), F32), V((6, D, D), BF16), V((2, groups if groups > 1 else 1, 3, PR, D), BF16),
        V((2, D, TB), BF16), V((2, D, TB), BF16), V((D, TB), BF16), V((D, TB), BF16),
        dma(10), dma(4), dma(4), dma(2), dma(2), dma(4), dma(4), dma(3, 2), dma(3, 2), dma(1, 2), dma(1, 2),
        dma(4), dma(4), dma(4, TB // MID), dma(4, TB // MID), dma(4), dma(4), dma(vslots), dma(vslots),
        dma(2), dma(2), one, one, dma(OWN), dma(OWN), dma(OWN), dma(OWN), dma(vslots), dma(vslots),
        dma(2, groups), dma(2, groups), dma(2, OWN), dma(2, OWN), dma(6, 2), dma(6, 2), dma(6, 2), dma(6, 2), dma(2), dma(2), one, one,
    ]
    return pl.pallas_call(
        functools.partial(layer_kernel, wide),
        out_shape=[
            jax.ShapeDtypeStruct((TB, D), BF16),
            jax.ShapeDtypeStruct((TB, D), F32),
            jax.ShapeDtypeStruct((6, CW, D), BF16),
            jax.ShapeDtypeStruct((6, CW, D), F32),
            jax.ShapeDtypeStruct((8, D), F32),
            jax.ShapeDtypeStruct((16, CW), F32),
        ],
        in_specs=[any_, any_, vm, any_, any_, any_, any_, vm, vm],
        out_specs=[any_, any_, any_, any_, vm, vm],
        scratch_shapes=scratch,
        compiler_params=pltpu.CompilerParams(
            collective_id=0, has_side_effects=True, vmem_limit_bytes=62 * MB
        ),
        name="layer",
    )(tokens, cotangent, pay, in_w, out_w, in_m, out_m, shared, split)


def muon_step(weights, orthogonal):
    return weights - 0.2 * (0.2 * math.sqrt(D) * orthogonal + 0.01 * weights)


def adam_step(values, moment_one, moment_two, gradient):
    moment_one = 0.9 * moment_one + 0.1 * gradient
    moment_two = 0.999 * moment_two + 0.001 * gradient * gradient
    step_ratio = (
        moment_one / (1.0 - 0.9**STEP) / (jnp.sqrt(moment_two / (1.0 - 0.999**STEP)) + 1e-08)
    )
    return (moment_one, moment_two, values - 0.3 * (step_ratio + 0.01 * values))


def blend(average, weights):
    return 0.6 * average + 0.4 * weights


def update_kernel(
    otok, ograd, mom, orth, in_w, out_w, in_a, out_a,
    tok_o, grad_o, inm_o, outm_o, inw_o, outw_o, inl_o, outl_o, ina_o, outa_o,
):
    tok_o[...] = otok[...]
    grad_o[...] = ograd[...]
    for k in range(4):
        inm_o[k] = mom[k].astype(F32).T
        new = muon_step(in_w[k], orth[k].T)
        inw_o[k] = new
        inl_o[k] = new.astype(BF16)
        ina_o[k] = blend(in_a[k], new)
    for k in range(2):
        outm_o[k] = mom[4 + k].astype(F32)
        new = muon_step(out_w[k], orth[4 + k])
        outw_o[k] = new
        outl_o[k] = new.astype(BF16)
        outa_o[k] = blend(out_a[k], new)


def run_update(otok, ograd, mom, orth, in_w, out_w, in_a, out_a):
    vm = pl.BlockSpec(memory_space=pltpu.VMEM)
    S = jax.ShapeDtypeStruct
    return pl.pallas_call(
        update_kernel,
        out_shape=[
            S((TB, D), BF16), S((TB, D), F32), S((4, D, CW), F32), S((2, CW, D), F32),
            S((4, D, CW), F32), S((2, CW, D), F32), S((4, D, CW), BF16), S((2, CW, D), BF16),
            S((4, D, CW), F32), S((2, CW, D), F32),
        ],
        in_specs=[vm] * 8,
        out_specs=[vm] * 10,
        compiler_params=pltpu.CompilerParams(vmem_limit_bytes=40 * MB),
        name="update",
    )(otok, ograd, mom, orth, in_w, out_w, in_a, out_a)


def body(
    wide, tokens, cotangent, segments, padding, generative, in_weights, out_weights, in_momenta,
    out_momenta, in_average, out_average, shared_values, shared_moment1, shared_moment2,
    shared_average, split_values, split_moment1, split_moment2, split_average,
):
    is_open = (padding == 0) & (generative == 0)
    pay = jnp.concatenate(
        [
            segments.reshape(TB // CW, CW).astype(F32),
            jnp.where(is_open, segments, -1).reshape(TB // CW, CW).astype(F32),
            split_values[2:3],
            jnp.zeros((7, CW), F32),
        ],
        axis=0,
    )
    otok, ograd, mom, orth, vec, vec2 = run_layer(
        wide, tokens, cotangent, pay, in_weights, out_weights, in_momenta, out_momenta,
        shared_values, split_values,
    )
    (
        result, grad_tokens, moment_in, moment_out, new_in, new_out, low_in, low_out, avg_in, avg_out,
    ) = run_update(otok, ograd, mom, orth, in_weights, out_weights, in_average, out_average)
    place = lax.axis_index("narrow") * CW
    sum_split = jnp.concatenate(
        [vec2[0:1], vec2[8:9], lax.dynamic_slice(vec, (6, place), (1, CW))], axis=0
    )
    shared_one, shared_two, shared_new = adam_step(
        shared_values, shared_moment1, shared_moment2, vec[:6]
    )
    split_one, split_two, split_new = adam_step(
        split_values, split_moment1, split_moment2, sum_split
    )
    return (
        result, grad_tokens, moment_in, moment_out, new_in, new_out, low_in, low_out, avg_in, avg_out,
        shared_one, shared_two, shared_new, blend(shared_average, shared_new),
        split_one, split_two, split_new, blend(split_average, split_new),
    )


def solution(mesh):
    rows = P(("wide", "narrow"), None)
    flat = P(("wide", "narrow"))
    cols = P(None, None, "narrow")
    outs = P(None, "narrow", None)
    vec = P(None, "narrow")
    return jax.shard_map(
        functools.partial(body, mesh.shape["wide"]),
        mesh=mesh,
        in_specs=(
            rows, rows, flat, flat, flat, cols, outs, cols, outs, cols, outs,
            P(), P(), P(), P(), vec, vec, vec, vec,
        ),
        out_specs=(
            rows, rows, cols, outs, cols, outs, cols, outs, cols, outs,
            P(), P(), P(), P(), vec, vec, vec, vec,
        ),
        check_vma=False,
    )
```

time: 620 us -> 141 us (0.23); the launches traced: 611 us -> 139 us
  waiting for transfers between devices: 311 us -> 0 us
  Pallas kernels: 0 us -> 126 us
  matrix products: 108 us -> 0 us
  blocking collectives: 85.6 us -> 0 us
  other arithmetic: 67.3 us -> 2.69 us
  between operations: 16 us -> 0.77 us
  local copies, waits for them, and re-layouts: 20.9 us -> 8.65 us
    reduce_scatter x4 -> x0, waiting for transfers between devices: 133 us -> none  [the longest x1 44.6 us: body(): lax.psum_scatter(jnp.dot(context_low, low_out[0], preferred_element_type=...]
    pallas_call x0 -> x2, Pallas kernels: none -> 126 us  [the longest x1 123 us: run_layer(): pl.pallas_call(functools.partial(layer_kernel, wide), out_shape=[jax.Shap...]
    psum x2 -> x0, waiting for transfers between devices: 110 us -> none  [the longest x1 88.7 us: body(): lax.psum((grad_in, grad_out, grad_split), 'wide')]
    dot_general x49 -> x0, matrix products: 108 us -> none  [the longest x8 13.1 us: masked_scores(): jnp.einsum('qhe,khe->hqk', q_block, k_row, preferred_element_type=jnp.flo...]
    all_gather x4 -> x0, waiting for transfers between devices: 67.9 us -> none  [the longest x1 22.7 us: body(): lax.all_gather(grad_second.astype(jnp.bfloat16), 'narrow', axis=0, tiled=...]
    psum x2 -> x0, blocking collectives: 61.2 us -> none  [the longest x1 40.2 us: body(): sum_shared = lax.psum(grad_shared, ('wide', 'narrow'))]
    all_gather x4 -> x0, blocking collectives: 24.4 us -> none  [the longest x1 7.37 us: body(): lax.all_gather(chosen.astype(jnp.bfloat16), 'narrow', axis=1, tiled=True)]
    reduce_sum x16 -> x0, other arithmetic: 23.2 us -> none  [the longest x4 10.1 us: per_block(): row_total = jnp.sum(exp_terms, axis=-1, keepdims=True)]
  transfers between devices with their start and end apart: 10 -> 0, of which waited for: 10 -> 0; matrix products, arithmetic and copies ran while one was open for 4% -> 0% of each run, Pallas kernels for 0% -> 0%
where the time goes in v1:
time: 141 us; the launch traced here: 139 us
  Pallas kernels  126 us (89%)
  local copies, waits for them, and re-layouts  8.65 us (6%)
  other arithmetic  2.69 us (2%)
    pallas_call x1, Pallas kernels, run_layer(): pl.pallas_call(functools.partial(layer_kernel, wide), out_shape=[jax.Shap...  123 us
    unnamed x34, local copies, waits for them, and re-layouts  7.12 us
    pallas_call x1, Pallas kernels, run_update(): pl.pallas_call(update_kernel, out_shape=[S((TB, D), BF16), S((TB, D), F32...  3.53 us

profile of v1, /device:TPU:0, one launch (start us, length us, event | category | flops | bytes accessed | tf_op | source)
XLA Modules:
  0.0 138.6 jit_solution(10216295655009140611)
XLA Ops:
  0.7 0.8 convert_bitcast_fusion.1
  1.4 0.1 pad.6.clone
  1.5 0.7 slice.12
  2.2 0.7 maximum_maximum_fusion.refs_2_
  2.9 0.0 copy-start.13
  2.9 0.0 copy-start.15
  2.9 0.0 copy-start.16
  2.9 0.0 copy-start
  2.9 0.0 copy-start.1
  2.9 123.0 %layer.1 = (bf16[512,512]{1,0:T(8,128)(2,1)}, f32[512,512]{1,0:T(8,128)}, bf16[6,128,512]{2,1,0:T(8,128)(2,1)}, f32[6,128,512]{2,1,0:T(8,128)}, f32[8,512]{1,0:T(8,128)}, /*index=5*/f32[16,128]{1,0:T(8,128)}) custom-call(bf16[512,512]{1,0:T(8,128)(2,1)} %refs_0_.1, bf16[512,512]{1,0:T(8,128)(2,1)} %refs_1_.1, f32[16,128]{1,0:T(8,128)} %maximum_maximum_fusion.refs_2_, ...), custom_call_target="tpu_custom_call" | custom-call | tf_op jit(solution)/shard_map/layer/pallas_call | solution.py:690
  125.9 0.8 fusion.4
  126.6 0.0 copy-done.13
  126.6 0.0 copy-done.14
  126.6 0.0 copy-done.15
  126.7 0.0 copy-done.16
  126.7 0.6 multiply_add_fusion.2
  127.3 0.0 copy-done
  127.3 0.0 copy-done.1
  127.3 1.4 %copy-done.2 = f32[6,128,512]{2,1,0:T(8,128)S(1)} copy-done((f32[6,128,512]{2,1,0:T(8,128)S(1)}, f32[6,128,512]{2,1,0:T(8,128)}, u32[]{:S(2)}) %copy-start.2) | copy-done | bytes 1572888
  128.7 1.2 copy-done.3
  129.9 1.2 copy-done.4
  131.1 1.1 copy-done.5
  132.3 1.0 copy-done.6
  133.3 1.0 copy-done.7
  134.4 0.0 copy-start.12
  134.4 3.5 %update.1 = (bf16[512,512]{1,0:T(8,128)(2,1)}, f32[512,512]{1,0:T(8,128)}, f32[4,512,128]{2,1,0:T(8,128)}, f32[2,128,512]{2,1,0:T(8,128)}, f32[4,512,128]{2,1,0:...) custom-call(bf16[512,512]{1,0:T(8,128)(2,1)S(1)} %copy-done.7, ...), custom_call_target="tpu_custom_call" | custom-call | tf_op jit(solution)/shard_map/update/pallas_call | solution.py:750
  137.9 0.0 copy-done.8
  137.9 0.0 copy-done.9
  137.9 0.0 copy-done.10
  137.9 0.0 copy-done.11
  138.0 0.0 copy-done.12
  138.0 0.6 multiply_add_fusion
  (12 shorter events, 0.0 us)
Async XLA Ops:
  2.9 123.8 %copy-start.13 = (f32[3,128]{1,0:T(4,128)S(1)}, f32[3,128]{1,0:T(4,128)}, u32[]{:S(2)}) copy-start(f32[3,128]{1,0:T(4,128)} %refs_8_.1) | copy-start | bytes 4612
  2.9 123.8 %copy-start.14 = (f32[3,128]{1,0:T(4,128)S(1)}, f32[3,128]{1,0:T(4,128)}, u32[]{:S(2)}) copy-start(f32[3,128]{1,0:T(4,128)} %param.37) | copy-start | bytes 4612
  2.9 123.8 %copy-start.15 = (f32[3,128]{1,0:T(4,128)S(1)}, f32[3,128]{1,0:T(4,128)}, u32[]{:S(2)}) copy-start(f32[3,128]{1,0:T(4,128)} %param.36) | copy-start | bytes 4612
  2.9 123.8 %copy-start.16 = (f32[3,128]{1,0:T(4,128)S(1)}, f32[3,128]{1,0:T(4,128)}, u32[]{:S(2)}) copy-start(f32[3,128]{1,0:T(4,128)} %param.35) | copy-start | bytes 4612
  2.9 124.4 %copy-start = (f32[4,512,128]{2,1,0:T(8,128)S(1)}, f32[4,512,128]{2,1,0:T(8,128)}, u32[]{:S(2)}) copy-start(f32[4,512,128]{2,1,0:T(8,128)} %in_w.1) | copy-start | bytes 3145732
  2.9 124.4 %copy-start.1 = (f32[2,128,512]{2,1,0:T(8,128)S(1)}, f32[2,128,512]{2,1,0:T(8,128)}, u32[]{:S(2)}) copy-start(f32[2,128,512]{2,1,0:T(8,128)} %out_w.1) | copy-start | bytes 1572868
  127.3 1.4 %copy-start.2 = (f32[6,128,512]{2,1,0:T(8,128)S(1)}, f32[6,128,512]{2,1,0:T(8,128)}, u32[]{:S(2)}) copy-start(f32[6,128,512]{2,1,0:T(8,128)} %get-tuple-element.37.orth) | copy-start | bytes 4718596
  128.7 1.2 copy-start.3
  129.9 1.2 copy-start.4
  131.1 1.1 copy-start.5
  132.3 1.0 copy-start.6
  133.3 1.0 copy-start.7
  134.4 3.6 %copy-start.8 = (f32[6,512]{1,0:T(8,128)S(1)}, f32[6,512]{1,0:T(8,128)}, u32[]{:S(2)}) copy-start(f32[6,512]{1,0:T(8,128)} %refs_7_.1) | copy-start | bytes 36868
  134.4 3.6 %copy-start.9 = (f32[8,512]{1,0:T(8,128)S(1)}, f32[8,512]{1,0:T(8,128)}, u32[]{:S(2)}) copy-start(f32[8,512]{1,0:T(8,128)} %get-tuple-element.48) | copy-start | bytes 49156
  134.4 3.6 %copy-start.10 = (f32[6,512]{1,0:T(8,128)S(1)}, f32[6,512]{1,0:T(8,128)}, u32[]{:S(2)}) copy-start(f32[6,512]{1,0:T(8,128)} %param.33) | copy-start | bytes 36868
  134.4 3.6 %copy-start.11 = (f32[6,512]{1,0:T(8,128)S(1)}, f32[6,512]{1,0:T(8,128)}, u32[]{:S(2)}) copy-start(f32[6,512]{1,0:T(8,128)} %param.32) | copy-start | bytes 36868
  134.4 3.6 %copy-start.12 = (f32[6,512]{1,0:T(8,128)S(1)}, f32[6,512]{1,0:T(8,128)}, u32[]{:S(2)}) copy-start(f32[6,512]{1,0:T(8,128)} %param.31) | copy-start | bytes 36868

commit v2 on v1

--- a/solution.py
+++ b/solution.py
@@ -17,6 +17,8 @@
 TB = LEN // NAR
 CW = D // NAR
 OWN = 8
+LINE = OWN // 2
+HR = CW // 2
 PR = CW // OWN
 MID = 256
 
@@ -45,17 +47,17 @@
 
 def layer_kernel(wide, *refs):
     (
-        tok_h, cot_h, pay_i, win_h, wout_h, min_h, mout_h, shared, split,
+        tok_h, cot_h, seg_i, pad_i, gen_i, win_h, wout_h, min_h, mout_h, shared, split,
         otok_h, ograd_h, omom_h, oorth_h, ovec, ovec2,
         tok, cot, pay, win_f, wout_f, mT, wqkvT, wqkv, wup, wod, bcol,
         qp, kTp, vTp, qT, rdn, s_ref, e_ref, ctxn, ctx_s, ctxf,
-        hr, act, du, dr2r, dr1r, dr1, dcst, dcr, vecs, vecw, dkT, dvT, gT,
-        gst, gr1, gs2, gr2, est, erx, lst, lrx, lv, mom, grp,
-        dxs, dxr1, dxs2, dxr2,
+        hr, act, du, dr2r, dr1r, dcst, dcr, vecs, vecw, dkT, dvT, gT,
+        gst, gr1, es1, er1, zse, zre, yf, ybs, ybr, lr1, zs, zr, lv, mom, grp, grl,
+        dxr1, dxr2,
         loc_sem, ag_s, ag_r, rly_s, rly_r, pay_s, pay_r, wg_s, wg_r, wr_s, wr_r,
-        ctx_sem, ctx_rem, dc_sem, dc_rem, vn_s, vn_r, vw_s, vw_r,
-        g1_s, g1_r, g2_s, g2_r, es_s, es_r, ls_s, ls_r, lv_s, lv_r, gp_s, gp_r,
-        aw_s, aw_r, an_s, an_r, ar_s, ar_r, dx1_s, dx1_r, dx2_s, dx2_r,
+        ctx_sem, ctx_rem, dc_sem, dc_rem, vn_s, vn_r, vw_s, vw_r, lv_s, lv_r,
+        g1_s, g1_r, g2_s, g2_r, g3_s, g3_r, l1_s, l1_r, zs_s, zs_r, gp_s, gp_r,
+        aq_s, aq_r, ap_s, ap_r, an_s, an_r, ar_s, ar_r, ow_s, ow_r, ez_s, ez_r, la_s, la_r, sw_s, sw_r, dx1_s, dx1_r, dx2_s, dx2_r,
     ) = refs
     n = lax.axis_index("narrow")
     w = lax.axis_index("wide")
@@ -93,11 +95,11 @@
         return copy
 
     own = rows(n, TB)
-    xbuf = s_ref.at[:, 0:D]
-    ograd = s_ref.at[:, D:2 * D]
+    ograd = s_ref.at[:, 3 * D:4 * D]
     orth = mT
     rln = rdn
     otok = cot
+    dxs, dxs2 = (act, du), dr2r
 
     l_tok = pltpu.make_async_copy(tok_h, tok.at[own], loc_sem.at[0])
     l_win = pltpu.make_async_copy(win_h, win_f, loc_sem.at[1])
@@ -128,7 +130,15 @@
 
     if groups > 1:
         lax.fori_loop(1, groups, greet_group, 0)
-    pay[n] = pay_i[...]
+    seg = seg_i[...]
+    closed = jnp.logical_or(pad_i[...] != 0, gen_i[...] != 0)
+    pay[n] = jnp.concatenate(
+        [
+            seg.astype(F32), jnp.where(closed, -1, seg).astype(F32),
+            split[2:3, :], jnp.zeros((7, CW), F32),
+        ],
+        axis=0,
+    )
     l_tok.wait()
     pl.semaphore_wait(barrier, 3 + (OWN - 1) + (groups - 1))
 
@@ -357,7 +367,8 @@
         d1f = s1 * (
             en - jnp.mean(en, axis=1, keepdims=True) - x1 * jnp.mean(en * x1, axis=1, keepdims=True)
         )
-        dr1[rr, :] = d1f
+        for k in range(NAR):
+            win_f[k, rr, :] = d1f[:, k * CW:(k + 1) * CW]
         d1 = d1f.astype(BF16)
         dr1r[rr, :] = d1
         dcst[rr, :] = mm_nt(d1, wod[0]).astype(BF16)
@@ -390,77 +401,132 @@
     for k, (left, right) in enumerate(((du, hr), (ctxf, dr1r), (act, dr2r))):
         grad = mm_tn(left[...], right[...]).astype(BF16)
         for t in range(NAR):
-            gst[t, k] = grad[t * CW:(t + 1) * CW]
-    start(ncopy(gst.at[n3], gr1.at[1], g1_s.at[1], g1_r.at[1], n1))
-    start(ncopy(gst.at[n1], gr1.at[0], g1_s.at[0], g1_r.at[0], n1))
-
-    def group_loop(fn, first=1, count=OWN):
+            gst[k, t % 2, t // 2] = grad[t * CW:(t + 1) * CW]
+        start(ncopy(gst.at[k, 1 - b0], gr1.at[k], g1_s.at[k], g1_r.at[k], n1))
+
+    def loop(fn, first, count):
         def go(i, c):
             fn(i)
             return c
 
         lax.fori_loop(first, count, go, 0)
 
+    def group_loop(fn, first=1, count=OWN):
+        loop(fn, first, count)
+
     def member(i):
         return lax.rem(o + i, OWN)
 
-    def scatter(i, src, dst, ssem, rsem):
-        u = member(i)
-        piece = pl.ds(pl.multiple_of(u * PR, PR), PR)
-        return wcopy(src.at[:, piece, :], dst.at[o], ssem.at[i], rsem.at[o], g * OWN + u)
-
-    def scatter_all(*where):
-        group_loop(lambda i: scatter(i, *where).start())
-
-    def scatter_done(*where):
-        group_loop(lambda i: scatter(i, *where).wait_send())
-
-    mine = pl.ds(pl.multiple_of(o * PR, PR), PR)
-    place = pl.ds(pl.multiple_of(n * CW + o * PR, PR), PR)
+    pb = lax.rem(o, 2)
+    qa = o // 2
+    pair = g * OWN + 2 * qa + (1 - pb)
+
+    def line(i):
+        return lax.rem(qa + i, LINE)
+
+    def line_dev(u):
+        return g * OWN + 2 * u + pb
+
+    keep = pl.ds(pl.multiple_of(pb * HR, HR), HR)
+    away = pl.ds(pl.multiple_of((1 - pb) * HR, HR), HR)
+
+    def at_rows(first, size):
+        return pl.ds(pl.multiple_of(b0 * CW + first, PR), size)
+
+    def batch(k):
+        return pl.ds(k, 1)
+
+    def z_copy(k, i):
+        u = line(i)
+        src = zs.at[batch(k), pl.ds(pl.multiple_of(u * PR, PR), PR), :]
+        return wcopy(src, zr.at[qa, batch(k)], zs_s.at[k, i], zs_r.at[k, qa], line_dev(u))
+
+    def z_scatter(k):
+        loop(lambda i: z_copy(k, i).start(), 1, LINE)
 
     def across(k, i):
-        return wcopy(
-            grp.at[k, g], grp.at[k, g], gp_s.at[k, i], gp_r.at[k, g], lax.rem(g + i, groups) * OWN + o
-        )
-
-    def collect(base, src, dst, ssem, rsem):
-        k = 0 if base == 3 else 1
-        dst[o] = src[:, mine, :]
+        ref = grl.at[g, batch(k)]
+        return wcopy(ref, ref, gp_s.at[k, i], gp_r.at[k, g], lax.rem(g + i, groups) * OWN + o)
+
+    def share(k, u, i):
+        ref = mom.at[batch(k), b1, at_rows(pb * HR + u * PR, PR), :]
+        return wcopy(ref, ref, aq_s.at[k, i], aq_r.at[k, u], line_dev(line(i)))
+
+    def z_collect(k):
+        bt = batch(k)
+        zr[qa, bt] = zs[bt, pl.ds(pl.multiple_of(qa * PR, PR), PR), :]
 
         def take(i):
-            v = member(i)
-            wcopy(src.at[:, mine, :], dst.at[v], ssem.at[0], rsem.at[v], g * OWN + v).wait_recv()
-
-        group_loop(take)
-        total = lax.fori_loop(
-            0, OWN, lambda v, t: t + dst[v].astype(F32), jnp.zeros((3, PR, D), F32)
-        )
+            v = line(i)
+            wcopy(zr.at[v, bt], zr.at[v, bt], zs_s.at[k, 0], zs_r.at[k, v], line_dev(v)).wait_recv()
+
+        loop(take, 1, LINE)
+        total = zr[0, bt].astype(F32)
+        for v in range(1, LINE):
+            total = total + zr[v, bt].astype(F32)
         if groups > 1:
-            grp[k, g] = total.astype(BF16)
-            group_loop(lambda i: across(k, i).start(), 1, groups)
+            grl[g, bt] = total.astype(BF16)
+            loop(lambda i: across(k, i).start(), 1, groups)
 
             def meet(i):
                 v = lax.rem(g + i, groups)
-                wcopy(grp.at[k, v], grp.at[k, v], gp_s.at[k, i], gp_r.at[k, v], v * OWN + o).wait_recv()
-
-            group_loop(meet, 1, groups)
+                ref = grl.at[v, bt]
+                wcopy(ref, ref, gp_s.at[k, i], gp_r.at[k, v], v * OWN + o).wait_recv()
+
+            loop(meet, 1, groups)
             total = lax.fori_loop(
-                0, groups, lambda v, t: t + grp[k, v].astype(F32), jnp.zeros((3, PR, D), F32)
+                0, groups, lambda v, t: t + grl[v, bt].astype(F32), jnp.zeros_like(total)
             )
-        total = total + 0.5 * mT[pl.ds(base, 3), mine, :]
-        mom[pl.ds(base, 3), place, :] = total.astype(BF16)
-        group_loop(lambda i: share(base, o, i).start())
-
-    def share(base, u, i):
-        ref = mom.at[pl.ds(base, 3), pl.ds(pl.multiple_of(n * CW + u * PR, PR), PR), :]
-        k = 0 if base == 3 else 1
-        return wcopy(ref, ref, aw_s.at[k, i], aw_r.at[k, u], g * OWN + member(i))
-
-    def share_wait(base):
-        group_loop(lambda i: share(base, member(i), i).wait_recv())
-
-    def share_done(base):
-        group_loop(lambda i: share(base, o, i).wait_send())
+        mine = pl.ds(pl.multiple_of(pb * HR + qa * PR, PR), PR)
+        total = total + 0.5 * mT[bt, mine, :]
+        mom[bt, b1, at_rows(pb * HR + qa * PR, PR), :] = total.astype(BF16)
+        loop(lambda i: share(k, qa, i).start(), 1, LINE)
+
+    def half_copy(k, b):
+        ref = mom.at[batch(k), b1, at_rows(b * HR, HR), :]
+        return wcopy(ref, ref, ap_s.at[k], ap_r.at[k], pair)
+
+    def half_send(k):
+        loop(lambda i: share(k, line(i), i).wait_recv(), 1, LINE)
+        half_copy(k, pb).start()
+
+    def spread(k, x, t, target, sems, semr):
+        ref = quarter(k, t)
+        return ncopy(ref, ref, sems.at[x], semr.at[x], target)
+
+    def quarter(k, t):
+        return mom.at[k, t // 2, pl.ds(pl.multiple_of(lax.rem(t, 2) * CW, CW), CW), :]
+
+    def late_fan(m):
+        half_copy(m, 1 - pb).wait_recv()
+        if m < 2:
+            @pl.when(b0 != m)
+            def _():
+                near_copy(m).start()
+
+            start(far_copy(m))
+        else:
+            start(spread(2, 1, n, n2, an_s, an_r))
+            start(spread(2, 0, n, n1, an_s, an_r))
+
+    def near_copy(m):
+        return ncopy(quarter(m, n), quarter(m, n), la_s.at[m, 0], la_r.at[n], m + 2 * b1)
+
+    def far_copy(m):
+        return ncopy(quarter(m, n), quarter(m, n), la_s.at[m, 1], la_r.at[n], m + 2 * (1 - b1))
+
+    def late_wait():
+        for x in (1, 2, 3):
+            t = rel(x)
+            ncopy(quarter(b0, t), quarter(b0, t), la_s.at[0, 0], la_r.at[t], t).wait_recv()
+
+    def relay(k):
+        spread(k, 1, n2, n2, an_s, an_r).wait_recv()
+        start(spread(k, 0, n2, n1, ar_s, ar_r))
+
+    def gathered(k):
+        spread(k, 0, n1, n1, an_s, an_r).wait_recv()
+        spread(k, 0, n3, n1, ar_s, ar_r).wait_recv()
 
     def vec_copy(buf, ss, rs, i, v):
         return wcopy(buf.at[v], buf.at[v], ss.at[i], rs.at[v], g * OWN + member(i))
@@ -490,14 +556,122 @@
         if groups > 1:
             group_loop(lambda i: vec_across(buf, ss, rs, i, g).wait_send(), 1, groups)
 
-    def spread(m, x, t, target, sems, semr):
-        ref = mom.at[m, pl.ds(pl.multiple_of(t * CW, CW), CW), :]
-        return ncopy(ref, ref, sems.at[m, x], semr.at[m, x], target)
+    def pair_copy(m):
+        return wcopy(es1.at[m], er1.at[m], g2_s.at[m], g2_r.at[m], pair)
+
+    def chip_sum(m, part):
+        return gst[m, b0, :, part, :].astype(F32) + gr1[m, :, part, :].astype(F32)
+
+    def early_pair(m):
+        ncopy(gst.at[m, b0], gr1.at[m], g1_s.at[m], g1_r.at[m], n1).wait_recv()
+        es1[m] = chip_sum(m, away).astype(BF16)
+        start(pair_copy(m))
+
+    def e_line(m, i):
+        u = line(i)
+        src = zse.at[m, :, pl.ds(pl.multiple_of(u * PR, PR), PR), :]
+        return wcopy(src, zre.at[m, qa], ez_s.at[m, i], ez_r.at[m, qa], line_dev(u))
+
+    def early_line(m):
+        pair_copy(m).wait_recv()
+        zse[m] = (chip_sum(m, keep) + er1[m].astype(F32)).astype(BF16)
+        loop(lambda i: e_line(m, i).start(), 1, LINE)
+
+    def e_across(m, i):
+        ref = grp.at[g, m]
+        return wcopy(ref, ref, gp_s.at[3 + m, i], gp_r.at[3 + m, g], lax.rem(g + i, groups) * OWN + o)
+
+    def over_copy(m):
+        return ncopy(ybs.at[m], ybr.at[m], g3_s.at[m], g3_r.at[m], n2)
+
+    def early_over(m):
+        zre[m, qa] = zse[m, :, pl.ds(pl.multiple_of(qa * PR, PR), PR), :]
+
+        def take(i):
+            v = line(i)
+            ref = zre.at[m, v]
+            wcopy(ref, ref, ez_s.at[m, 0], ez_r.at[m, v], line_dev(v)).wait_recv()
+
+        loop(take, 1, LINE)
+        total = zre[m, 0].astype(F32)
+        for v in range(1, LINE):
+            total = total + zre[m, v].astype(F32)
+        if groups > 1:
+            grp[g, m] = total.astype(BF16)
+            loop(lambda i: e_across(m, i).start(), 1, groups)
+
+            def meet(i):
+                v = lax.rem(g + i, groups)
+                ref = grp.at[v, m]
+                wcopy(ref, ref, gp_s.at[3 + m, i], gp_r.at[3 + m, v], v * OWN + o).wait_recv()
+
+            loop(meet, 1, groups)
+            total = lax.fori_loop(
+                0, groups, lambda v, t: t + grp[v, m].astype(F32), jnp.zeros_like(total)
+            )
+        mine = pl.ds(pl.multiple_of(pb * HR + qa * PR, PR), PR)
+        old = 0.5 * mT[3 + m, mine, :]
+        for y in range(2):
+            part = total[y] + jnp.where(b1 == y, old, 0.0)
+            yf[m, y] = part
+            ybs[m, y] = part.astype(BF16)
+        start(over_copy(m))
+
+    def e_share(m, u, i):
+        ref = mom.at[3 + m, :, at_rows(pb * HR + u * PR, PR), :]
+        return wcopy(ref, ref, aq_s.at[3 + m, i], aq_r.at[3 + m, u], line_dev(line(i)))
+
+    def early_back(m):
+        over_copy(m).wait_recv()
+        mom[3 + m, :, at_rows(pb * HR + qa * PR, PR), :] = (yf[m] + ybr[m].astype(F32)).astype(BF16)
+        loop(lambda i: e_share(m, qa, i).start(), 1, LINE)
+
+    def e_half(m, b):
+        ref = mom.at[3 + m, :, at_rows(b * HR, HR), :]
+        return wcopy(ref, ref, ap_s.at[3 + m], ap_r.at[3 + m], pair)
+
+    def early_half(m):
+        loop(lambda i: e_share(m, line(i), i).wait_recv(), 1, LINE)
+        start(e_half(m, pb))
+
+    def e_near(m, c):
+        ref = mom.at[3 + m, :, pl.ds(pl.multiple_of(c * CW, CW), CW), :]
+        return ncopy(ref, ref, ow_s.at[m], ow_r.at[m], n1)
+
+    def early_near(m):
+        e_half(m, 1 - pb).wait_recv()
+        start(e_near(m, b0))
+
+    def early_got(m):
+        e_near(m, 1 - b0).wait_recv()
+
+    def vec_early():
+        for x in (1, 2, 3):
+            arrived(vecs.at[rel(x)], vn_s.at[x], vn_r.at[x], rel(x))
+        vecw[o] = ((vecs[0] + vecs[1]) + vecs[2]) + vecs[3]
+        vec_send(vecw, vw_s, vw_r)
+
+    plan = {
+        0: [(early_pair, 0), (early_pair, 1), (early_pair, 2)],
+        1: [(lambda m: vec_early(), 0)],
+        2: [(early_line, 0)],
+        3: [(early_line, 1)],
+        4: [(early_over, 0)],
+        5: [(early_line, 2), (early_over, 1)],
+        6: [(early_back, 0)],
+        7: [(early_back, 1), (early_over, 2)],
+    }
 
     dkT[...] = jnp.zeros_like(dkT)
     dvT[...] = jnp.zeros_like(dvT)
     lane = lax.broadcasted_iota(jnp.int32, (TB, CW), 1)
     low_lane = lane < HD
+
+    def after(k):
+        held = len(pending)
+        for fn, arg in plan.get(k, ()):
+            fn(arg)
+        del pending[held:]
 
     def backward(i, _):
         t = rel(i)
@@ -532,134 +706,172 @@
             gT[hs, rr] = (mm_nt(kTp[h, hs, :], ds) * 0.125).astype(BF16)
             dkT[hs, :] += mm(qT[hs, rr], ds)
             dvT[hs, :] += mm(dcT[hs, :], e)
-
-        @pl.when(i == 0)
-        def _():
-            for k in (1, 0):
-                ncopy(gst.at[n1], gr1.at[k], g1_s.at[k], g1_r.at[k], n1).wait_recv()
-            gs2[...] = (gst[n2].astype(F32) + gr1[1].astype(F32)).astype(BF16)
-            ncopy(gs2, gr2, g2_s, g2_r, n2).start()
-            for x in (1, 2, 3):
-                arrived(vecs.at[rel(x)], vn_s.at[x], vn_r.at[x], rel(x))
-            vecw[o] = ((vecs[0] + vecs[1]) + vecs[2]) + vecs[3]
-            vec_send(vecw, vw_s, vw_r)
-
-        @pl.when(i == 2)
-        def _():
-            ncopy(gs2, gr2, g2_s, g2_r, n2).wait_recv()
-            est[...] = (gst[n].astype(F32) + gr1[0].astype(F32) + gr2[...].astype(F32)).astype(BF16)
-            scatter_all(est, erx, es_s, es_r)
+            for k in range(NAR):
+                pl.when(i == k)(functools.partial(after, 2 * k + h))
 
         return 0
 
     lax.fori_loop(0, NAR, backward, 0)
-    pending.append(ncopy(gs2, gr2, g2_s, g2_r, n2))
     gT[CW:2 * CW, :] = dkT[...].astype(BF16)
     gT[2 * CW:, :] = dvT[...].astype(BF16)
 
-    gin = mm(gT[...], tok[...]).astype(BF16)
-    for k in range(3):
-        lst[k] = gin[k * CW:(k + 1) * CW]
-    scatter_all(lst, lrx, ls_s, ls_r)
+    def late_pair(m):
+        src = dr1r.at[pl.ds(pl.multiple_of(m * CW + (1 - pb) * HR, HR), HR)]
+        return wcopy(src, lr1.at[m], l1_s.at[m], l1_r.at[m], pair)
+
+    for m in range(3):
+        dr1r[m * CW:(m + 1) * CW, :] = mm(gT[m * CW:(m + 1) * CW, :], tok[...]).astype(BF16)
+        start(late_pair(m))
     one = jnp.ones((8, LEN), BF16)
     lv[o, 0:8, :] = mm_nt(one, gT[0:CW, :])
     lv[o, 8:16, :] = mm_nt(one, gT[2 * CW:, :])
     vec_send(lv, lv_s, lv_r)
-    collect(3, est, erx, es_s, es_r)
-
     def dx(t):
         return mm(wqkv[...], gT[:, rows(t, TB)])
 
-    dxs[1] = dx(n3).astype(BF16)
-    start(ncopy(dxs.at[1], dxr1.at[1], dx1_s.at[1], dx1_r.at[1], n1))
-    dxs[0] = dx(n1).astype(BF16)
-    start(ncopy(dxs.at[0], dxr1.at[0], dx1_s.at[0], dx1_r.at[0], n1))
+    def late_line(m):
+        late_pair(m).wait_recv()
+        kept = dr1r[pl.ds(pl.multiple_of(m * CW + pb * HR, HR), HR), :]
+        zs[m] = (kept.astype(F32) + lr1[m].astype(F32)).astype(BF16)
+        z_scatter(m)
+
+    def newton_begin(m, j):
+        xin = mom[m].reshape(D, D).astype(F32)
+        s_ref[:, j * D:(j + 1) * D] = xin * (1.0 / (jnp.sqrt(jnp.sum(xin * xin)) + 1e-07))
+
+    def newton_step(j):
+        xb = s_ref.at[:, j * D:(j + 1) * D]
+        x = xb[...]
+        xl = x.astype(BF16)
+        a = mm_nt(xl, xl)
+        al = a.astype(BF16)
+        p = (COEF_B * a + COEF_C * mm(al, al)).astype(BF16)
+        xb[...] = COEF_A * x + mm(p, xl)
+
+    def newton_last(j, part):
+        xb = s_ref.at[:, j * D:(j + 1) * D]
+        xl = xb[...].astype(BF16)
+        xo = xb[part, :]
+        a = mm_nt(xo.astype(BF16), xl).astype(BF16)
+        y = mm(a, xl)
+        z = mm_nt(y.astype(BF16), xl).astype(BF16)
+        return COEF_A * xo + COEF_B * y + COEF_C * mm(z, xl)
+
+    def newton(m, j, part):
+        newton_begin(m, j)
+        for _ in range(NS_ITERS - 1):
+            newton_step(j)
+        return newton_last(j, part)
+
+    dxs[1][...] = dx(n3).astype(BF16)
+    start(ncopy(dxs[1], dxr1.at[1], dx1_s.at[1], dx1_r.at[1], n1))
+    dxs[0][...] = dx(n1).astype(BF16)
+    start(ncopy(dxs[0], dxr1.at[0], dx1_s.at[0], dx1_r.at[0], n1))
+    early_back(2)
+    late_line(0)
+    late_line(1)
+    late_line(2)
+    early_half(0)
     over = dx(n2)
-    ncopy(dxs.at[1], dxr1.at[1], dx1_s.at[1], dx1_r.at[1], n1).wait_recv()
+    ncopy(dxs[1], dxr1.at[1], dx1_s.at[1], dx1_r.at[1], n1).wait_recv()
     dxs2[...] = (over + dxr1[1].astype(F32)).astype(BF16)
     start(ncopy(dxs2, dxr2, dx2_s, dx2_r, n2))
-    ograd[...] = dx(n).T + dr1[...]
-
-    share_wait(3)
-
-    def fan(base):
-        for m in range(base, base + 3):
-            start(spread(m, 1, n, n2, an_s, an_r))
-            start(spread(m, 0, n, n1, an_s, an_r))
-
-    def newton(m):
-        xin = mom[m].astype(F32)
-        norm = jnp.sqrt(jnp.sum(xin * xin)) + 1e-07
-        xbuf[...] = xin / norm
-
-        def step(_, c):
-            x = xbuf[...]
-            xl = x.astype(BF16)
-            a = mm_nt(xl, xl)
-            al = a.astype(BF16)
-            p = (COEF_B * a + COEF_C * mm(al, al)).astype(BF16)
-            xbuf[...] = COEF_A * x + mm(p, xl)
-            return c
-
-        lax.fori_loop(0, NS_ITERS, step, 0)
-        orth[m] = xbuf[mycols, :]
-
-    fan(3)
-    collect(0, lst, lrx, ls_s, ls_r)
-    for m in range(3, 6):
-        spread(m, 1, n2, n2, an_s, an_r).wait_recv()
-        start(spread(m, 0, n2, n1, ar_s, ar_r))
-    share_wait(0)
-    fan(0)
-    for m in range(3, 6):
-        spread(m, 0, n1, n1, an_s, an_r).wait_recv()
-        spread(m, 0, n3, n1, ar_s, ar_r).wait_recv()
-
-    def newton_late(m, c):
-        newton(m)
-        return c
-
-    lax.fori_loop(3, 6, newton_late, 0)
-    for m in range(0, 3):
-        spread(m, 1, n2, n2, an_s, an_r).wait_recv()
-        start(spread(m, 0, n2, n1, ar_s, ar_r))
-
-    ncopy(dxs.at[0], dxr1.at[0], dx1_s.at[0], dx1_r.at[0], n1).wait_recv()
+    early_half(1)
+    z_collect(0)
+    early_near(0)
+    early_half(2)
+    z_collect(1)
+    early_near(1)
+    dxo = dx(n).T
+    for k in range(NAR):
+        cols = slice(k * CW, (k + 1) * CW)
+        ograd[:, cols] = dxo[:, cols] + win_f[k]
+    z_collect(2)
+    early_near(2)
+    early_got(0)
+    early_got(1)
+
+    both = pl.ds(pl.multiple_of(b1 * 2 * CW, 2 * CW), 2 * CW)
+
+    def swap(m, k):
+        return ncopy(dkT.at[:, k * D:(k + 1) * D], orth.at[m], sw_s.at[k], sw_r.at[k], n1)
+
+    def give(base, k, res):
+        first, second = res[0:CW], res[CW:]
+        orth[base + b0] = jnp.where(b0 == 0, first, second)
+        dkT[:, k * D:(k + 1) * D] = jnp.where(b0 == 0, second, first)
+        start(swap(base + b0, k))
+
+    newton_begin(3 + b0, 0)
+    half_send(0)
+    newton_step(0)
+    half_send(1)
+    half_send(2)
+    newton_step(0)
+    late_fan(0)
+    late_fan(1)
+    give(3, 1, newton_last(0, both))
+    late_fan(2)
+    early_got(2)
+    newton_begin(5, 1)
+    newton_step(1)
+    newton_step(1)
+    orth[5] = newton_last(1, mycols)
+    relay(2)
+
+    ncopy(dxs[0], dxr1.at[0], dx1_s.at[0], dx1_r.at[0], n1).wait_recv()
     ncopy(dxs2, dxr2, dx2_s, dx2_r, n2).wait_recv()
     ograd[...] = ograd[...] + (dxr1[0].astype(F32) + dxr2[...].astype(F32)).T
     l_ograd = pltpu.make_async_copy(ograd, ograd_h, loc_sem.at[7])
     l_ograd.start()
 
-    for m in range(0, 3):
-        spread(m, 0, n1, n1, an_s, an_r).wait_recv()
-        spread(m, 0, n3, n1, ar_s, ar_r).wait_recv()
-    l_mom = pltpu.make_async_copy(mom.at[:, mycols, :], omom_h, loc_sem.at[8])
+    late_wait()
+    give(0, 0, newton(b0, 0, both))
+    gathered(2)
+    l_mom = pltpu.make_async_copy(
+        mom.at[:, b1, pl.ds(pl.multiple_of(b0 * CW, CW), CW), :], omom_h, loc_sem.at[8]
+    )
     l_mom.start()
-    lax.fori_loop(0, 3, newton_late, 0)
+    orth[2] = newton(2, 1, mycols)
+    swap(4 - b0, 1).wait_recv()
+    swap(1 - b0, 0).wait_recv()
     l_orth = pltpu.make_async_copy(orth, oorth_h, loc_sem.at[9])
     l_orth.start()
 
     ovec[...] = vec_sum(vecw, vw_s, vw_r)
-    ovec2[...] = vec_sum(lv, lv_s, lv_r)
+    late = vec_sum(lv, lv_s, lv_r)
+    ovec2[0:1, :] = late[0:1]
+    ovec2[1:2, :] = late[8:9]
+    ovec2[2:3, :] = ovec[6:7, mycols]
+    ovec2[3:8, :] = jnp.zeros((5, CW), F32)
+
+    for m in range(3):
+        pending.extend((pair_copy(m), over_copy(m)))
+    for m in range(2):
+        @pl.when(b0 != m)
+        def _():
+            near_copy(m).wait_send()
 
     for c in pending:
         c.wait_send()
     vec_done(vecw, vw_s, vw_r)
     vec_done(lv, lv_s, lv_r)
-    if groups > 1:
-        for k in (0, 1):
-            group_loop(lambda i: across(k, i).wait_send(), 1, groups)
-    scatter_done(est, erx, es_s, es_r)
-    scatter_done(lst, lrx, ls_s, ls_r)
-    share_done(3)
-    share_done(0)
+    for k in range(3):
+        half_copy(k, pb).wait_send()
+        loop(lambda i: z_copy(k, i).wait_send(), 1, LINE)
+        loop(lambda i: share(k, qa, i).wait_send(), 1, LINE)
+        loop(lambda i: e_line(k, i).wait_send(), 1, LINE)
+        loop(lambda i: e_share(k, qa, i).wait_send(), 1, LINE)
+        if groups > 1:
+            loop(lambda i: across(k, i).wait_send(), 1, groups)
+            loop(lambda i: e_across(k, i).wait_send(), 1, groups)
     l_otok.wait()
     l_ograd.wait()
     l_mom.wait()
     l_orth.wait()
 
 
-def run_layer(wide, tokens, cotangent, pay, in_w, out_w, in_m, out_m, shared, split):
+def run_layer(wide, tokens, cotangent, seg, pad, gen, in_w, out_w, in_m, out_m, shared, split):
     any_ = pl.BlockSpec(memory_space=pl.ANY)
     vm = pl.BlockSpec(memory_space=pltpu.VMEM)
     V = pltpu.VMEM
@@ -676,16 +888,23 @@
         V((LEN, CW), F32), V((TB, LEN), F32), V((2, LEN, LEN), BF16),
         V((LEN, CW), F32), V((LEN, CW), BF16), V((TB, D), BF16),
         V((TB, D), BF16), V((TB, D), BF16), V((TB, D), BF16), V((TB, D), BF16), V((TB, D), BF16),
-        V((TB, D), F32), V((TB, D), BF16), V((LEN, CW), BF16),
+        V((TB, D), BF16), V((LEN, CW), BF16),
         V((NAR, 8, D), F32), V((vslots, 8, D), F32), V((CW, LEN), F32), V((CW, LEN), F32), V((3 * CW, LEN), BF16),
-        V((NAR, 3, CW, D), BF16), V((2, 3, CW, D), BF16), V((3, CW, D), BF16), V((3, CW, D), BF16),
-        V((3, CW, D), BF16), V((OWN, 3, PR, D), BF16), V((3, CW, D), BF16), V((OWN, 3, PR, D), BF16),
-        V((vslots, 16, CW), F32), V((6, D, D), BF16), V((2, groups if groups > 1 else 1, 3, PR, D), BF16),
-        V((2, D, TB), BF16), V((2, D, TB), BF16), V((D, TB), BF16), V((D, TB), BF16),
+        V((3, 2, 2, CW, D), BF16), V((3, 2, CW, D), BF16), V((3, 2, HR, D), BF16), V((3, 2, HR, D), BF16),
+        V((3, 2, HR, D), BF16), V((3, LINE, 2, PR, D), BF16), V((3, 2, PR, D), F32), V((3, 2, PR, D), BF16),
+        V((3, 2, PR, D), BF16), V((3, HR, D), BF16),
+        V((3, HR, D), BF16), V((LINE, 3, PR, D), BF16), V((vslots, 16, CW), F32), V((6, 2, D // 2, D), BF16),
+        V((groups, 3, 2, PR, D) if groups > 1 else (1, 1, 1, PR, D), BF16),
+        V((groups, 3, PR, D) if groups > 1 else (1, 1, PR, D), BF16),
+        V((2, D, TB), BF16), V((D, TB), BF16),
         dma(10), dma(4), dma(4), dma(2), dma(2), dma(4), dma(4), dma(3, 2), dma(3, 2), dma(1, 2), dma(1, 2),
         dma(4), dma(4), dma(4, TB // MID), dma(4, TB // MID), dma(4), dma(4), dma(vslots), dma(vslots),
-        dma(2), dma(2), one, one, dma(OWN), dma(OWN), dma(OWN), dma(OWN), dma(vslots), dma(vslots),
-        dma(2, groups), dma(2, groups), dma(2, OWN), dma(2, OWN), dma(6, 2), dma(6, 2), dma(6, 2), dma(6, 2), dma(2), dma(2), one, one,
+        dma(vslots), dma(vslots),
+        dma(3), dma(3), dma(3), dma(3), dma(3), dma(3), dma(3), dma(3), dma(3, LINE), dma(3, LINE),
+        dma(6, groups), dma(6, groups),
+        dma(6, LINE), dma(6, LINE), dma(6), dma(6), dma(2), dma(2), dma(2), dma(2),
+        dma(3), dma(3), dma(3, LINE), dma(3, LINE), dma(2, 2), dma(4), dma(2), dma(2),
+        dma(2), dma(2), one, one,
     ]
     return pl.pallas_call(
         functools.partial(layer_kernel, wide),
@@ -695,16 +914,16 @@
             jax.ShapeDtypeStruct((6, CW, D), BF16),
             jax.ShapeDtypeStruct((6, CW, D), F32),
             jax.ShapeDtypeStruct((8, D), F32),
-            jax.ShapeDtypeStruct((16, CW), F32),
+            jax.ShapeDtypeStruct((8, CW), F32),
         ],
-        in_specs=[any_, any_, vm, any_, any_, any_, any_, vm, vm],
+        in_specs=[any_, any_, vm, vm, vm, any_, any_, any_, any_, vm, vm],
         out_specs=[any_, any_, any_, any_, vm, vm],
         scratch_shapes=scratch,
         compiler_params=pltpu.CompilerParams(
             collective_id=0, has_side_effects=True, vmem_limit_bytes=62 * MB
         ),
         name="layer",
-    )(tokens, cotangent, pay, in_w, out_w, in_m, out_m, shared, split)
+    )(tokens, cotangent, seg, pad, gen, in_w, out_w, in_m, out_m, shared, split)
 
 
 def muon_step(weights, orthogonal):
@@ -725,40 +944,102 @@
 
 
 def update_kernel(
-    otok, ograd, mom, orth, in_w, out_w, in_a, out_a,
+    otok, ograd, mom, orth, in_w, out_w, in_a, out_a, vec, vec2,
+    sv, s1, s2, sa, pv, p1, p2, pa,
     tok_o, grad_o, inm_o, outm_o, inw_o, outw_o, inl_o, outl_o, ina_o, outa_o,
+    s1_o, s2_o, sv_o, sa_o, p1_o, p2_o, pv_o, pa_o,
+    mom_b, orth_b, inw_b, outw_b, ina_b, outa_b,
+    inm_v, outm_v, inw_v, outw_v, inl_v, outl_v, ina_v, outa_v, grad_v, tok_v, thru, rsem, wsem,
 ):
-    tok_o[...] = otok[...]
-    grad_o[...] = ograd[...]
-    for k in range(4):
-        inm_o[k] = mom[k].astype(F32).T
-        new = muon_step(in_w[k], orth[k].T)
-        inw_o[k] = new
-        inl_o[k] = new.astype(BF16)
-        ina_o[k] = blend(in_a[k], new)
-    for k in range(2):
-        outm_o[k] = mom[4 + k].astype(F32)
-        new = muon_step(out_w[k], orth[4 + k])
-        outw_o[k] = new
-        outl_o[k] = new.astype(BF16)
-        outa_o[k] = blend(out_a[k], new)
-
-
-def run_update(otok, ograd, mom, orth, in_w, out_w, in_a, out_a):
+    whole = [
+        pltpu.make_async_copy(ograd, grad_v, thru.at[0]),
+        pltpu.make_async_copy(otok, tok_v, thru.at[1]),
+    ]
+    back = [
+        pltpu.make_async_copy(grad_v, grad_o, thru.at[2]),
+        pltpu.make_async_copy(tok_v, tok_o, thru.at[3]),
+    ]
+    reads, writes = [], []
+    for k in range(6):
+        j, inner = (k, True) if k < 4 else (k - 4, False)
+        srcs = (mom.at[k], orth.at[k], (in_w if inner else out_w).at[j], (in_a if inner else out_a).at[j])
+        dsts = (
+            mom_b.at[k], orth_b.at[k], (inw_b if inner else outw_b).at[j], (ina_b if inner else outa_b).at[j],
+        )
+        reads.append([pltpu.make_async_copy(s, d, rsem.at[k, i]) for i, (s, d) in enumerate(zip(srcs, dsts))])
+        bufs = (inm_v, inw_v, inl_v, ina_v) if inner else (outm_v, outw_v, outl_v, outa_v)
+        outs = (inm_o, inw_o, inl_o, ina_o) if inner else (outm_o, outw_o, outl_o, outa_o)
+        writes.append(
+            [pltpu.make_async_copy(s.at[j], d.at[j], wsem.at[k, i]) for i, (s, d) in enumerate(zip(bufs, outs))]
+        )
+    for c in reads[0]:
+        c.start()
+    for c in reads[1]:
+        c.start()
+    for c in whole:
+        c.start()
+    for k in range(2, 6):
+        for c in reads[k]:
+            c.start()
+    s1_o[...], s2_o[...], shared_new = adam_step(sv[...], s1[...], s2[...], vec[0:6, :])
+    sv_o[...] = shared_new
+    sa_o[...] = blend(sa[...], shared_new)
+    p1_o[...], p2_o[...], split_new = adam_step(pv[...], p1[...], p2[...], vec2[0:3, :])
+    pv_o[...] = split_new
+    pa_o[...] = blend(pa[...], split_new)
+    for k in range(6):
+        if k in (1, 2):
+            whole[k - 1].wait()
+            back[k - 1].start()
+        for c in reads[k]:
+            c.wait()
+        if k < 4:
+            inm_v[k] = mom_b[k].astype(F32).T
+            new = muon_step(inw_b[k], orth_b[k].T)
+            inw_v[k] = new
+            inl_v[k] = new.astype(BF16)
+            ina_v[k] = blend(ina_b[k], new)
+        else:
+            j = k - 4
+            outm_v[j] = mom_b[k].astype(F32)
+            new = muon_step(outw_b[j], orth_b[k])
+            outw_v[j] = new
+            outl_v[j] = new.astype(BF16)
+            outa_v[j] = blend(outa_b[j], new)
+        for c in writes[k]:
+            c.start()
+    for c in back:
+        c.wait()
+    for k in range(6):
+        for c in writes[k]:
+            c.wait()
+
+
+def run_update(*args):
     vm = pl.BlockSpec(memory_space=pltpu.VMEM)
+    any_ = pl.BlockSpec(memory_space=pl.ANY)
     S = jax.ShapeDtypeStruct
+    V = pltpu.VMEM
+    inner, outer = (4, D, CW), (2, CW, D)
     return pl.pallas_call(
         update_kernel,
         out_shape=[
-            S((TB, D), BF16), S((TB, D), F32), S((4, D, CW), F32), S((2, CW, D), F32),
-            S((4, D, CW), F32), S((2, CW, D), F32), S((4, D, CW), BF16), S((2, CW, D), BF16),
-            S((4, D, CW), F32), S((2, CW, D), F32),
+            S((TB, D), BF16), S((TB, D), F32), S(inner, F32), S(outer, F32), S(inner, F32), S(outer, F32),
+            S(inner, BF16), S(outer, BF16), S(inner, F32), S(outer, F32),
+        ]
+        + [S((6, D), F32)] * 4
+        + [S((3, CW), F32)] * 4,
+        in_specs=[any_] * 8 + [vm] * 10,
+        out_specs=[any_] * 10 + [vm] * 8,
+        scratch_shapes=[
+            V((6, CW, D), BF16), V((6, CW, D), F32), V(inner, F32), V(outer, F32), V(inner, F32), V(outer, F32),
+            V(inner, F32), V(outer, F32), V(inner, F32), V(outer, F32), V(inner, BF16), V(outer, BF16),
+            V(inner, F32), V(outer, F32), V((TB, D), F32), V((TB, D), BF16),
+            pltpu.SemaphoreType.DMA((4,)), pltpu.SemaphoreType.DMA((6, 4)), pltpu.SemaphoreType.DMA((6, 4)),
         ],
-        in_specs=[vm] * 8,
-        out_specs=[vm] * 10,
-        compiler_params=pltpu.CompilerParams(vmem_limit_bytes=40 * MB),
+        compiler_params=pltpu.CompilerParams(vmem_limit_bytes=60 * MB),
         name="update",
-    )(otok, ograd, mom, orth, in_w, out_w, in_a, out_a)
+    )(*args)
 
 
 def body(
@@ -766,37 +1047,17 @@
     out_momenta, in_average, out_average, shared_values, shared_moment1, shared_moment2,
     shared_average, split_values, split_moment1, split_moment2, split_average,
 ):
-    is_open = (padding == 0) & (generative == 0)
-    pay = jnp.concatenate(
-        [
-            segments.reshape(TB // CW, CW).astype(F32),
-            jnp.where(is_open, segments, -1).reshape(TB // CW, CW).astype(F32),
-            split_values[2:3],
-            jnp.zeros((7, CW), F32),
-        ],
-        axis=0,
-    )
+    flags = [v.reshape(TB // CW, CW) for v in (segments, padding, generative)]
     otok, ograd, mom, orth, vec, vec2 = run_layer(
-        wide, tokens, cotangent, pay, in_weights, out_weights, in_momenta, out_momenta,
+        wide, tokens, cotangent, *flags, in_weights, out_weights, in_momenta, out_momenta,
         shared_values, split_values,
     )
-    (
-        result, grad_tokens, moment_in, moment_out, new_in, new_out, low_in, low_out, avg_in, avg_out,
-    ) = run_update(otok, ograd, mom, orth, in_weights, out_weights, in_average, out_average)
-    place = lax.axis_index("narrow") * CW
-    sum_split = jnp.concatenate(
-        [vec2[0:1], vec2[8:9], lax.dynamic_slice(vec, (6, place), (1, CW))], axis=0
-    )
-    shared_one, shared_two, shared_new = adam_step(
-        shared_values, shared_moment1, shared_moment2, vec[:6]
-    )
-    split_one, split_two, split_new = adam_step(
-        split_values, split_moment1, split_moment2, sum_split
-    )
-    return (
-        result, grad_tokens, moment_in, moment_out, new_in, new_out, low_in, low_out, avg_in, avg_out,
-        shared_one, shared_two, shared_new, blend(shared_average, shared_new),
-        split_one, split_two, split_new, blend(split_average, split_new),
+    return tuple(
+        run_update(
+            otok, ograd, mom, orth, in_weights, out_weights, in_average, out_average, vec, vec2,
+            shared_values, shared_moment1, shared_moment2, shared_average,
+            split_values, split_moment1, split_moment2, split_average,
+        )
     )
 
 

time: 141 us -> 114 us (0.81); the launches traced: 139 us -> 114 us
  Pallas kernels: 126 us -> 113 us
  local copies, waits for them, and re-layouts: 8.65 us -> 0 us
  other arithmetic: 2.69 us -> 0 us
    pallas_call x1, Pallas kernels: 123 us -> 106 us  [run_layer(): pl.pallas_call(functools.partial(layer_kernel, wide), out_shape=[jax.Shap...]
    unnamed x34 -> x0, local copies, waits for them, and re-layouts: 7.12 us -> none
    pallas_call x1, Pallas kernels: 3.53 us -> 7.68 us  [run_update(): pl.pallas_call(update_kernel, out_shape=[S((TB, D), BF16), S((TB, D), F32...]
    slice x2 -> x0, local copies, waits for them, and re-layouts: 1.46 us -> none  [the longest x1 0.77 us: body(): vec2[0:1]]
where the time goes in v2:
time: 114 us
  Pallas kernels  113 us (99%)
    pallas_call x1, Pallas kernels, run_layer(): pl.pallas_call(functools.partial(layer_kernel, wide), out_shape=[jax.Shap...  106 us
    pallas_call x1, Pallas kernels, run_update(): pl.pallas_call(update_kernel, out_shape=[S((TB, D), BF16), S((TB, D), F32...  7.68 us

profile of v2, /device:TPU:0, one launch (start us, length us, event | category | flops | bytes accessed | tf_op | source)
XLA Modules:
  0.0 114.1 jit_solution(16436954893622847214)
XLA Ops:
  0.7 105.6 %layer.1 = (bf16[512,512]{1,0:T(8,128)(2,1)}, f32[512,512]{1,0:T(8,128)}, bf16[6,128,512]{2,1,0:T(8,128)(2,1)}, f32[6,128,512]{2,1,0:T(8,128)}, f32[8,512]{1,0:T(8,128)}, /*index=5*/f32[8,128]{1,0:T(8,128)}) custom-call(bf16[512,512]{1,0:T(8,128)(2,1)} %refs_0_.1, bf16[512,512]{1,0:T(8,128)(2,1)} %refs_1_.1, s32[4,128]{1,0:T(4,128)} %bitcast.3, ...), custom_call_target="tpu_custom_call" | custom-call | tf_op jit(solution)/shard_map/layer/pallas_call | solution.py:909
  106.3 7.7 %update.1 = (bf16[512,512]{1,0:T(8,128)(2,1)}, f32[512,512]{1,0:T(8,128)}, f32[4,512,128]{2,1,0:T(8,128)}, f32[2,128,512]{2,1,0:T(8,128)}, f32[4,512,128]{2,1,0:...) custom-call(bf16[512,512]{1,0:T(8,128)(2,1)} %get-tuple-element.24.o, ...), custom_call_target="tpu_custom_call" | custom-call | tf_op jit(solution)/shard_map/update/pallas_call | solution.py:1024

commit v3 on v2

--- a/solution.py
+++ b/solution.py
@@ -19,6 +19,7 @@
 OWN = 8
 LINE = OWN // 2
 HR = CW // 2
+HC = D // 2
 PR = CW // OWN
 MID = 256
 
@@ -52,12 +53,12 @@
         tok, cot, pay, win_f, wout_f, mT, wqkvT, wqkv, wup, wod, bcol,
         qp, kTp, vTp, qT, rdn, s_ref, e_ref, ctxn, ctx_s, ctxf,
         hr, act, du, dr2r, dr1r, dcst, dcr, vecs, vecw, dkT, dvT, gT,
-        gst, gr1, es1, er1, zse, zre, yf, ybs, ybr, lr1, zs, zr, lv, mom, grp, grl,
+        gst, gr1, eys, eyr, es1, er1, zse, zre, lr1, zs, zr, zd, zdr, lv, mom, grp, grl,
         dxr1, dxr2,
         loc_sem, ag_s, ag_r, rly_s, rly_r, pay_s, pay_r, wg_s, wg_r, wr_s, wr_r,
         ctx_sem, ctx_rem, dc_sem, dc_rem, vn_s, vn_r, vw_s, vw_r, lv_s, lv_r,
-        g1_s, g1_r, g2_s, g2_r, g3_s, g3_r, l1_s, l1_r, zs_s, zs_r, gp_s, gp_r,
-        aq_s, aq_r, ap_s, ap_r, an_s, an_r, ar_s, ar_r, ow_s, ow_r, ez_s, ez_r, la_s, la_r, sw_s, sw_r, dx1_s, dx1_r, dx2_s, dx2_r,
+        g1_s, g1_r, g2_s, g2_r, g3_s, g3_r, l1_s, l1_r, zs_s, zs_r, zd_s, zd_r, ad_s, ad_r, gp_s, gp_r,
+        aq_s, aq_r, ap_s, ap_r, ow_s, ow_r, ez_s, ez_r, ey_s, ey_r, la_s, la_r, sw_s, sw_r, dx1_s, dx1_r, dx2_s, dx2_r,
     ) = refs
     n = lax.axis_index("narrow")
     w = lax.axis_index("wide")
@@ -175,10 +176,6 @@
             ncopy(wod.at[:, cols, :], wod.at[:, cols, :], sems.at[x, 0], semr.at[x, 0], target),
             ncopy(wup.at[:, cols], wup.at[:, cols], sems.at[x, 1], semr.at[x, 1], target),
         ]
-
-    for x in (2, 1):
-        for c in wg_list(wg_s, wg_r, x, n, rel(x)):
-            start(c)
 
     bcol[0] = jnp.broadcast_to(split[0:1, :], (CW, CW)).T
     bcol[1] = jnp.broadcast_to(split[1:2, :], (CW, CW)).T
@@ -248,6 +245,9 @@
             for c in (0, 1):
                 arrived(ag_rows(n2, c), ag_s.at[2 + c], ag_r.at[2 + c], n2)
                 ncopy(ag_rows(n2, c), ag_rows(n2, c), rly_s.at[c], rly_r.at[c], n1).start()
+            for x in (2, 1):
+                for c in wg_list(wg_s, wg_r, x, n, rel(x)):
+                    c.start()
 
         @pl.when(i == 3)
         def _():
@@ -258,6 +258,8 @@
         return 0
 
     lax.fori_loop(0, NAR, project_step, 0)
+    for x in (2, 1):
+        pending.extend(wg_list(wg_s, wg_r, x, n, rel(x)))
     for c in (0, 1):
         pending.append(ncopy(ag_rows(n2, c), ag_rows(n2, c), rly_s.at[c], rly_r.at[c], n1))
 
@@ -298,7 +300,7 @@
             x = lo + 2 * hi
             ctx_copy(x, t).start()
 
-        @pl.when(i == 0)
+        @pl.when(i == 2)
         def _():
             for c in wg_list(wg_s, wg_r, 2, n2, n2):
                 c.wait_recv()
@@ -430,103 +432,148 @@
     keep = pl.ds(pl.multiple_of(pb * HR, HR), HR)
     away = pl.ds(pl.multiple_of((1 - pb) * HR, HR), HR)
 
-    def at_rows(first, size):
-        return pl.ds(pl.multiple_of(b0 * CW + first, PR), size)
-
-    def batch(k):
-        return pl.ds(k, 1)
-
-    def z_copy(k, i):
-        u = line(i)
-        src = zs.at[batch(k), pl.ds(pl.multiple_of(u * PR, PR), PR), :]
-        return wcopy(src, zr.at[qa, batch(k)], zs_s.at[k, i], zs_r.at[k, qa], line_dev(u))
-
-    def z_scatter(k):
-        loop(lambda i: z_copy(k, i).start(), 1, LINE)
-
-    def across(k, i):
-        ref = grl.at[g, batch(k)]
-        return wcopy(ref, ref, gp_s.at[k, i], gp_r.at[k, g], lax.rem(g + i, groups) * OWN + o)
-
-    def share(k, u, i):
-        ref = mom.at[batch(k), b1, at_rows(pb * HR + u * PR, PR), :]
-        return wcopy(ref, ref, aq_s.at[k, i], aq_r.at[k, u], line_dev(line(i)))
-
-    def z_collect(k):
-        bt = batch(k)
-        zr[qa, bt] = zs[bt, pl.ds(pl.multiple_of(qa * PR, PR), PR), :]
+    keepc = pl.ds(pl.multiple_of(pb * HC, HC), HC)
+    awayc = pl.ds(pl.multiple_of((1 - pb) * HC, HC), HC)
+
+    def piece(v):
+        return pl.ds(pl.multiple_of(v * PR, PR), PR)
+
+    def unit_rows(u):
+        return pl.ds(u * CW, CW)
+
+    def unit_mom(u, part, cols):
+        if u == 0:
+            return mom.at[2, b1, b0, :, part, cols]
+        return mom.at[pl.ds(0, 2), b1, b0, u - 1, part, cols]
+
+    def l1_copy(u):
+        return wcopy(dr1r.at[unit_rows(u), awayc], lr1.at[u], l1_s.at[u], l1_r.at[u], pair)
+
+    def l1(u, lhs):
+        dr1r[unit_rows(u), :] = mm(lhs, tok[...]).astype(BF16)
+        start(l1_copy(u))
+
+    def z_copy(u, i):
+        v = line(i)
+        return wcopy(zs.at[u, :, piece(v), :], zr.at[u, qa], zs_s.at[u, i], zs_r.at[u, qa], line_dev(v))
+
+    def owned(u, total):
+        if groups > 1:
+            grl[g, u] = total.astype(BF16)
+            loop(lambda i: across(u, i).start(), 1, groups)
+
+            def meet(i):
+                v = lax.rem(g + i, groups)
+                ref = grl.at[v, u]
+                wcopy(ref, ref, gp_s.at[u, i], gp_r.at[u, v], v * OWN + o).wait_recv()
+
+            loop(meet, 1, groups)
+            total = lax.fori_loop(
+                0, groups, lambda v, t: t + grl[v, u].astype(F32), jnp.zeros_like(total)
+            )
+        for k in range(2):
+            m, first = (2, k * HR) if u == 0 else (k, (u - 1) * HR)
+            old = mT[m, pl.ds(pl.multiple_of(first + qa * PR, PR), PR), keepc]
+            new = (total[k] + 0.5 * old).astype(BF16)
+            if u == 0:
+                mom[2, b1, b0, k, piece(qa), keepc] = new
+            else:
+                mom[k, b1, b0, u - 1, piece(qa), keepc] = new
+
+    def half_cols(b):
+        return pl.ds(pl.multiple_of(b * HC, HC), HC)
+
+    def d1_copy(i):
+        v = member(i)
+        src = zd.at[:, piece(v // 2), half_cols(lax.rem(v, 2))]
+        return wcopy(src, zdr.at[o], zd_s.at[i], zd_r.at[o], g * OWN + v)
+
+    def d1(lhs):
+        zd[...] = mm(lhs, tok[...]).astype(BF16).reshape(2, HR, D)
+        group_loop(lambda i: d1_copy(i).start())
+
+    def d2_copy(v, i):
+        ref = unit_mom(2, piece(v // 2), half_cols(lax.rem(v, 2)))
+        return wcopy(ref, ref, ad_s.at[i], ad_r.at[v], g * OWN + member(i))
+
+    def d2():
+        zdr[o] = zd[:, piece(qa), keepc]
+
+        def take(i):
+            v = member(i)
+            wcopy(zdr.at[v], zdr.at[v], zd_s.at[0], zd_r.at[v], g * OWN + v).wait_recv()
+
+        group_loop(take)
+        total = zdr[0].astype(F32)
+        for v in range(1, OWN):
+            total = total + zdr[v].astype(F32)
+        owned(2, total)
+        group_loop(lambda i: d2_copy(o, i).start())
+
+    def l2(u):
+        l1_copy(u).wait_recv()
+        both = dr1r[unit_rows(u), keepc].astype(F32) + lr1[u].astype(F32)
+        zs[u] = both.astype(BF16).reshape(2, HR, HC)
+        loop(lambda i: z_copy(u, i).start(), 1, LINE)
+
+    def across(u, i):
+        ref = grl.at[g, u]
+        return wcopy(ref, ref, gp_s.at[u, i], gp_r.at[u, g], lax.rem(g + i, groups) * OWN + o)
+
+    def share(u, v, i):
+        ref = unit_mom(u, piece(v), keepc)
+        return wcopy(ref, ref, aq_s.at[u, i], aq_r.at[u, v], line_dev(line(i)))
+
+    def l3(u):
+        zr[u, qa] = zs[u, :, piece(qa), :]
 
         def take(i):
             v = line(i)
-            wcopy(zr.at[v, bt], zr.at[v, bt], zs_s.at[k, 0], zs_r.at[k, v], line_dev(v)).wait_recv()
+            wcopy(zr.at[u, v], zr.at[u, v], zs_s.at[u, 0], zs_r.at[u, v], line_dev(v)).wait_recv()
 
         loop(take, 1, LINE)
-        total = zr[0, bt].astype(F32)
+        total = zr[u, 0].astype(F32)
         for v in range(1, LINE):
-            total = total + zr[v, bt].astype(F32)
-        if groups > 1:
-            grl[g, bt] = total.astype(BF16)
-            loop(lambda i: across(k, i).start(), 1, groups)
-
-            def meet(i):
-                v = lax.rem(g + i, groups)
-                ref = grl.at[v, bt]
-                wcopy(ref, ref, gp_s.at[k, i], gp_r.at[k, v], v * OWN + o).wait_recv()
-
-            loop(meet, 1, groups)
-            total = lax.fori_loop(
-                0, groups, lambda v, t: t + grl[v, bt].astype(F32), jnp.zeros_like(total)
-            )
-        mine = pl.ds(pl.multiple_of(pb * HR + qa * PR, PR), PR)
-        total = total + 0.5 * mT[bt, mine, :]
-        mom[bt, b1, at_rows(pb * HR + qa * PR, PR), :] = total.astype(BF16)
-        loop(lambda i: share(k, qa, i).start(), 1, LINE)
-
-    def half_copy(k, b):
-        ref = mom.at[batch(k), b1, at_rows(b * HR, HR), :]
-        return wcopy(ref, ref, ap_s.at[k], ap_r.at[k], pair)
-
-    def half_send(k):
-        loop(lambda i: share(k, line(i), i).wait_recv(), 1, LINE)
-        half_copy(k, pb).start()
-
-    def spread(k, x, t, target, sems, semr):
-        ref = quarter(k, t)
-        return ncopy(ref, ref, sems.at[x], semr.at[x], target)
-
-    def quarter(k, t):
-        return mom.at[k, t // 2, pl.ds(pl.multiple_of(lax.rem(t, 2) * CW, CW), CW), :]
-
-    def late_fan(m):
-        half_copy(m, 1 - pb).wait_recv()
-        if m < 2:
-            @pl.when(b0 != m)
+            total = total + zr[u, v].astype(F32)
+        owned(u, total)
+        loop(lambda i: share(u, qa, i).start(), 1, LINE)
+
+    def half_copy(u, cols):
+        ref = unit_mom(u, pl.ds(0, HR), cols)
+        return wcopy(ref, ref, ap_s.at[u], ap_r.at[u], pair)
+
+    def l4(u):
+        loop(lambda i: share(u, line(i), i).wait_recv(), 1, LINE)
+        half_copy(u, keepc).start()
+
+    fans = {0: [(0, 2, 1)], 1: [(1, 0, 0), (2, 1, 1)], 2: [(3, 0, 0), (4, 1, 1)]}
+
+    def fan_ref(u, m, t):
+        low = lax.rem(t, 2)
+        return mom.at[2, t // 2, low] if u == 0 else mom.at[m, t // 2, low, u - 1]
+
+    def near_copy(u, f, m, c):
+        return ncopy(fan_ref(u, m, n), fan_ref(u, m, n), la_s.at[f, 0], la_r.at[f, n], c + 2 * b1)
+
+    def far_copy(u, f, m, c):
+        return ncopy(fan_ref(u, m, n), fan_ref(u, m, n), la_s.at[f, 1], la_r.at[f, n], c + 2 * (1 - b1))
+
+    def l5(u):
+        if u < 2:
+            half_copy(u, awayc).wait_recv()
+        else:
+            group_loop(lambda i: d2_copy(member(i), i).wait_recv())
+        for f, m, c in fans[u]:
+            far_copy(u, f, m, c).start()
+
+            @pl.when(b0 != c)
             def _():
-                near_copy(m).start()
-
-            start(far_copy(m))
-        else:
-            start(spread(2, 1, n, n2, an_s, an_r))
-            start(spread(2, 0, n, n1, an_s, an_r))
-
-    def near_copy(m):
-        return ncopy(quarter(m, n), quarter(m, n), la_s.at[m, 0], la_r.at[n], m + 2 * b1)
-
-    def far_copy(m):
-        return ncopy(quarter(m, n), quarter(m, n), la_s.at[m, 1], la_r.at[n], m + 2 * (1 - b1))
-
-    def late_wait():
+                near_copy(u, f, m, c).start()
+
+    def fan_wait(u, f, m):
         for x in (1, 2, 3):
             t = rel(x)
-            ncopy(quarter(b0, t), quarter(b0, t), la_s.at[0, 0], la_r.at[t], t).wait_recv()
-
-    def relay(k):
-        spread(k, 1, n2, n2, an_s, an_r).wait_recv()
-        start(spread(k, 0, n2, n1, ar_s, ar_r))
-
-    def gathered(k):
-        spread(k, 0, n1, n1, an_s, an_r).wait_recv()
-        spread(k, 0, n3, n1, ar_s, ar_r).wait_recv()
+            ncopy(fan_ref(u, m, t), fan_ref(u, m, t), la_s.at[0, 0], la_r.at[f, t], t).wait_recv()
 
     def vec_copy(buf, ss, rs, i, v):
         return wcopy(buf.at[v], buf.at[v], ss.at[i], rs.at[v], g * OWN + member(i))
@@ -556,36 +603,45 @@
         if groups > 1:
             group_loop(lambda i: vec_across(buf, ss, rs, i, g).wait_send(), 1, groups)
 
+    def over_copy(m):
+        return ncopy(eys.at[m], eyr.at[m], g3_s.at[m], g3_r.at[m], n2)
+
+    def chip_sum(m, y, part):
+        return gst[m, b0, y, part, :].astype(F32) + gr1[m, y, part, :].astype(F32)
+
+    def early_over(m):
+        ncopy(gst.at[m, b0], gr1.at[m], g1_s.at[m], g1_r.at[m], n1).wait_recv()
+        eys[m] = chip_sum(m, 1 - b1, slice(None)).astype(BF16)
+        start(over_copy(m))
+
     def pair_copy(m):
         return wcopy(es1.at[m], er1.at[m], g2_s.at[m], g2_r.at[m], pair)
 
-    def chip_sum(m, part):
-        return gst[m, b0, :, part, :].astype(F32) + gr1[m, :, part, :].astype(F32)
-
     def early_pair(m):
-        ncopy(gst.at[m, b0], gr1.at[m], g1_s.at[m], g1_r.at[m], n1).wait_recv()
-        es1[m] = chip_sum(m, away).astype(BF16)
+        over_copy(m).wait_recv()
+        es1[m] = (chip_sum(m, b1, away) + eyr[m, away, :].astype(F32)).astype(BF16)
         start(pair_copy(m))
 
     def e_line(m, i):
         u = line(i)
-        src = zse.at[m, :, pl.ds(pl.multiple_of(u * PR, PR), PR), :]
-        return wcopy(src, zre.at[m, qa], ez_s.at[m, i], ez_r.at[m, qa], line_dev(u))
+        return wcopy(zse.at[m, piece(u), :], zre.at[m, qa], ez_s.at[m, i], ez_r.at[m, qa], line_dev(u))
 
     def early_line(m):
         pair_copy(m).wait_recv()
-        zse[m] = (chip_sum(m, keep) + er1[m].astype(F32)).astype(BF16)
+        total = chip_sum(m, b1, keep) + eyr[m, keep, :].astype(F32) + er1[m].astype(F32)
+        zse[m] = total.astype(BF16)
         loop(lambda i: e_line(m, i).start(), 1, LINE)
 
     def e_across(m, i):
         ref = grp.at[g, m]
         return wcopy(ref, ref, gp_s.at[3 + m, i], gp_r.at[3 + m, g], lax.rem(g + i, groups) * OWN + o)
 
-    def over_copy(m):
-        return ncopy(ybs.at[m], ybr.at[m], g3_s.at[m], g3_r.at[m], n2)
-
-    def early_over(m):
-        zre[m, qa] = zse[m, :, pl.ds(pl.multiple_of(qa * PR, PR), PR), :]
+    def e_swap(m, y):
+        ref = mom.at[3 + m, y, b0, pb, piece(qa), :]
+        return ncopy(ref, ref, ey_s.at[m], ey_r.at[m], n2)
+
+    def early_sum(m):
+        zre[m, qa] = zse[m, piece(qa), :]
 
         def take(i):
             v = line(i)
@@ -609,25 +665,20 @@
             total = lax.fori_loop(
                 0, groups, lambda v, t: t + grp[v, m].astype(F32), jnp.zeros_like(total)
             )
-        mine = pl.ds(pl.multiple_of(pb * HR + qa * PR, PR), PR)
-        old = 0.5 * mT[3 + m, mine, :]
-        for y in range(2):
-            part = total[y] + jnp.where(b1 == y, old, 0.0)
-            yf[m, y] = part
-            ybs[m, y] = part.astype(BF16)
-        start(over_copy(m))
+        old = mT[3 + m, pl.ds(pl.multiple_of(pb * HR + qa * PR, PR), PR), :]
+        mom[3 + m, b1, b0, pb, piece(qa), :] = (total + 0.5 * old).astype(BF16)
+        start(e_swap(m, b1))
 
     def e_share(m, u, i):
-        ref = mom.at[3 + m, :, at_rows(pb * HR + u * PR, PR), :]
+        ref = mom.at[3 + m, :, b0, pb, piece(u), :]
         return wcopy(ref, ref, aq_s.at[3 + m, i], aq_r.at[3 + m, u], line_dev(line(i)))
 
     def early_back(m):
-        over_copy(m).wait_recv()
-        mom[3 + m, :, at_rows(pb * HR + qa * PR, PR), :] = (yf[m] + ybr[m].astype(F32)).astype(BF16)
+        e_swap(m, 1 - b1).wait_recv()
         loop(lambda i: e_share(m, qa, i).start(), 1, LINE)
 
     def e_half(m, b):
-        ref = mom.at[3 + m, :, at_rows(b * HR, HR), :]
+        ref = mom.at[3 + m, :, b0, b]
         return wcopy(ref, ref, ap_s.at[3 + m], ap_r.at[3 + m], pair)
 
     def early_half(m):
@@ -635,15 +686,15 @@
         start(e_half(m, pb))
 
     def e_near(m, c):
-        ref = mom.at[3 + m, :, pl.ds(pl.multiple_of(c * CW, CW), CW), :]
+        ref = mom.at[3 + m, :, c]
         return ncopy(ref, ref, ow_s.at[m], ow_r.at[m], n1)
 
     def early_near(m):
         e_half(m, 1 - pb).wait_recv()
-        start(e_near(m, b0))
-
-    def early_got(m):
-        e_near(m, 1 - b0).wait_recv()
+
+        @pl.when(b0 != m % 2)
+        def _():
+            e_near(m, b0).start()
 
     def vec_early():
         for x in (1, 2, 3):
@@ -652,28 +703,41 @@
         vec_send(vecw, vw_s, vw_r)
 
     plan = {
-        0: [(early_pair, 0), (early_pair, 1), (early_pair, 2)],
-        1: [(lambda m: vec_early(), 0)],
-        2: [(early_line, 0)],
-        3: [(early_line, 1)],
-        4: [(early_over, 0)],
-        5: [(early_line, 2), (early_over, 1)],
-        6: [(early_back, 0)],
-        7: [(early_back, 1), (early_over, 2)],
+        ("a", 0): [(early_over, 0)],
+        ("a", 1): [(early_over, 1)],
+        ("a", 2): [(early_over, 2)],
+        ("a", 3): [(lambda m: vec_early(), 0)],
+        (0, 1, 0): [(early_pair, 0)],
+        (0, 1, 1): [(l2, 0)],
+        (0, 2, 0): [(early_pair, 1)],
+        (0, 3, 0): [(early_pair, 2), (early_line, 0)],
+        (0, 3, 1): [(l3, 0)],
+        (1, 0, 0): [(early_line, 1)],
+        (1, 1, 0): [(early_line, 2), (early_sum, 0)],
+        (1, 1, 1): [(l4, 0), (l2, 1)],
+        (1, 2, 0): [(early_sum, 1)],
+        (1, 2, 1): [(early_back, 0)],
+        (1, 3, 0): [(early_sum, 2), (l5, 0)],
+        (1, 3, 1): [(l3, 1)],
     }
+
+    def after(i, key):
+        for k in range(NAR):
+            point = (key[0], k) + key[1:]
+            if point in plan:
+                @pl.when(i == k)
+                def _():
+                    held = len(pending)
+                    for fn, arg in plan[point]:
+                        fn(arg)
+                    del pending[held:]
 
     dkT[...] = jnp.zeros_like(dkT)
     dvT[...] = jnp.zeros_like(dvT)
     lane = lax.broadcasted_iota(jnp.int32, (TB, CW), 1)
     low_lane = lane < HD
 
-    def after(k):
-        held = len(pending)
-        for fn, arg in plan.get(k, ()):
-            fn(arg)
-        del pending[held:]
-
-    def backward(i, _):
+    def backward_v(i, _):
         t = rel(i)
         rr = rows(t, TB)
 
@@ -699,141 +763,143 @@
             tail = delta[h] - top
             base = (1 - h) * HD
             extra = jnp.where(lane == base, -top, jnp.where(lane == base + 1, -tail, 0.0))
-            left = jnp.where(low_lane == (h == 0), full, extra).astype(BF16)
-            s_ref[...] = mm(left, vTp[h])
-            e = e_ref[h, rr, :]
-            ds = e * s_ref[...].astype(BF16)
+            qp[h, rr, 0:CW] = jnp.where(low_lane == (h == 0), full, extra).astype(BF16)
+            dvT[hs, :] += mm(dcT[hs, :], e_ref[h, rr, :])
+        after(i, ("a",))
+        return 0
+
+    lax.fori_loop(0, NAR, backward_v, 0)
+    gT[2 * CW:, :] = dvT[...].astype(BF16)
+    l1(0, gT[2 * CW:, :])
+
+    def backward(h):
+        hs = slice(h * HD, (h + 1) * HD)
+        ks = slice(CW + h * HD, CW + (h + 1) * HD)
+
+        def block(i, _):
+            rr = rows(rel(i), TB)
+            s_ref[...] = mm(qp[h, rr, 0:CW], vTp[h])
+            ds = e_ref[h, rr, :] * s_ref[...].astype(BF16)
             gT[hs, rr] = (mm_nt(kTp[h, hs, :], ds) * 0.125).astype(BF16)
+            after(i, (h, 0))
             dkT[hs, :] += mm(qT[hs, rr], ds)
-            dvT[hs, :] += mm(dcT[hs, :], e)
-            for k in range(NAR):
-                pl.when(i == k)(functools.partial(after, 2 * k + h))
-
-        return 0
-
-    lax.fori_loop(0, NAR, backward, 0)
-    gT[CW:2 * CW, :] = dkT[...].astype(BF16)
-    gT[2 * CW:, :] = dvT[...].astype(BF16)
-
-    def late_pair(m):
-        src = dr1r.at[pl.ds(pl.multiple_of(m * CW + (1 - pb) * HR, HR), HR)]
-        return wcopy(src, lr1.at[m], l1_s.at[m], l1_r.at[m], pair)
-
-    for m in range(3):
-        dr1r[m * CW:(m + 1) * CW, :] = mm(gT[m * CW:(m + 1) * CW, :], tok[...]).astype(BF16)
-        start(late_pair(m))
-    one = jnp.ones((8, LEN), BF16)
-    lv[o, 0:8, :] = mm_nt(one, gT[0:CW, :])
-    lv[o, 8:16, :] = mm_nt(one, gT[2 * CW:, :])
-    vec_send(lv, lv_s, lv_r)
+            after(i, (h, 1))
+            return 0
+
+        lax.fori_loop(0, NAR, block, 0)
+        gT[ks, :] = dkT[hs, :].astype(BF16)
+        lhs = jnp.concatenate([gT[hs, :], gT[ks, :]], axis=0)
+        if h == 0:
+            l1(1, lhs)
+        else:
+            d1(lhs)
+
+    backward(0)
+    backward(1)
+
     def dx(t):
         return mm(wqkv[...], gT[:, rows(t, TB)])
 
-    def late_line(m):
-        late_pair(m).wait_recv()
-        kept = dr1r[pl.ds(pl.multiple_of(m * CW + pb * HR, HR), HR), :]
-        zs[m] = (kept.astype(F32) + lr1[m].astype(F32)).astype(BF16)
-        z_scatter(m)
-
-    def newton_begin(m, j):
+    both_rows = pl.ds(pl.multiple_of(b1 * 2 * CW, 2 * CW), 2 * CW)
+    XB = s_ref.at[:, 0:D]
+
+    def newton_begin(m):
         xin = mom[m].reshape(D, D).astype(F32)
-        s_ref[:, j * D:(j + 1) * D] = xin * (1.0 / (jnp.sqrt(jnp.sum(xin * xin)) + 1e-07))
-
-    def newton_step(j):
-        xb = s_ref.at[:, j * D:(j + 1) * D]
-        x = xb[...]
+        XB[...] = xin * (1.0 / (jnp.sqrt(jnp.sum(xin * xin)) + 1e-07))
+
+    def newton_step():
+        x = XB[...]
         xl = x.astype(BF16)
         a = mm_nt(xl, xl)
         al = a.astype(BF16)
         p = (COEF_B * a + COEF_C * mm(al, al)).astype(BF16)
-        xb[...] = COEF_A * x + mm(p, xl)
-
-    def newton_last(j, part):
-        xb = s_ref.at[:, j * D:(j + 1) * D]
-        xl = xb[...].astype(BF16)
-        xo = xb[part, :]
+        XB[...] = COEF_A * x + mm(p, xl)
+
+    def swap(m, k):
+        return ncopy(dkT.at[:, k * D:(k + 1) * D], orth.at[m], sw_s.at[k], sw_r.at[k], n1)
+
+    def newton_last(m, k):
+        xl = XB[...].astype(BF16)
+        xo = XB[both_rows, :]
         a = mm_nt(xo.astype(BF16), xl).astype(BF16)
         y = mm(a, xl)
         z = mm_nt(y.astype(BF16), xl).astype(BF16)
-        return COEF_A * xo + COEF_B * y + COEF_C * mm(z, xl)
-
-    def newton(m, j, part):
-        newton_begin(m, j)
-        for _ in range(NS_ITERS - 1):
-            newton_step(j)
-        return newton_last(j, part)
+        res = COEF_A * xo + COEF_B * y + COEF_C * mm(z, xl)
+        first, second = res[0:CW], res[CW:]
+        orth[m] = jnp.where(b0 == 0, first, second)
+        dkT[:, k * D:(k + 1) * D] = jnp.where(b0 == 0, second, first)
+        start(swap(m, k))
+
+    def dx2_copy(c):
+        cols = slice(c * MID, (c + 1) * MID)
+        return ncopy(dxs2.at[:, cols], dxr2.at[:, cols], dx2_s.at[c], dx2_r.at[c], n2)
 
     dxs[1][...] = dx(n3).astype(BF16)
     start(ncopy(dxs[1], dxr1.at[1], dx1_s.at[1], dx1_r.at[1], n1))
     dxs[0][...] = dx(n1).astype(BF16)
     start(ncopy(dxs[0], dxr1.at[0], dx1_s.at[0], dx1_r.at[0], n1))
-    early_back(2)
-    late_line(0)
-    late_line(1)
-    late_line(2)
+    early_back(1)
+    over = dx(n2)
     early_half(0)
-    over = dx(n2)
+    one = jnp.ones((8, LEN), BF16)
+    upper_rows = lax.broadcasted_iota(jnp.int32, (8, CW), 0) < 4
+    lv[o] = jnp.where(upper_rows, mm_nt(one, gT[0:CW, :]), mm_nt(one, gT[2 * CW:, :]))
     ncopy(dxs[1], dxr1.at[1], dx1_s.at[1], dx1_r.at[1], n1).wait_recv()
     dxs2[...] = (over + dxr1[1].astype(F32)).astype(BF16)
-    start(ncopy(dxs2, dxr2, dx2_s, dx2_r, n2))
-    early_half(1)
-    z_collect(0)
-    early_near(0)
-    early_half(2)
-    z_collect(1)
-    early_near(1)
+    start(dx2_copy(0))
+    early_back(2)
+    l4(1)
     dxo = dx(n).T
     for k in range(NAR):
         cols = slice(k * CW, (k + 1) * CW)
         ograd[:, cols] = dxo[:, cols] + win_f[k]
-    z_collect(2)
+    d2()
+    early_near(0)
+    early_half(1)
+
+    @pl.when(b0 == 0)
+    def _():
+        e_near(0, 1).wait_recv()
+
+    @pl.when(b0 == 1)
+    def _():
+        fan_wait(0, 0, 2)
+
+    newton_begin(3 - b0)
+    newton_step()
+    early_half(2)
+    l5(1)
+    early_near(1)
+    vec_send(lv, lv_s, lv_r)
+    newton_step()
+    l5(2)
+    start(dx2_copy(1))
     early_near(2)
-    early_got(0)
-    early_got(1)
-
-    both = pl.ds(pl.multiple_of(b1 * 2 * CW, 2 * CW), 2 * CW)
-
-    def swap(m, k):
-        return ncopy(dkT.at[:, k * D:(k + 1) * D], orth.at[m], sw_s.at[k], sw_r.at[k], n1)
-
-    def give(base, k, res):
-        first, second = res[0:CW], res[CW:]
-        orth[base + b0] = jnp.where(b0 == 0, first, second)
-        dkT[:, k * D:(k + 1) * D] = jnp.where(b0 == 0, second, first)
-        start(swap(base + b0, k))
-
-    newton_begin(3 + b0, 0)
-    half_send(0)
-    newton_step(0)
-    half_send(1)
-    half_send(2)
-    newton_step(0)
-    late_fan(0)
-    late_fan(1)
-    give(3, 1, newton_last(0, both))
-    late_fan(2)
-    early_got(2)
-    newton_begin(5, 1)
-    newton_step(1)
-    newton_step(1)
-    orth[5] = newton_last(1, mycols)
-    relay(2)
+    newton_last(3 - b0, 1)
+
+    e_near(2 - b0, 1 - b0).wait_recv()
+    newton_begin(5 - b0)
+    newton_step()
+    newton_step()
+    newton_last(5 - b0, 2)
+    fan_wait(1, 1 + b0, b0)
+    fan_wait(2, 3 + b0, b0)
+    newton_begin(b0)
+    l_mom = pltpu.make_async_copy(mom.at[:, b1, b0], omom_h, loc_sem.at[8])
+    l_mom.start()
+    newton_step()
+    newton_step()
+    newton_last(b0, 0)
 
     ncopy(dxs[0], dxr1.at[0], dx1_s.at[0], dx1_r.at[0], n1).wait_recv()
-    ncopy(dxs2, dxr2, dx2_s, dx2_r, n2).wait_recv()
+    for c in (0, 1):
+        dx2_copy(c).wait_recv()
     ograd[...] = ograd[...] + (dxr1[0].astype(F32) + dxr2[...].astype(F32)).T
     l_ograd = pltpu.make_async_copy(ograd, ograd_h, loc_sem.at[7])
     l_ograd.start()
 
-    late_wait()
-    give(0, 0, newton(b0, 0, both))
-    gathered(2)
-    l_mom = pltpu.make_async_copy(
-        mom.at[:, b1, pl.ds(pl.multiple_of(b0 * CW, CW), CW), :], omom_h, loc_sem.at[8]
-    )
-    l_mom.start()
-    orth[2] = newton(2, 1, mycols)
-    swap(4 - b0, 1).wait_recv()
+    swap(2 + b0, 1).wait_recv()
+    swap(4 + b0, 2).wait_recv()
     swap(1 - b0, 0).wait_recv()
     l_orth = pltpu.make_async_copy(orth, oorth_h, loc_sem.at[9])
     l_orth.start()
@@ -841,25 +907,35 @@
     ovec[...] = vec_sum(vecw, vw_s, vw_r)
     late = vec_sum(lv, lv_s, lv_r)
     ovec2[0:1, :] = late[0:1]
-    ovec2[1:2, :] = late[8:9]
+    ovec2[1:2, :] = late[4:5]
     ovec2[2:3, :] = ovec[6:7, mycols]
     ovec2[3:8, :] = jnp.zeros((5, CW), F32)
 
     for m in range(3):
-        pending.extend((pair_copy(m), over_copy(m)))
-    for m in range(2):
-        @pl.when(b0 != m)
+        pending.extend((pair_copy(m), over_copy(m), e_swap(m, b1)))
+        if m < 2:
+            pending.append(half_copy(m, keepc))
+        for f, k, c in fans[m]:
+            pending.append(far_copy(m, f, k, c))
+
+            @pl.when(b0 != c)
+            def _():
+                near_copy(m, f, k, c).wait_send()
+
+        @pl.when(b0 != m % 2)
         def _():
-            near_copy(m).wait_send()
+            e_near(m, b0).wait_send()
 
     for c in pending:
         c.wait_send()
     vec_done(vecw, vw_s, vw_r)
     vec_done(lv, lv_s, lv_r)
+    group_loop(lambda i: d1_copy(i).wait_send())
+    group_loop(lambda i: d2_copy(o, i).wait_send())
     for k in range(3):
-        half_copy(k, pb).wait_send()
-        loop(lambda i: z_copy(k, i).wait_send(), 1, LINE)
-        loop(lambda i: share(k, qa, i).wait_send(), 1, LINE)
+        if k < 2:
+            loop(lambda i: z_copy(k, i).wait_send(), 1, LINE)
+            loop(lambda i: share(k, qa, i).wait_send(), 1, LINE)
         loop(lambda i: e_line(k, i).wait_send(), 1, LINE)
         loop(lambda i: e_share(k, qa, i).wait_send(), 1, LINE)
         if groups > 1:
@@ -890,28 +966,30 @@
         V((TB, D), BF16), V((TB, D), BF16), V((TB, D), BF16), V((TB, D), BF16), V((TB, D), BF16),
         V((TB, D), BF16), V((LEN, CW), BF16),
         V((NAR, 8, D), F32), V((vslots, 8, D), F32), V((CW, LEN), F32), V((CW, LEN), F32), V((3 * CW, LEN), BF16),
-        V((3, 2, 2, CW, D), BF16), V((3, 2, CW, D), BF16), V((3, 2, HR, D), BF16), V((3, 2, HR, D), BF16),
-        V((3, 2, HR, D), BF16), V((3, LINE, 2, PR, D), BF16), V((3, 2, PR, D), F32), V((3, 2, PR, D), BF16),
-        V((3, 2, PR, D), BF16), V((3, HR, D), BF16),
-        V((3, HR, D), BF16), V((LINE, 3, PR, D), BF16), V((vslots, 16, CW), F32), V((6, 2, D // 2, D), BF16),
-        V((groups, 3, 2, PR, D) if groups > 1 else (1, 1, 1, PR, D), BF16),
+        V((3, 2, 2, CW, D), BF16), V((3, 2, CW, D), BF16), V((3, CW, D), BF16), V((3, CW, D), BF16),
+        V((3, HR, D), BF16), V((3, HR, D), BF16), V((3, HR, D), BF16), V((3, LINE, PR, D), BF16), V((3, CW, HC), BF16),
+        V((2, 2, HR, HC), BF16), V((2, LINE, 2, PR, HC), BF16), V((2, HR, D), BF16), V((OWN, 2, PR, HC), BF16),
+        V((vslots, 8, CW), F32),
+        V((6, 2, 2, 2, HR, D), BF16),
         V((groups, 3, PR, D) if groups > 1 else (1, 1, PR, D), BF16),
+        V((groups, 3, 2, PR, HC) if groups > 1 else (1, 1, 1, PR, HC), BF16),
         V((2, D, TB), BF16), V((D, TB), BF16),
         dma(10), dma(4), dma(4), dma(2), dma(2), dma(4), dma(4), dma(3, 2), dma(3, 2), dma(1, 2), dma(1, 2),
         dma(4), dma(4), dma(4, TB // MID), dma(4, TB // MID), dma(4), dma(4), dma(vslots), dma(vslots),
         dma(vslots), dma(vslots),
         dma(3), dma(3), dma(3), dma(3), dma(3), dma(3), dma(3), dma(3), dma(3, LINE), dma(3, LINE),
+        dma(OWN), dma(OWN), dma(OWN), dma(OWN),
         dma(6, groups), dma(6, groups),
-        dma(6, LINE), dma(6, LINE), dma(6), dma(6), dma(2), dma(2), dma(2), dma(2),
-        dma(3), dma(3), dma(3, LINE), dma(3, LINE), dma(2, 2), dma(4), dma(2), dma(2),
-        dma(2), dma(2), one, one,
+        dma(6, LINE), dma(6, LINE), dma(6), dma(6),
+        dma(3), dma(3), dma(3, LINE), dma(3, LINE), dma(3), dma(3), dma(5, 2), dma(5, 4), dma(3), dma(3),
+        dma(2), dma(2), dma(2), dma(2),
     ]
     return pl.pallas_call(
         functools.partial(layer_kernel, wide),
         out_shape=[
             jax.ShapeDtypeStruct((TB, D), BF16),
             jax.ShapeDtypeStruct((TB, D), F32),
-            jax.ShapeDtypeStruct((6, CW, D), BF16),
+            jax.ShapeDtypeStruct((6, 2, HR, D), BF16),
             jax.ShapeDtypeStruct((6, CW, D), F32),
             jax.ShapeDtypeStruct((8, D), F32),
             jax.ShapeDtypeStruct((8, CW), F32),
@@ -994,14 +1072,14 @@
         for c in reads[k]:
             c.wait()
         if k < 4:
-            inm_v[k] = mom_b[k].astype(F32).T
+            inm_v[k] = mom_b[k].reshape(CW, D).astype(F32).T
             new = muon_step(inw_b[k], orth_b[k].T)
             inw_v[k] = new
             inl_v[k] = new.astype(BF16)
             ina_v[k] = blend(ina_b[k], new)
         else:
             j = k - 4
-            outm_v[j] = mom_b[k].astype(F32)
+            outm_v[j] = mom_b[k].reshape(CW, D).astype(F32)
             new = muon_step(outw_b[j], orth_b[k])
             outw_v[j] = new
             outl_v[j] = new.astype(BF16)
@@ -1032,7 +1110,7 @@
         in_specs=[any_] * 8 + [vm] * 10,
         out_specs=[any_] * 10 + [vm] * 8,
         scratch_shapes=[
-            V((6, CW, D), BF16), V((6, CW, D), F32), V(inner, F32), V(outer, F32), V(inner, F32), V(outer, F32),
+            V((6, 2, HR, D), BF16), V((6, CW, D), F32), V(inner, F32), V(outer, F32), V(inner, F32), V(outer, F32),
             V(inner, F32), V(outer, F32), V(inner, F32), V(outer, F32), V(inner, BF16), V(outer, BF16),
             V(inner, F32), V(outer, F32), V((TB, D), F32), V((TB, D), BF16),
             pltpu.SemaphoreType.DMA((4,)), pltpu.SemaphoreType.DMA((6, 4)), pltpu.SemaphoreType.DMA((6, 4)),

time: 114 us -> 106 us (0.930)
  Pallas kernels: 113 us -> 105 us
    pallas_call x1, Pallas kernels: 106 us -> 97.2 us  [run_layer(): pl.pallas_call(functools.partial(layer_kernel, wide), out_shape=[jax.Shap...]
where the time goes in v3:
time: 106 us
  Pallas kernels  105 us (99%)
    pallas_call x1, Pallas kernels, run_layer(): pl.pallas_call(functools.partial(layer_kernel, wide), out_shape=[jax.Shap...  97.2 us
    pallas_call x1, Pallas kernels, run_update(): pl.pallas_call(update_kernel, out_shape=[S((TB, D), BF16), S((TB, D), F32...  7.68 us

profile of v3, /device:TPU:0, one launch (start us, length us, event | category | flops | bytes accessed | tf_op | source)
XLA Modules:
  0.0 105.7 jit_solution(12994141867284143801)
XLA Ops:
  0.7 97.2 %layer.1 = (bf16[512,512]{1,0:T(8,128)(2,1)}, f32[512,512]{1,0:T(8,128)}, bf16[6,2,64,512]{3,2,1,0:T(8,128)(2,1)}, f32[6,128,512]{2,1,0:T(8,128)}, f32[8,512]{1,0:T(8,128)}, /*index=5*/f32[8,128]{1,0:T(8,128)}) custom-call(bf16[512,512]{1,0:T(8,128)(2,1)} %refs_0_.1, bf16[512,512]{1,0:T(8,128)(2,1)} %refs_1_.1, s32[4,128]{1,0:T(4,128)} %bitcast.3, ...), custom_call_target="tpu_custom_call" | custom-call | tf_op jit(solution)/shard_map/layer/pallas_call | solution.py:987
  97.9 7.7 %update.1 = (bf16[512,512]{1,0:T(8,128)(2,1)}, f32[512,512]{1,0:T(8,128)}, f32[4,512,128]{2,1,0:T(8,128)}, f32[2,128,512]{2,1,0:T(8,128)}, f32[4,512,128]{2,1,0:...) custom-call(bf16[512,512]{1,0:T(8,128)(2,1)} %get-tuple-element.24.o, ...), custom_call_target="tpu_custom_call" | custom-call | tf_op jit(solution)/shard_map/update/pallas_call | solution.py:1102

commit v4 on v3

--- a/solution.py
+++ b/solution.py
@@ -97,7 +97,7 @@
 
     own = rows(n, TB)
     ograd = s_ref.at[:, 3 * D:4 * D]
-    orth = mT
+    ograd_b = hr
     rln = rdn
     otok = cot
     dxs, dxs2 = (act, du), dr2r
@@ -180,88 +180,104 @@
     bcol[0] = jnp.broadcast_to(split[0:1, :], (CW, CW)).T
     bcol[1] = jnp.broadcast_to(split[1:2, :], (CW, CW)).T
 
-    def project(t):
-        tb = tok[rows(t, TB), :]
+    def project(t, c):
+        rr = pl.ds(pl.multiple_of(t * TB + c * half, half), half)
+        tb = tok[rr, :]
         qk = mm(tb, wqkv[:, 0:2 * CW])
         q = (qk[:, :CW] + split[0:1, :]).astype(BF16)
         k = qk[:, CW:].astype(BF16)
         q8 = q.astype(F32) * 0.125
         prod = q8 * k.astype(F32)
-        lane = lax.broadcasted_iota(jnp.int32, (TB, CW), 1)
-        low = lane < HD
+        low = lax.broadcasted_iota(jnp.int32, (half, CW), 1) < HD
         d0 = jnp.sum(jnp.where(low, prod, 0.0), axis=1, keepdims=True)
         d1 = jnp.sum(jnp.where(low, 0.0, prod), axis=1, keepdims=True)
-        rdn[rows(t, TB), :] = jnp.where(low, d0, d1)
+        rdn[rr, :] = jnp.where(low, d0, d1)
         lane1 = lax.broadcasted_iota(jnp.int32, (CW, CW), 1).astype(F32)
-        for j in range(TB // CW):
-            seg = jnp.broadcast_to(pay[t, j:j + 1, :], (CW, CW)).T
+        lowj = lane1 < HD
+        for j in range(half // CW):
+            seg = jnp.broadcast_to(pay[t, pl.ds(c * (half // CW) + j, 1), :], (CW, CW)).T
             part = q8[j * CW:(j + 1) * CW, :]
-            lowj = lane1 < HD
             hot = lambda base: jnp.where(seg == lane1 + base, 1.0, 0.0)
-            rr = pl.ds(pl.multiple_of(t * TB + j * CW, CW), CW)
-            qp[0, rr, 0:CW] = jnp.where(lowj, part, hot(-float(HD))).astype(BF16)
-            qp[1, rr, 0:CW] = jnp.where(lowj, hot(0.0), part).astype(BF16)
+            rj = pl.ds(pl.multiple_of(t * TB + c * half + j * CW, CW), CW)
+            qp[0, rj, 0:CW] = jnp.where(lowj, part, hot(-float(HD))).astype(BF16)
+            qp[1, rj, 0:CW] = jnp.where(lowj, hot(0.0), part).astype(BF16)
             rest = hot(float(HD)).astype(BF16)
-            qp[0, rr, CW:] = rest
-            qp[1, rr, CW:] = rest
+            qp[0, rj, CW:] = rest
+            qp[1, rj, CW:] = rest
         tT = mm_nt(wqkvT[...], tb)
-        bq = jnp.concatenate([bcol[0]] * (TB // CW), axis=1)
-        bv = jnp.concatenate([bcol[1]] * (TB // CW), axis=1)
-        cols = rows(t, TB)
-        qT[:, cols] = ((tT[0:CW] + bq).astype(BF16).astype(F32) * 0.125).astype(BF16)
+        bq = jnp.concatenate([bcol[0]] * (half // CW), axis=1)
+        bv = jnp.concatenate([bcol[1]] * (half // CW), axis=1)
+        qT[:, rr] = ((tT[0:CW] + bq).astype(BF16).astype(F32) * 0.125).astype(BF16)
         kT = tT[CW:2 * CW].astype(BF16)
         vT = (tT[2 * CW:] + bv).astype(BF16)
-        code = jnp.concatenate([pay[t, 4 + j:5 + j, :] for j in range(TB // CW)], axis=1)
-        rowi = lax.broadcasted_iota(jnp.int32, (HD, TB), 0).astype(F32)
+        code = jnp.concatenate(
+            [pay[t, pl.ds(4 + c * (half // CW) + j, 1), :] for j in range(half // CW)], axis=1
+        )
+        rowi = lax.broadcasted_iota(jnp.int32, (HD, half), 0).astype(F32)
         keep = lambda base: jnp.where(code == rowi + base, 0.0, NEG).astype(BF16)
         first, second, third = keep(0.0), keep(float(HD)), keep(float(2 * HD))
-        ones = jnp.ones((HD, TB), BF16)
-        kTp[0, 0:HD, cols] = kT[0:HD]
-        kTp[0, HD:CW, cols] = first
-        kTp[1, 0:HD, cols] = first
-        kTp[1, HD:CW, cols] = kT[HD:]
-        vTp[0, 0:HD, cols] = vT[0:HD]
-        vTp[0, HD:, cols] = ones
-        vTp[1, 0:HD, cols] = ones
-        vTp[1, HD:, cols] = vT[HD:]
+        ones = jnp.ones((HD, half), BF16)
+        kTp[0, 0:HD, rr] = kT[0:HD]
+        kTp[0, HD:CW, rr] = first
+        kTp[1, 0:HD, rr] = first
+        kTp[1, HD:CW, rr] = kT[HD:]
+        vTp[0, 0:HD, rr] = vT[0:HD]
+        vTp[0, HD:, rr] = ones
+        vTp[1, 0:HD, rr] = ones
+        vTp[1, HD:, rr] = vT[HD:]
         for h in range(2):
-            kTp[h, CW:CW + HD, cols] = second
-            kTp[h, CW + HD:, cols] = third
+            kTp[h, CW:CW + HD, rr] = second
+            kTp[h, CW + HD:, rr] = third
+
+    def relayed(c):
+        return ncopy(ag_rows(n2, c), ag_rows(n2, c), rly_s.at[c], rly_r.at[c], n1)
 
     def project_step(i, _):
-        @pl.when(i == 1)
+        @pl.when(i == 2)
         def _():
             arrived(pay.at[n1], pay_s.at[1], pay_r.at[1], n1)
-            for c in (0, 1):
-                arrived(ag_rows(n1, c), ag_s.at[c], ag_r.at[c], n1)
+            arrived(ag_rows(n1, 0), ag_s.at[0], ag_r.at[0], n1)
             l_min.wait()
             for k in range(4):
                 mT[k] = win_f[k].T
 
-        @pl.when(i == 2)
+        @pl.when(i == 3)
+        def _():
+            arrived(ag_rows(n1, 1), ag_s.at[1], ag_r.at[1], n1)
+
+        @pl.when(i == 4)
         def _():
             arrived(pay.at[n2], pay_s.at[2], pay_r.at[2], n2)
             arrived(pay.at[n3], pay_s.at[3], pay_r.at[3], n3)
-            for c in (0, 1):
-                arrived(ag_rows(n2, c), ag_s.at[2 + c], ag_r.at[2 + c], n2)
-                ncopy(ag_rows(n2, c), ag_rows(n2, c), rly_s.at[c], rly_r.at[c], n1).start()
+            arrived(ag_rows(n2, 0), ag_s.at[2], ag_r.at[2], n2)
+            relayed(0).start()
+
+        @pl.when(i == 5)
+        def _():
+            arrived(ag_rows(n3, 0), rly_s.at[0], rly_r.at[0], n1)
+
+        @pl.when(i == 6)
+        def _():
+            arrived(ag_rows(n2, 1), ag_s.at[3], ag_r.at[3], n2)
+            relayed(1).start()
             for x in (2, 1):
                 for c in wg_list(wg_s, wg_r, x, n, rel(x)):
                     c.start()
 
-        @pl.when(i == 3)
+        @pl.when(i == 7)
         def _():
-            for c in (0, 1):
-                arrived(ag_rows(n3, c), rly_s.at[c], rly_r.at[c], n1)
-
-        project(rel(i))
+            arrived(ag_rows(n3, 1), rly_s.at[1], rly_r.at[1], n1)
+
+        far = i // 4
+        x = (1 - far) * (i // 2) + far * (2 + lax.rem(i, 2))
+        c = (1 - far) * lax.rem(i, 2) + far * (i // 2 - 2)
+        project(rel(x), c)
         return 0
 
-    lax.fori_loop(0, NAR, project_step, 0)
+    lax.fori_loop(0, 2 * NAR, project_step, 0)
     for x in (2, 1):
         pending.extend(wg_list(wg_s, wg_r, x, n, rel(x)))
-    for c in (0, 1):
-        pending.append(ncopy(ag_rows(n2, c), ag_rows(n2, c), rly_s.at[c], rly_r.at[c], n1))
+    pending.extend((relayed(0), relayed(1)))
 
     eye = lax.broadcasted_iota(jnp.int32, (CW, CW), 0) == lax.broadcasted_iota(jnp.int32, (CW, CW), 1)
 
@@ -287,9 +303,15 @@
             top = jnp.max(s, axis=1, keepdims=True)
             e = jnp.exp(s - top).astype(BF16)
             e_ref[h, rr, :] = e
-            parts.append(mm_nt(vTp[h], e))
-        num = jnp.concatenate([parts[0][:HD], parts[1][HD:]], axis=0)
-        den = 1.0 / jnp.concatenate([parts[0][HD:], parts[1][:HD]], axis=0)
+            parts.append(mm_nt(vTp[0, 0:HD + 16, :] if h == 0 else vTp[1, HD - 16:, :], e))
+        num = jnp.concatenate([parts[0][:HD], parts[1][16:]], axis=0)
+        den = jnp.concatenate(
+            [
+                jnp.broadcast_to(1.0 / parts[0][HD:HD + 1], (HD, TB)),
+                jnp.broadcast_to(1.0 / parts[1][0:1], (HD, TB)),
+            ],
+            axis=0,
+        )
         cn = (num * den).T
         ctxn[rr, :] = cn
         rln[rr, :] = den.T
@@ -404,7 +426,7 @@
         grad = mm_tn(left[...], right[...]).astype(BF16)
         for t in range(NAR):
             gst[k, t % 2, t // 2] = grad[t * CW:(t + 1) * CW]
-        start(ncopy(gst.at[k, 1 - b0], gr1.at[k], g1_s.at[k], g1_r.at[k], n1))
+        ncopy(gst.at[k, 1 - b0], gr1.at[k], g1_s.at[k], g1_r.at[k], n1).start()
 
     def loop(fn, first, count):
         def go(i, c):
@@ -706,7 +728,6 @@
         ("a", 0): [(early_over, 0)],
         ("a", 1): [(early_over, 1)],
         ("a", 2): [(early_over, 2)],
-        ("a", 3): [(lambda m: vec_early(), 0)],
         (0, 1, 0): [(early_pair, 0)],
         (0, 1, 1): [(l2, 0)],
         (0, 2, 0): [(early_pair, 1)],
@@ -771,6 +792,8 @@
     lax.fori_loop(0, NAR, backward_v, 0)
     gT[2 * CW:, :] = dvT[...].astype(BF16)
     l1(0, gT[2 * CW:, :])
+    for k in range(3):
+        ncopy(gst.at[k, 1 - b0], gr1.at[k], g1_s.at[k], g1_r.at[k], n1).wait_send()
 
     def backward(h):
         hs = slice(h * HD, (h + 1) * HD)
@@ -815,8 +838,11 @@
         p = (COEF_B * a + COEF_C * mm(al, al)).astype(BF16)
         XB[...] = COEF_A * x + mm(p, xl)
 
+    def orth(m):
+        return gst.at[m // 2, lax.rem(m, 2), 0]
+
     def swap(m, k):
-        return ncopy(dkT.at[:, k * D:(k + 1) * D], orth.at[m], sw_s.at[k], sw_r.at[k], n1)
+        return ncopy(gst.at[k, 0, 1], orth(m), sw_s.at[k], sw_r.at[k], n1)
 
     def newton_last(m, k):
         xl = XB[...].astype(BF16)
@@ -826,8 +852,8 @@
         z = mm_nt(y.astype(BF16), xl).astype(BF16)
         res = COEF_A * xo + COEF_B * y + COEF_C * mm(z, xl)
         first, second = res[0:CW], res[CW:]
-        orth[m] = jnp.where(b0 == 0, first, second)
-        dkT[:, k * D:(k + 1) * D] = jnp.where(b0 == 0, second, first)
+        gst[m // 2, lax.rem(m, 2), 0] = jnp.where(b0 == 0, first, second).astype(BF16)
+        gst[k, 0, 1] = jnp.where(b0 == 0, second, first).astype(BF16)
         start(swap(m, k))
 
     def dx2_copy(c):
@@ -840,22 +866,23 @@
     start(ncopy(dxs[0], dxr1.at[0], dx1_s.at[0], dx1_r.at[0], n1))
     early_back(1)
     over = dx(n2)
-    early_half(0)
     one = jnp.ones((8, LEN), BF16)
     upper_rows = lax.broadcasted_iota(jnp.int32, (8, CW), 0) < 4
     lv[o] = jnp.where(upper_rows, mm_nt(one, gT[0:CW, :]), mm_nt(one, gT[2 * CW:, :]))
     ncopy(dxs[1], dxr1.at[1], dx1_s.at[1], dx1_r.at[1], n1).wait_recv()
     dxs2[...] = (over + dxr1[1].astype(F32)).astype(BF16)
     start(dx2_copy(0))
-    early_back(2)
+    early_half(0)
     l4(1)
     dxo = dx(n).T
     for k in range(NAR):
         cols = slice(k * CW, (k + 1) * CW)
         ograd[:, cols] = dxo[:, cols] + win_f[k]
     d2()
+    settled = pending[:]
+    pending.clear()
+    early_back(2)
     early_near(0)
-    early_half(1)
 
     @pl.when(b0 == 0)
     def _():
@@ -867,43 +894,45 @@
 
     newton_begin(3 - b0)
     newton_step()
+    early_half(1)
+    l5(1)
+    newton_step()
+    vec_early()
+    vec_send(lv, lv_s, lv_r)
+    newton_last(3 - b0, 1)
+    l5(2)
+    early_near(1)
     early_half(2)
-    l5(1)
-    early_near(1)
-    vec_send(lv, lv_s, lv_r)
-    newton_step()
-    l5(2)
+
+    def fans_wait():
+        fan_wait(1, 1 + b0, b0)
+        fan_wait(2, 3 + b0, b0)
+
+    for c in settled:
+        c.wait_send()
+    for k in range(3):
+        loop(lambda i: e_line(k, i).wait_send(), 1, LINE)
+        if k < 2:
+            loop(lambda i: z_copy(k, i).wait_send(), 1, LINE)
+            loop(lambda i: share(k, qa, i).wait_send(), 1, LINE)
+    group_loop(lambda i: d1_copy(i).wait_send())
+
+    @pl.when(b0 == 0)
+    def _():
+        fans_wait()
+
+    @pl.when(b0 == 1)
+    def _():
+        e_near(1, 0).wait_recv()
+
     start(dx2_copy(1))
-    early_near(2)
-    newton_last(3 - b0, 1)
-
-    e_near(2 - b0, 1 - b0).wait_recv()
-    newton_begin(5 - b0)
+    newton_begin(4 * b0)
     newton_step()
     newton_step()
-    newton_last(5 - b0, 2)
-    fan_wait(1, 1 + b0, b0)
-    fan_wait(2, 3 + b0, b0)
-    newton_begin(b0)
+    newton_last(4 * b0, 2)
+    early_near(2)
     l_mom = pltpu.make_async_copy(mom.at[:, b1, b0], omom_h, loc_sem.at[8])
     l_mom.start()
-    newton_step()
-    newton_step()
-    newton_last(b0, 0)
-
-    ncopy(dxs[0], dxr1.at[0], dx1_s.at[0], dx1_r.at[0], n1).wait_recv()
-    for c in (0, 1):
-        dx2_copy(c).wait_recv()
-    ograd[...] = ograd[...] + (dxr1[0].astype(F32) + dxr2[...].astype(F32)).T
-    l_ograd = pltpu.make_async_copy(ograd, ograd_h, loc_sem.at[7])
-    l_ograd.start()
-
-    swap(2 + b0, 1).wait_recv()
-    swap(4 + b0, 2).wait_recv()
-    swap(1 - b0, 0).wait_recv()
-    l_orth = pltpu.make_async_copy(orth, oorth_h, loc_sem.at[9])
-    l_orth.start()
-
     ovec[...] = vec_sum(vecw, vw_s, vw_r)
     late = vec_sum(lv, lv_s, lv_r)
     ovec2[0:1, :] = late[0:1]
@@ -911,6 +940,31 @@
     ovec2[2:3, :] = ovec[6:7, mycols]
     ovec2[3:8, :] = jnp.zeros((5, CW), F32)
 
+    @pl.when(b0 == 0)
+    def _():
+        e_near(2, 1).wait_recv()
+
+    @pl.when(b0 == 1)
+    def _():
+        fans_wait()
+
+    newton_begin(5 - 4 * b0)
+    newton_step()
+    newton_step()
+    newton_last(5 - 4 * b0, 0)
+
+    ncopy(dxs[0], dxr1.at[0], dx1_s.at[0], dx1_r.at[0], n1).wait_recv()
+    for c in (0, 1):
+        dx2_copy(c).wait_recv()
+    ograd_b[...] = (ograd[...] + (dxr1[0].astype(F32) + dxr2[...].astype(F32)).T).astype(BF16)
+    l_ograd = pltpu.make_async_copy(ograd_b, ograd_h, loc_sem.at[7])
+    l_ograd.start()
+    swap(2 + b0, 1).wait_recv()
+    swap(4 * (1 - b0), 2).wait_recv()
+    swap(1 + 4 * b0, 0).wait_recv()
+    l_orth = pltpu.make_async_copy(gst.at[:, :, 0], oorth_h, loc_sem.at[9])
+    l_orth.start()
+
     for m in range(3):
         pending.extend((pair_copy(m), over_copy(m), e_swap(m, b1)))
         if m < 2:
@@ -930,13 +984,8 @@
         c.wait_send()
     vec_done(vecw, vw_s, vw_r)
     vec_done(lv, lv_s, lv_r)
-    group_loop(lambda i: d1_copy(i).wait_send())
     group_loop(lambda i: d2_copy(o, i).wait_send())
     for k in range(3):
-        if k < 2:
-            loop(lambda i: z_copy(k, i).wait_send(), 1, LINE)
-            loop(lambda i: share(k, qa, i).wait_send(), 1, LINE)
-        loop(lambda i: e_line(k, i).wait_send(), 1, LINE)
         loop(lambda i: e_share(k, qa, i).wait_send(), 1, LINE)
         if groups > 1:
             loop(lambda i: across(k, i).wait_send(), 1, groups)
@@ -988,9 +1037,9 @@
         functools.partial(layer_kernel, wide),
         out_shape=[
             jax.ShapeDtypeStruct((TB, D), BF16),
-            jax.ShapeDtypeStruct((TB, D), F32),
+            jax.ShapeDtypeStruct((TB, D), BF16),
             jax.ShapeDtypeStruct((6, 2, HR, D), BF16),
-            jax.ShapeDtypeStruct((6, CW, D), F32),
+            jax.ShapeDtypeStruct((3, 2, CW, D), BF16),
             jax.ShapeDtypeStruct((8, D), F32),
             jax.ShapeDtypeStruct((8, CW), F32),
         ],
@@ -1027,10 +1076,10 @@
     tok_o, grad_o, inm_o, outm_o, inw_o, outw_o, inl_o, outl_o, ina_o, outa_o,
     s1_o, s2_o, sv_o, sa_o, p1_o, p2_o, pv_o, pa_o,
     mom_b, orth_b, inw_b, outw_b, ina_b, outa_b,
-    inm_v, outm_v, inw_v, outw_v, inl_v, outl_v, ina_v, outa_v, grad_v, tok_v, thru, rsem, wsem,
+    inm_v, outm_v, inw_v, outw_v, inl_v, outl_v, ina_v, outa_v, grad_v, grad_b, tok_v, thru, rsem, wsem,
 ):
     whole = [
-        pltpu.make_async_copy(ograd, grad_v, thru.at[0]),
+        pltpu.make_async_copy(ograd, grad_b, thru.at[0]),
         pltpu.make_async_copy(otok, tok_v, thru.at[1]),
     ]
     back = [
@@ -1040,7 +1089,7 @@
     reads, writes = [], []
     for k in range(6):
         j, inner = (k, True) if k < 4 else (k - 4, False)
-        srcs = (mom.at[k], orth.at[k], (in_w if inner else out_w).at[j], (in_a if inner else out_a).at[j])
+        srcs = (mom.at[k], orth.at[k // 2, k % 2], (in_w if inner else out_w).at[j], (in_a if inner else out_a).at[j])
         dsts = (
             mom_b.at[k], orth_b.at[k], (inw_b if inner else outw_b).at[j], (ina_b if inner else outa_b).at[j],
         )
@@ -1068,19 +1117,21 @@
     for k in range(6):
         if k in (1, 2):
             whole[k - 1].wait()
+            if k == 1:
+                grad_v[...] = grad_b[...].astype(F32)
             back[k - 1].start()
         for c in reads[k]:
             c.wait()
         if k < 4:
             inm_v[k] = mom_b[k].reshape(CW, D).astype(F32).T
-            new = muon_step(inw_b[k], orth_b[k].T)
+            new = muon_step(inw_b[k], orth_b[k].astype(F32).T)
             inw_v[k] = new
             inl_v[k] = new.astype(BF16)
             ina_v[k] = blend(ina_b[k], new)
         else:
             j = k - 4
             outm_v[j] = mom_b[k].reshape(CW, D).astype(F32)
-            new = muon_step(outw_b[j], orth_b[k])
+            new = muon_step(outw_b[j], orth_b[k].astype(F32))
             outw_v[j] = new
             outl_v[j] = new.astype(BF16)
             outa_v[j] = blend(outa_b[j], new)
@@ -1110,9 +1161,9 @@
         in_specs=[any_] * 8 + [vm] * 10,
         out_specs=[any_] * 10 + [vm] * 8,
         scratch_shapes=[
-            V((6, 2, HR, D), BF16), V((6, CW, D), F32), V(inner, F32), V(outer, F32), V(inner, F32), V(outer, F32),
+            V((6, 2, HR, D), BF16), V((6, CW, D), BF16), V(inner, F32), V(outer, F32), V(inner, F32), V(outer, F32),
             V(inner, F32), V(outer, F32), V(inner, F32), V(outer, F32), V(inner, BF16), V(outer, BF16),
-            V(inner, F32), V(outer, F32), V((TB, D), F32), V((TB, D), BF16),
+            V(inner, F32), V(outer, F32), V((TB, D), F32), V((TB, D), BF16), V((TB, D), BF16),
             pltpu.SemaphoreType.DMA((4,)), pltpu.SemaphoreType.DMA((6, 4)), pltpu.SemaphoreType.DMA((6, 4)),
         ],
         compiler_params=pltpu.CompilerParams(vmem_limit_bytes=60 * MB),

time: 106 us -> 104 us (0.981)
  Pallas kernels: 105 us -> 103 us
    pallas_call x1, Pallas kernels: 97.2 us -> 95.6 us  [run_layer(): pl.pallas_call(functools.partial(layer_kernel, wide), out_shape=[jax.Shap...]
where the time goes in v4:
time: 104 us
  Pallas kernels  103 us (99%)
    pallas_call x1, Pallas kernels, run_layer(): pl.pallas_call(functools.partial(layer_kernel, wide), out_shape=[jax.Shap...  95.6 us
    pallas_call x1, Pallas kernels, run_update(): pl.pallas_call(update_kernel, out_shape=[S((TB, D), BF16), S((TB, D), F32...  7.35 us

profile of v4, /device:TPU:0, one launch (start us, length us, event | category | flops | bytes accessed | tf_op | source)
XLA Modules:
  0.0 103.8 jit_solution(14712214192064872185)
XLA Ops:
  0.7 95.6 %layer.1 = (bf16[512,512]{1,0:T(8,128)(2,1)}, bf16[512,512]{1,0:T(8,128)(2,1)}, bf16[6,2,64,512]{3,2,1,0:T(8,128)(2,1)}, bf16[3,2,128,512]{3,2,1,0:T(8,128)(2,1)}, f32[8,512]{1,0:T(8,128)}, /*index=5*/f32[8,128]{1,0:T(8,128)}) custom-call(bf16[512,512]{1,0:T(8,128)(2,1)} %refs_0_.1, bf16[512,512]{1,0:T(8,128)(2,1)} %refs_1_.1, s32[4,128]{1,0:T(4,128)} %bitcast.3, ...), custom_call_target="tpu_custom_call" | custom-call | tf_op jit(solution)/shard_map/layer/pallas_call | solution.py:1036
  96.3 7.4 %update.1 = (bf16[512,512]{1,0:T(8,128)(2,1)}, f32[512,512]{1,0:T(8,128)}, f32[4,512,128]{2,1,0:T(8,128)}, f32[2,128,512]{2,1,0:T(8,128)}, f32[4,512,128]{2,1,0:...) custom-call(bf16[512,512]{1,0:T(8,128)(2,1)} %get-tuple-element.24.o, ...), custom_call_target="tpu_custom_call" | custom-call | tf_op jit(solution)/shard_map/update/pallas_call | solution.py:1153

commit v5 on v4

--- a/solution.py
+++ b/solution.py
@@ -51,7 +51,7 @@
         tok_h, cot_h, seg_i, pad_i, gen_i, win_h, wout_h, min_h, mout_h, shared, split,
         otok_h, ograd_h, omom_h, oorth_h, ovec, ovec2,
         tok, cot, pay, win_f, wout_f, mT, wqkvT, wqkv, wup, wod, bcol,
-        qp, kTp, vTp, qT, rdn, s_ref, e_ref, ctxn, ctx_s, ctxf,
+        qp, kTp, vTp, qT, rdn, s_ref, e_ref, tops_n, ctxn, ctx_s, ctxf,
         hr, act, du, dr2r, dr1r, dcst, dcr, vecs, vecw, dkT, dvT, gT,
         gst, gr1, eys, eyr, es1, er1, zse, zre, lr1, zs, zr, zd, zdr, lv, mom, grp, grl,
         dxr1, dxr2,
@@ -274,22 +274,65 @@
         project(rel(x), c)
         return 0
 
-    lax.fori_loop(0, 2 * NAR, project_step, 0)
+    lax.fori_loop(0, NAR, project_step, 0)
+
+    eye = lax.broadcasted_iota(jnp.int32, (CW, CW), 0) == lax.broadcasted_iota(jnp.int32, (CW, CW), 1)
+    sh = s_ref.at[:, 0:2 * TB]
+    near_keys = rows(b1, 2 * TB)
+    far_keys = rows(1 - b1, 2 * TB)
+    lane_low = lax.broadcasted_iota(jnp.int32, (TB, CW), 1) < HD
+
+    def v_rows(h):
+        return slice(0, HD + 16) if h == 0 else slice(HD - 16, CW)
+
+    def both_heads(parts):
+        num = jnp.concatenate([parts[0][:HD], parts[1][16:]], axis=0)
+        den = jnp.concatenate(
+            [
+                jnp.broadcast_to(parts[0][HD:HD + 1], (HD, TB)),
+                jnp.broadcast_to(parts[1][0:1], (HD, TB)),
+            ],
+            axis=0,
+        )
+        return num.T, den.T
+
+    def attend_near(x, _):
+        t = rel(x)
+        rr = rows(t, TB)
+        low = lax.rem(t, 2)
+        parts, tops = [], []
+        for h in range(2):
+            sh[...] = mm(qp[h, rr, :], kTp[h, :, near_keys])
+            for j in range(TB // CW):
+                diag = rdn[pl.ds(pl.multiple_of(t * TB + j * CW, CW), CW), h * HD:h * HD + 1]
+                cc = pl.ds(pl.multiple_of(low * TB + j * CW, CW), CW)
+                sub = pl.ds(j * CW, CW)
+                s_ref[sub, cc] = jnp.where(eye, diag, s_ref[sub, cc])
+            sv = sh[...]
+            top = jnp.max(sv, axis=1, keepdims=True)
+            e = jnp.exp(sv - top).astype(BF16)
+            e_ref[h, rr, near_keys] = e
+            parts.append(mm_nt(vTp[h, v_rows(h), near_keys], e))
+            tops.append(top)
+        num, den = both_heads(parts)
+        ctxn[rr, :] = num
+        rln[rr, :] = den
+        tops_n[low] = jnp.where(lane_low, tops[0], tops[1])
+        return 0
+
+    lax.fori_loop(0, 2, attend_near, 0)
+    lax.fori_loop(NAR, 2 * NAR, project_step, 0)
     for x in (2, 1):
         pending.extend(wg_list(wg_s, wg_r, x, n, rel(x)))
     pending.extend((relayed(0), relayed(1)))
 
-    eye = lax.broadcasted_iota(jnp.int32, (CW, CW), 0) == lax.broadcasted_iota(jnp.int32, (CW, CW), 1)
-
     def ctx_copy(x, t):
         return ncopy(
             ctx_s.at[rows(t, TB)], ctxf.at[:, mycols], ctx_sem.at[x], ctx_rem.at[x], t
         )
 
-    def attend(i, _):
-        hi = 1 - i // 2
-        lo = lax.rem((i + 1) // 2, 2)
-        t = lax.rem(b0 + lo, 2) + 2 * lax.rem(b1 + hi, 2)
+    def attend_far(i, _):
+        t = rel(2 + i)
         rr = rows(t, TB)
         parts = []
         for h in range(2):
@@ -299,39 +342,60 @@
                 diag = rdn[cc, h * HD:h * HD + 1]
                 sub = pl.ds(j * CW, CW)
                 s_ref[sub, cc] = jnp.where(eye, diag, s_ref[sub, cc])
-            s = s_ref[...]
-            top = jnp.max(s, axis=1, keepdims=True)
-            e = jnp.exp(s - top).astype(BF16)
+            sv = s_ref[...]
+            top = jnp.max(sv, axis=1, keepdims=True)
+            e = jnp.exp(sv - top).astype(BF16)
             e_ref[h, rr, :] = e
-            parts.append(mm_nt(vTp[0, 0:HD + 16, :] if h == 0 else vTp[1, HD - 16:, :], e))
-        num = jnp.concatenate([parts[0][:HD], parts[1][16:]], axis=0)
-        den = jnp.concatenate(
-            [
-                jnp.broadcast_to(1.0 / parts[0][HD:HD + 1], (HD, TB)),
-                jnp.broadcast_to(1.0 / parts[1][0:1], (HD, TB)),
-            ],
-            axis=0,
-        )
-        cn = (num * den).T
+            parts.append(mm_nt(vTp[h, v_rows(h), :], e))
+        num, den = both_heads(parts)
+        inv = 1.0 / den
+        cn = num * inv
         ctxn[rr, :] = cn
-        rln[rr, :] = den.T
+        rln[rr, :] = inv
         ctx_s[rr, :] = cn.astype(BF16)
-
-        @pl.when(i < 3)
-        def _():
-            x = lo + 2 * hi
-            ctx_copy(x, t).start()
-
-        @pl.when(i == 2)
+        ctx_copy(2 + i, t).start()
+        return 0
+
+    def attend_rest(i, _):
+        t = rel(1 - i)
+
+        @pl.when(i == 1)
         def _():
             for c in wg_list(wg_s, wg_r, 2, n2, n2):
                 c.wait_recv()
             for c in wg_list(wr_s, wr_r, 0, n2, n1):
                 c.start()
 
+        rr = rows(t, TB)
+        low = lax.rem(t, 2)
+        parts, shrink = [], []
+        for h in range(2):
+            sh[...] = mm(qp[h, rr, :], kTp[h, :, far_keys])
+            sv = sh[...]
+            old = tops_n[low, :, h * HD:h * HD + 1]
+            top = jnp.maximum(jnp.max(sv, axis=1, keepdims=True), old)
+            less = jnp.exp(old - top)
+            e = jnp.exp(sv - top).astype(BF16)
+            e_ref[h, rr, far_keys] = e
+            e_ref[h, rr, near_keys] = (e_ref[h, rr, near_keys].astype(F32) * less).astype(BF16)
+            parts.append(mm_nt(vTp[h, v_rows(h), far_keys], e))
+            shrink.append(less)
+        num, den = both_heads(parts)
+        less = jnp.where(lane_low, shrink[0], shrink[1])
+        inv = 1.0 / (rln[rr, :] * less + den)
+        cn = (ctxn[rr, :] * less + num) * inv
+        ctxn[rr, :] = cn
+        rln[rr, :] = inv
+        ctx_s[rr, :] = cn.astype(BF16)
+
+        @pl.when(i == 0)
+        def _():
+            ctx_copy(1, t).start()
+
         return 0
 
-    lax.fori_loop(0, NAR, attend, 0)
+    lax.fori_loop(0, 2, attend_far, 0)
+    lax.fori_loop(0, 2, attend_rest, 0)
     pending.extend(wg_list(wr_s, wr_r, 0, n2, n1))
     for x in (1, 2, 3):
         pending.append(ctx_copy(x, rel(x)))
@@ -1010,7 +1074,7 @@
         V((3 * CW, D), BF16), V((D, 3 * CW), BF16),
         V((D, D), BF16), V((2, D, D), BF16), V((2, CW, CW), F32),
         V((2, LEN, 2 * CW), BF16), V((2, 2 * CW, LEN), BF16), V((2, CW, LEN), BF16), V((CW, LEN), BF16),
-        V((LEN, CW), F32), V((TB, LEN), F32), V((2, LEN, LEN), BF16),
+        V((LEN, CW), F32), V((TB, LEN), F32), V((2, LEN, LEN), BF16), V((2, TB, CW), F32),
         V((LEN, CW), F32), V((LEN, CW), BF16), V((TB, D), BF16),
         V((TB, D), BF16), V((TB, D), BF16), V((TB, D), BF16), V((TB, D), BF16), V((TB, D), BF16),
         V((TB, D), BF16), V((LEN, CW), BF16),

time: 104 us -> 103 us (level)
    pallas_call x1, Pallas kernels: 95.6 us -> 94.5 us  [run_layer(): pl.pallas_call(functools.partial(layer_kernel, wide), out_shape=[jax.Shap...]
where the time goes in v5:
time: 103 us
  Pallas kernels  102 us (99%)
    pallas_call x1, Pallas kernels, run_layer(): pl.pallas_call(functools.partial(layer_kernel, wide), out_shape=[jax.Shap...  94.5 us
    pallas_call x1, Pallas kernels, run_update(): pl.pallas_call(update_kernel, out_shape=[S((TB, D), BF16), S((TB, D), F32...  7.35 us

profile of v5, /device:TPU:0, one launch (start us, length us, event | category | flops | bytes accessed | tf_op | source)
XLA Modules:
  0.0 102.7 jit_solution(13585245706187554699)
XLA Ops:
  0.7 94.5 %layer.1 = (bf16[512,512]{1,0:T(8,128)(2,1)}, bf16[512,512]{1,0:T(8,128)(2,1)}, bf16[6,2,64,512]{3,2,1,0:T(8,128)(2,1)}, bf16[3,2,128,512]{3,2,1,0:T(8,128)(2,1)}, f32[8,512]{1,0:T(8,128)}, /*index=5*/f32[8,128]{1,0:T(8,128)}) custom-call(bf16[512,512]{1,0:T(8,128)(2,1)} %refs_0_.1, bf16[512,512]{1,0:T(8,128)(2,1)} %refs_1_.1, s32[4,128]{1,0:T(4,128)} %bitcast.3, ...), custom_call_target="tpu_custom_call" | custom-call | tf_op jit(solution)/shard_map/layer/pallas_call | solution.py:1100
  95.2 7.4 %update.1 = (bf16[512,512]{1,0:T(8,128)(2,1)}, f32[512,512]{1,0:T(8,128)}, f32[4,512,128]{2,1,0:T(8,128)}, f32[2,128,512]{2,1,0:T(8,128)}, f32[4,512,128]{2,1,0:...) custom-call(bf16[512,512]{1,0:T(8,128)(2,1)} %get-tuple-element.24.o, ...), custom_call_target="tpu_custom_call" | custom-call | tf_op jit(solution)/shard_map/update/pallas_call | solution.py:1217

commit v6 on v5

--- a/solution.py
+++ b/solution.py
@@ -374,12 +374,12 @@
             sv = sh[...]
             old = tops_n[low, :, h * HD:h * HD + 1]
             top = jnp.maximum(jnp.max(sv, axis=1, keepdims=True), old)
-            less = jnp.exp(old - top)
+            less = jnp.exp(old - top).astype(BF16)
             e = jnp.exp(sv - top).astype(BF16)
             e_ref[h, rr, far_keys] = e
-            e_ref[h, rr, near_keys] = (e_ref[h, rr, near_keys].astype(F32) * less).astype(BF16)
+            e_ref[h, rr, near_keys] = e_ref[h, rr, near_keys] * less
             parts.append(mm_nt(vTp[h, v_rows(h), far_keys], e))
-            shrink.append(less)
+            shrink.append(less.astype(F32))
         num, den = both_heads(parts)
         less = jnp.where(lane_low, shrink[0], shrink[1])
         inv = 1.0 / (rln[rr, :] * less + den)
@@ -890,9 +890,14 @@
     both_rows = pl.ds(pl.multiple_of(b1 * 2 * CW, 2 * CW), 2 * CW)
     XB = s_ref.at[:, 0:D]
 
-    def newton_begin(m):
-        xin = mom[m].reshape(D, D).astype(F32)
-        XB[...] = xin * (1.0 / (jnp.sqrt(jnp.sum(xin * xin)) + 1e-07))
+    def newton_first(m):
+        xl = mom[m].reshape(D, D)
+        x = xl.astype(F32)
+        inv = 1.0 / (jnp.sqrt(jnp.sum(x * x)) + 1e-07)
+        a = mm_nt(xl, xl) * (inv * inv)
+        al = a.astype(BF16)
+        p = (COEF_B * a + COEF_C * mm(al, al)).astype(BF16)
+        XB[...] = (COEF_A * x + mm(p, xl)) * inv
 
     def newton_step():
         x = XB[...]
@@ -956,8 +961,7 @@
     def _():
         fan_wait(0, 0, 2)
 
-    newton_begin(3 - b0)
-    newton_step()
+    newton_first(3 - b0)
     early_half(1)
     l5(1)
     newton_step()
@@ -990,8 +994,7 @@
         e_near(1, 0).wait_recv()
 
     start(dx2_copy(1))
-    newton_begin(4 * b0)
-    newton_step()
+    newton_first(4 * b0)
     newton_step()
     newton_last(4 * b0, 2)
     early_near(2)
@@ -1012,8 +1015,7 @@
     def _():
         fans_wait()
 
-    newton_begin(5 - 4 * b0)
-    newton_step()
+    newton_first(5 - 4 * b0)
     newton_step()
     newton_last(5 - 4 * b0, 0)
 

time: 103 us -> 102 us (level)
    pallas_call x1, Pallas kernels: 94.5 us -> 93.4 us  [run_layer(): pl.pallas_call(functools.partial(layer_kernel, wide), out_shape=[jax.Shap...]
where the time goes in v6:
time: 102 us
  Pallas kernels  101 us (99%)
    pallas_call x1, Pallas kernels, run_layer(): pl.pallas_call(functools.partial(layer_kernel, wide), out_shape=[jax.Shap...  93.4 us
    pallas_call x1, Pallas kernels, run_update(): pl.pallas_call(update_kernel, out_shape=[S((TB, D), BF16), S((TB, D), F32...  7.35 us

profile of v6, /device:TPU:0, one launch (start us, length us, event | category | flops | bytes accessed | tf_op | source)
XLA Modules:
  0.0 101.6 jit_solution(6475555455752114707)
XLA Ops:
  0.7 93.4 %layer.1 = (bf16[512,512]{1,0:T(8,128)(2,1)}, bf16[512,512]{1,0:T(8,128)(2,1)}, bf16[6,2,64,512]{3,2,1,0:T(8,128)(2,1)}, bf16[3,2,128,512]{3,2,1,0:T(8,128)(2,1)}, f32[8,512]{1,0:T(8,128)}, /*index=5*/f32[8,128]{1,0:T(8,128)}) custom-call(bf16[512,512]{1,0:T(8,128)(2,1)} %refs_0_.1, bf16[512,512]{1,0:T(8,128)(2,1)} %refs_1_.1, s32[4,128]{1,0:T(4,128)} %bitcast.3, ...), custom_call_target="tpu_custom_call" | custom-call | tf_op jit(solution)/shard_map/layer/pallas_call | solution.py:1102
  94.1 7.4 %update.1 = (bf16[512,512]{1,0:T(8,128)(2,1)}, f32[512,512]{1,0:T(8,128)}, f32[4,512,128]{2,1,0:T(8,128)}, f32[2,128,512]{2,1,0:T(8,128)}, f32[4,512,128]{2,1,0:...) custom-call(bf16[512,512]{1,0:T(8,128)(2,1)} %get-tuple-element.24.o, ...), custom_call_target="tpu_custom_call" | custom-call | tf_op jit(solution)/shard_map/update/pallas_call | solution.py:1219
